TPU v7x, 128 devices: a whole 4x4x4 slice. The times are simulated.
128 devices in a mesh: section: 4 (over y), bar: 32 (over x, z, core).
Axes of the slice: x: 4, y: 4, z: 4, core: 2. Of those that a mesh axis runs over, the one named last changes fastest.
Arguments:
- bar_in: bfloat16 [4, 128, 4096], P(None, None, 'bar'), may hold values from -6 to 6
- section_weight: bfloat16 [4, 4096, 4096], P('section', None, 'bar'), may hold values from -0.09375 to 0.09375
- section_gain: float32 [4, 4096], P('section'), may hold values from 0.1 to 1.9
- projection: bfloat16 [4096, 1024], P('bar'), may hold values from -0.09375 to 0.09375
- char_ids: int32 [4, 128, 128], P('section', 'bar'), may hold values from 0 to 127
- lengths: int32 [4, 128], P('section', 'bar'), may hold values from 1 to 128
- char_embed: bfloat16 [128, 1024], replicated, may hold values from -4 to 4
- char_pos: bfloat16 [128, 1024], replicated, may hold values from -3 to 3
- attn_in: bfloat16 [1024, 3072], P(('section', 'bar')), may hold values from -2 to 2
- attn_out: bfloat16 [1024, 1024], P(('section', 'bar')), may hold values from -0.1875 to 0.1875
- ffn_in: bfloat16 [1024, 4096], P(('section', 'bar')), may hold values from -0.1875 to 0.1875
- ffn_out: bfloat16 [4096, 1024], P(('section', 'bar')), may hold values from -0.09375 to 0.09375
- norm_gain: float32 [3, 1024], replicated, may hold values from 0.1 to 1.9
Outputs:
- char_logp: float32 [4, 128, 128], P('section', 'bar')
All inputs are finite; a program needn't handle non-finite values.
Results may differ from a plain program's by a relative error of at most 0.0009.
Values may be sent and summed in bfloat16 or wider, within the bound.
No kernel may reach another device: no remote copies, remote signals or barrier semaphores. Data moves between devices by JAX's collectives and lax.ppermute only.
A program may use at most 128 MiB of HBM per device.

v0:
```python
import jax
import jax.numpy as jnp
from jax import lax
from jax.sharding import PartitionSpec as P

CHD = 64


def from_behind(x, axis, by):
    count = lax.axis_size(axis)
    pairs = [(i, i + by) for i in range(count) if 0 <= i + by < count]
    return lax.ppermute(x, axis, pairs)


def rms_scale(values, gain_row):
    return values * lax.rsqrt(jnp.mean(values * values, axis=-1, keepdims=True) + 1e-05) * gain_row


def char_decoder(
    bar_vectors,
    char_ids,
    lengths,
    char_embed,
    char_pos,
    attn_in,
    attn_out,
    ffn_in,
    ffn_out,
    norm_gain,
):
    bar_count = bar_vectors.shape[0]
    char_count = char_ids.shape[1]
    vocab_size = char_embed.shape[0]
    model_width = char_embed.shape[1]
    head_count = model_width // CHD
    earlier = jax.nn.one_hot(char_ids[:, :-1].reshape(-1), vocab_size, dtype=jnp.bfloat16)
    embedded = jnp.dot(earlier, char_embed, preferred_element_type=jnp.float32).reshape(
        bar_count, char_count - 1, model_width
    )
    inputs = jnp.concatenate([bar_vectors.astype(jnp.float32)[:, None, :], embedded], axis=1)
    inputs = (inputs + char_pos.astype(jnp.float32)[None]).reshape(
        bar_count * char_count, model_width
    )
    normed = rms_scale(inputs, norm_gain[0]).astype(jnp.bfloat16)
    project = jnp.dot(normed, attn_in, preferred_element_type=jnp.float32).astype(jnp.bfloat16)
    project = project.reshape(bar_count, char_count, 3, head_count, CHD)
    queries = project[:, :, 0]
    keys_all = project[:, :, 1]
    values = project[:, :, 2]
    scores = jnp.einsum(
        "bqhd,bkhd->bhqk", queries, keys_all, preferred_element_type=jnp.float32
    ) * CHD ** (-0.5)
    position = jnp.arange(char_count)
    causal = position[None, :] <= position[:, None]
    scores = jnp.where(causal[None, None], scores, -1e30)
    weights = jax.nn.softmax(scores, axis=-1).astype(jnp.bfloat16)
    context = jnp.einsum(
        "bhqk,bkhd->bqhd", weights, values, preferred_element_type=jnp.float32
    ).astype(jnp.bfloat16)
    context = context.reshape(bar_count * char_count, model_width)
    hidden = inputs + jnp.dot(context, attn_out, preferred_element_type=jnp.float32)
    normed = rms_scale(hidden, norm_gain[1]).astype(jnp.bfloat16)
    middle = jax.nn.gelu(jnp.dot(normed, ffn_in, preferred_element_type=jnp.float32)).astype(
        jnp.bfloat16
    )
    hidden = hidden + jnp.dot(middle, ffn_out, preferred_element_type=jnp.float32)
    normed = rms_scale(hidden, norm_gain[2]).astype(jnp.bfloat16)
    logits = jnp.dot(normed, char_embed.T, preferred_element_type=jnp.float32)
    logprob = logits - jax.nn.logsumexp(logits, axis=-1, keepdims=True)
    picker = jax.nn.one_hot(char_ids.reshape(-1), vocab_size, dtype=jnp.float32)
    chosen = jnp.sum(picker * logprob, axis=-1).reshape(bar_count, char_count)
    live_mask = position[None, :] < lengths[:, None]
    return jnp.where(live_mask, chosen, 0.0)


def body(
    bar_in,
    section_weight,
    section_gain,
    projection,
    char_ids,
    lengths,
    char_embed,
    char_pos,
    attn_in,
    attn_out,
    ffn_in,
    ffn_out,
    norm_gain,
):
    section_count = lax.axis_size("section")
    section_index = lax.axis_index("section")
    micro_count = bar_in.shape[0]
    local_rows = bar_in.shape[1] // lax.axis_size("bar")
    weight_cols = section_weight[0]
    gain_row = section_gain[0]
    arriving = jnp.zeros(bar_in.shape[1:], jnp.bfloat16)
    finished = []
    for tick_index in range(micro_count + section_count - 1):
        if tick_index < micro_count:
            fresh = bar_in[tick_index]
        else:
            fresh = jnp.zeros_like(arriving)
        current = jnp.where(section_index == 0, fresh, arriving)
        gathered = lax.all_gather(current, "bar", axis=1, tiled=True)
        normed = rms_scale(gathered.astype(jnp.float32), gain_row).astype(jnp.bfloat16)
        update = jax.nn.gelu(jnp.dot(normed, weight_cols, preferred_element_type=jnp.float32))
        leaving = (current.astype(jnp.float32) + update).astype(jnp.bfloat16)
        if tick_index >= section_count - 1:
            finished.append(leaving)
        if tick_index < micro_count + section_count - 2:
            arriving = from_behind(leaving, "section", 1)
    stacked = jnp.stack(finished)
    vector_list = []
    for micro_index in range(micro_count):

        def micro_term(row_start, row_count, source=stacked[micro_index]):
            return jnp.dot(source, projection, preferred_element_type=jnp.float32)

        vector_list.append(
            lax.psum_scatter(
                micro_term(jnp.int32(0), local_rows * lax.axis_size("bar")),
                "bar",
                scatter_dimension=0,
                tiled=True,
            ).astype(jnp.bfloat16)
        )
    bar_vectors = lax.all_to_all(
        jnp.stack(vector_list), "section", split_axis=0, concat_axis=0, tiled=True
    )[section_count - 1]
    whole_in, whole_out, whole_up, whole_down = (
        lax.all_gather(attn_in, ("section", "bar"), axis=0, tiled=True),
        lax.all_gather(attn_out, ("section", "bar"), axis=0, tiled=True),
        lax.all_gather(ffn_in, ("section", "bar"), axis=0, tiled=True),
        lax.all_gather(ffn_out, ("section", "bar"), axis=0, tiled=True),
    )
    logprob = char_decoder(
        bar_vectors,
        char_ids[0],
        lengths[0],
        char_embed,
        char_pos,
        whole_in,
        whole_out,
        whole_up,
        whole_down,
        norm_gain,
    )
    return logprob[None]


def solution(mesh):
    in_specs = (
        P(None, None, "bar"),
        P("section", None, "bar"),
        P("section", None),
        P("bar", None),
        P("section", "bar", None),
        P("section", "bar"),
        P(),
        P(),
        P(("section", "bar"), None),
        P(("section", "bar"), None),
        P(("section", "bar"), None),
        P(("section", "bar"), None),
        P(),
    )
    out_specs = P("section", "bar", None)
    return jax.shard_map(body, mesh=mesh, in_specs=in_specs, out_specs=out_specs, check_vma=False)
```

profile of v0, /device:TPU:0, one launch (start us, length us, event | category | flops | bytes accessed | tf_op | source)
XLA Modules:
  0.0 672.6 jit_solution(7081801022963113505)
XLA Ops:
  8.1 47.1 %all-gather.33.cloned.1.call-done = bf16[1,128,4096]{2,1,0:T(8,128)(2,1)} async-done(((bf16[1,128,128]{2,1,0:T(8,128)(2,1)}), bf16[1,128,4096]{2,1,0:T(8,128)(2,1)}) %all-gather.33.cloned.1.call-update) | async-done | bytes 1048592 | tf_op jit(solution)/shard_map/all_gather | solution.py:105
  55.1 1.5 fusion.30
  56.7 1.8 fusion.110
  58.4 3.4 collective-permute-start
  61.8 1.6 collective-permute-done
  64.1 43.3 %all-gather.13.cloned.1.call-done = bf16[128,4096]{1,0:T(8,128)(2,1)} async-done(((bf16[128,128]{1,0:T(8,128)(2,1)}), bf16[128,4096]{1,0:T(8,128)(2,1)}) %all-gather.13.cloned.1.call-update) | async-done | bytes 1048592 | tf_op jit(solution)/shard_map/all_gather | solution.py:105
  107.4 1.5 fusion.12
  109.0 1.7 add_convert_fusion.5
  110.7 3.4 collective-permute-start.1
  114.1 1.6 collective-permute-done.1
  116.4 43.3 %all-gather.15.cloned.1.call-done = bf16[128,4096]{1,0:T(8,128)(2,1)} async-done(((bf16[128,128]{1,0:T(8,128)(2,1)}), bf16[128,4096]{1,0:T(8,128)(2,1)}) %all-gather.15.cloned.1.call-update) | async-done | bytes 1048592 | tf_op jit(solution)/shard_map/all_gather | solution.py:105
  159.7 1.5 fusion.15
  161.2 1.8 add_convert_fusion.4
  163.0 3.4 collective-permute-start.2
  166.4 1.6 collective-permute-done.2
  168.6 43.3 %all-gather.17.cloned.1.call-done = bf16[128,4096]{1,0:T(8,128)(2,1)} async-done(((bf16[128,128]{1,0:T(8,128)(2,1)}), bf16[128,4096]{1,0:T(8,128)(2,1)}) %all-gather.17.cloned.1.call-update) | async-done | bytes 1048592 | tf_op jit(solution)/shard_map/all_gather | solution.py:105
  212.0 1.5 fusion.18
  213.5 1.8 add_convert_fusion.3
  215.2 3.4 collective-permute-start.3
  218.6 1.6 collective-permute-done.3
  220.9 43.3 %all-gather.19.cloned.1.call-done = bf16[128,4096]{1,0:T(8,128)(2,1)} async-done(((bf16[128,128]{1,0:T(8,128)(2,1)}), bf16[128,4096]{1,0:T(8,128)(2,1)}) %all-gather.19.cloned.1.call-update) | async-done | bytes 1048592 | tf_op jit(solution)/shard_map/all_gather | solution.py:105
  264.2 1.5 fusion.21
  265.7 1.8 add_convert_fusion.2
  267.5 3.4 collective-permute-start.4
  270.9 1.6 collective-permute-done.4
  273.2 43.3 %all-gather.21.cloned.1.call-done = bf16[128,4096]{1,0:T(8,128)(2,1)} async-done(((bf16[128,128]{1,0:T(8,128)(2,1)}), bf16[128,4096]{1,0:T(8,128)(2,1)}) %all-gather.21.cloned.1.call-update) | async-done | bytes 1048592 | tf_op jit(solution)/shard_map/all_gather | solution.py:105
  316.5 1.5 fusion.24
  318.0 1.8 add_convert_fusion.1
  319.8 3.4 collective-permute-start.5
  323.2 1.6 collective-permute-done.5
  334.1 34.7 %all-gather.23.cloned.1.call-done = bf16[128,4096]{1,0:T(8,128)(2,1)} async-done(((bf16[128,128]{1,0:T(8,128)(2,1)}), bf16[128,4096]{1,0:T(8,128)(2,1)}) %all-gather.23.cloned.1.call-update) | async-done | bytes 1048592 | tf_op jit(solution)/shard_map/all_gather | solution.py:105
  368.8 1.5 fusion.27
  370.3 2.7 fusion.181
  373.0 152.3 %all-reduce.6 = (bf16[128,1024]{1,0:T(8,128)(2,1)S(1)}, bf16[128,1024]{1,0:T(8,128)(2,1)S(1)}, bf16[128,1024]{1,0:T(8,128)(2,1)S(1)}, bf16[128,1024]{1,0:T(8,128)(2,1)S(1)}) all-reduce(f32[128,1024]{1,0:T(8,128)} %fusion.181, f32[128,1024]{1,0:T(8,128)} %fusion.235, ...), channel_id=6, replica_groups=mesh['section'=4,'bar'=32] {'bar'}, use_global_device_ids=true, to_apply=%region_10.11.clone | all-reduce | flops 524288 | bytes 3145728
  526.0 4.3 all-to-all-start
  530.3 1.6 reshape.201
  532.0 3.8 all-to-all-done
  535.8 2.0 multiply_reduce_fusion.2
  538.1 7.6 %convolution_convert_fusion = bf16[512,3072]{1,0:T(8,128)(2,1)} fusion(bf16[512,1024]{1,0:T(8,128)(2,1)S(1)} %fusion.34, bf16[1024,3072]{1,0:T(8,128)(2,1)} %all-gather.25.cloned.1.call-done), kind=kOutput, calls=%fused_computation.10 | convolution fusion | flops 3222798336 | bytes 10485760 | tf_op jit(solution)/shard_map/dot_general | solution.py:45
  545.7 8.6 %reshape.213 = bf16[4,128,3,16,64]{4,3,2,1,0:T(8,128)(2,1)} reshape(bf16[512,3072]{1,0:T(8,128)(2,1)} %convolution_convert_fusion) | data formatting | bytes 6291456 | tf_op jit(solution)/shard_map/reshape | solution.py:46
  554.3 6.0 fusion.229
  560.3 2.8 copy.44
  563.1 3.7 copy.45
  566.9 3.6 copy.43
  570.4 2.1 fusion.62
  575.4 4.3 multiply_reduce_fusion.1
  579.7 68.8 %all-gather.31.cloned.1.call-done = bf16[4096,1024]{1,0:T(8,128)(2,1)} async-done(((bf16[32,1024]{1,0:T(8,128)(2,1)}), bf16[4096,1024]{1,0:T(8,128)(2,1)}) %all-gather.31.cloned.1.call-update) | async-done | bytes 8388624 | tf_op jit(solution)/shard_map/all_gather | solution.py:135
  648.5 16.2 %multiply_reduce_fusion = (f32[512]{0:T(512)S(1)}, f32[512,1024]{1,0:T(8,128)S(1)}) fusion(f32[512,1024]{1,0:T(8,128)} %get-tuple-element.20, bf16[4096,1024]{1,0:T(8,128)(2,1)} %all-gather.31.cloned.1.call-done, bf16[1024,4096]{1,0:T(8,128)(2,1)} %all-gather.29.cloned.1.call-done, f32[1024]{0:T(1024)S(1)} %bitcast.145, f32[512]{0:T(512)S(1)} %add_rsqrt_fusion.1), kind=kOutput, calls=%fused_computation.57 | convolution fusion | flops 8611954688 | bytes 20979712 | tf_op jit(solution)/shard_map/dot_general | solution.py:66
  (94 shorter events, 18.7 us)
Async XLA Ops:
  6.5 50.1 %copy-start = (bf16[1,4096,128]{2,1,0:T(8,128)(2,1)S(1)}, bf16[1,4096,128]{2,1,0:T(8,128)(2,1)}, u32[]{:S(2)}) copy-start(bf16[1,4096,128]{2,1,0:T(8,128)(2,1)} %param.14) | copy-start | bytes 3145732
  6.5 56.9 %copy-start.6 = (bf16[4,128,128]{2,1,0:T(8,128)(2,1)S(1)}, bf16[4,128,128]{2,1,0:T(8,128)(2,1)}, u32[]{:S(2)}) copy-start(bf16[4,128,128]{2,1,0:T(8,128)(2,1)} %param.13) | copy-start | bytes 393220
  6.5 48.6 %all-gather.33.cloned.1.call-start = ((), (), s32[]{:S(2)}) async-start(), calls=%async_computation.11 | async-start | bytes 1081344 | tf_op jit(solution)/shard_map/all_gather | solution.py:105
  8.0 99.4 %all-gather.13.cloned.1.call-start = ((), (), s32[]{:S(2)}) async-start(), calls=%async_computation.1 | async-start | bytes 1081344 | tf_op jit(solution)/shard_map/all_gather | solution.py:105
  56.7 52.3 %copy-start.11 = (f32[1,4096]{1,0:T(1,128)S(1)}, f32[1,4096]{1,0:T(1,128)}, u32[]{:S(2)}) copy-start(f32[1,4096]{1,0:T(1,128)} %param.15) | copy-start | bytes 49156
  58.4 5.0 collective-permute-start
  64.1 95.6 %all-gather.15.cloned.1.call-start = ((), (), s32[]{:S(2)}) async-start(), calls=%async_computation.2 | async-start | bytes 1081344 | tf_op jit(solution)/shard_map/all_gather | solution.py:105
  110.7 5.0 collective-permute-start.1
  116.3 95.6 %all-gather.17.cloned.1.call-start = ((), (), s32[]{:S(2)}) async-start(), calls=%async_computation.3 | async-start | bytes 1081344 | tf_op jit(solution)/shard_map/all_gather | solution.py:105
  163.0 5.0 collective-permute-start.2
  168.6 95.6 %all-gather.19.cloned.1.call-start = ((), (), s32[]{:S(2)}) async-start(), calls=%async_computation.4 | async-start | bytes 1081344 | tf_op jit(solution)/shard_map/all_gather | solution.py:105
  215.2 5.0 collective-permute-start.3
  220.8 95.6 %all-gather.21.cloned.1.call-start = ((), (), s32[]{:S(2)}) async-start(), calls=%async_computation.5 | async-start | bytes 1081344 | tf_op jit(solution)/shard_map/all_gather | solution.py:105
  267.5 5.0 collective-permute-start.4
  273.1 55.1 %copy-start.9 = (s32[1,4,128]{2,1,0:T(4,128)S(1)}, s32[1,4,128]{2,1,0:T(4,128)}, u32[]{:S(2)}) copy-start(s32[1,4,128]{2,1,0:T(4,128)} %param.17) | copy-start | bytes 6148
  273.1 55.2 %copy-start.13 = (u32[128]{0:T(128)S(1)}, u32[128]{0:T(128)}, u32[]{:S(2)}) copy-start(u32[128]{0:T(128)} %constant.61) | copy-start | bytes 1540
  273.1 56.4 %copy-start.8 = (f32[3,1024]{1,0:T(4,128)S(1)}, f32[3,1024]{1,0:T(4,128)}, u32[]{:S(2)}) copy-start(f32[3,1024]{1,0:T(4,128)} %param.25) | copy-start | bytes 36868
  273.1 95.6 %all-gather.23.cloned.1.call-start = ((), (), s32[]{:S(2)}) async-start(), calls=%async_computation.6 | async-start | bytes 1081344 | tf_op jit(solution)/shard_map/all_gather | solution.py:105
  318.0 13.0 %copy-start.2 = (bf16[128,1024]{1,0:T(8,128)(2,1)S(1)}, bf16[128,1024]{1,0:T(8,128)(2,1)}, u32[]{:S(2)}) copy-start(bf16[128,1024]{1,0:T(8,128)(2,1)} %param.16) | copy-start | bytes 786436
  319.8 5.0 collective-permute-start.5
  325.4 212.6 %all-gather.25.cloned.1.call-start = ((), (), s32[]{:S(2)}) async-start(), calls=%async_computation.7 | async-start | bytes 6340608 | tf_op jit(solution)/shard_map/all_gather | solution.py:132
  326.2 249.2 %all-gather.27.cloned.1.call-start = ((), (), s32[]{:S(2)}) async-start(), calls=%async_computation.8 | async-start | bytes 2113536 | tf_op jit(solution)/shard_map/all_gather | solution.py:133
  326.9 252.8 %all-gather.29.cloned.1.call-start = ((), (), s32[]{:S(2)}) async-start(), calls=%async_computation.9 | async-start | bytes 8454144 | tf_op jit(solution)/shard_map/all_gather | solution.py:134
  327.5 321.0 %all-gather.31.cloned.1.call-start = ((), (), s32[]{:S(2)}) async-start(), calls=%async_computation.10 | async-start | bytes 8454144 | tf_op jit(solution)/shard_map/all_gather | solution.py:135
  331.1 39.3 %copy-start.7 = (bf16[128,128]{1,0:T(8,128)(2,1)S(1)}, bf16[128,128]{1,0:T(8,128)(2,1)}, u32[]{:S(2)}) copy-start(bf16[128,128]{1,0:T(8,128)(2,1)} %broadcast_select_fusion) | copy-start | bytes 98308
  332.1 38.3 %copy-start.12 = (f32[1,4096]{1,0:T(1,128)S(1)}, f32[1,4096]{1,0:T(1,128)}, u32[]{:S(2)}) copy-start(f32[1,4096]{1,0:T(1,128)} %param.15) | copy-start | bytes 49156
  526.0 9.7 %all-to-all-start = ((bf16[4,4,1024]{2,1,0:T(4,128)(2,1)}), bf16[4,4,1024]{2,1,0:T(4,128)(2,1)S(1)}, u32[]{:S(2)}, u32[]{:S(2)}) async-start(bf16[4,4,1024]{2,1,0:T(4,128)(2,1)} %pad_maximum_fusion), calls=%async_computation | async-start | bytes 65536 | tf_op jit(solution)/shard_map/all_to_all | solution.py:128
  530.3 1.6 copy-start.5
  572.6 1.2 copy-start.3
  648.5 16.2 %copy-start.4 = (bf16[128,1024]{1,0:T(8,128)(2,1)S(1)}, bf16[128,1024]{1,0:T(8,128)(2,1)}, u32[]{:S(2)}) copy-start(bf16[128,1024]{1,0:T(8,128)(2,1)} %param.19) | copy-start | bytes 786436
  648.5 17.6 %copy-start.1 = (bf16[1,4096,128]{2,1,0:T(8,128)(2,1)S(1)}, bf16[1,4096,128]{2,1,0:T(8,128)(2,1)}, u32[]{:S(2)}) copy-start(bf16[1,4096,128]{2,1,0:T(8,128)(2,1)} %param.14) | copy-start | bytes 3145732
  664.6 0.8 copy-start.10
Sparse Core Ops, SparseCore 0:
  9.5 45.5 all-gather.32
  64.2 43.1 all-gather.12
  116.4 43.1 all-gather.14
  168.7 43.1 all-gather.16
  221.0 43.1 all-gather.18
  273.2 43.1 all-gather.20
  325.5 43.1 all-gather.22
  371.8 68.7 all-gather.24
  443.7 63.3 all-gather.26
  510.0 67.7 all-gather.28
  580.8 67.6 all-gather.30
where the time goes:
time: 675 us; the launch traced here: 673 us
  waiting for transfers between devices  383 us (57%)
  blocking collectives  152 us (23%)
  matrix products  49.2 us (7%)
  local copies, waits for them, and re-layouts  28.2 us (4%)
  starting transfers between devices  25.1 us (4%)
  other arithmetic  20.7 us (3%)
  between operations  14.3 us (2%)
    all_gather x7, waiting for transfers between devices, body(): gathered = lax.all_gather(current, 'bar', axis=1, tiled=True)  298 us
    unnamed x1, blocking collectives  152 us
    all_gather x1, waiting for transfers between devices, body(): lax.all_gather(ffn_out, ('section', 'bar'), axis=0, tiled=True)  68.8 us
    ppermute x6, starting transfers between devices, from_behind(): return lax.ppermute(x, axis, pairs)  20.4 us
    dot_general x1, matrix products, char_decoder(): jnp.dot(middle, ffn_out, preferred_element_type=jnp.float32)  16.2 us
  transfers between devices with their start and end apart: 18, of which 15 were waited for; matrix products, arithmetic and copies ran while one was open for 8% of the time, Pallas kernels for 0%

commit v1 on v0

v1 whole, which is shorter than its diff:
```python
import jax, jax.numpy as jnp
from jax import lax
from jax.sharding import PartitionSpec as P
from jax.experimental import pallas as pl
from jax.experimental.pallas import tpu as pltpu

BF=jnp.bfloat16
F32=jnp.float32

def rms_rows(v, g):
    return v * lax.rsqrt(jnp.mean(v * v, axis=-1, keepdims=True) + 1e-05) * g


def char_kernel(parts_ref, ids_ref, prev_ref, len_ref, embed_ref, pos_ref, gain_ref, pack_ref, out_ref,
                x_ref, n_ref, q_ref, k_ref, v_ref, c_ref, mid_ref, wq, wup, wdn, sems):
    bars, chars = ids_ref.shape
    width = embed_ref.shape[1]
    copies = []
    for j in range(4):
        copies.append(pltpu.make_async_copy(pack_ref.at[:, j], wq.at[j], sems.at[j]))
    for j in range(4):
        copies.append(pltpu.make_async_copy(pack_ref.at[:, 4 + j], wup.at[j], sems.at[4 + j]))
    for j in range(4):
        rows = pl.ds(32 * j, 32)
        copies.append(pltpu.make_async_copy(pack_ref.at[rows, 8:12], wdn.at[rows], sems.at[8 + j]))
    for i in (0, 1, 2, 3, 4, 8, 5, 9, 6, 10, 7, 11):
        copies[i].start()
    vocab = embed_ref.shape[0]
    vec = jnp.sum(parts_ref[...], axis=0).astype(BF).astype(F32)
    row_id = lax.broadcasted_iota(jnp.int32, (chars, width), 0)
    for b in range(bars):
        one_hot = (lax.broadcasted_iota(jnp.int32, (vocab, chars), 0) == prev_ref[b:b + 1, :]).astype(BF)
        emb = lax.dot_general(one_hot, embed_ref[...], (((0,), (0,)), ((), ())), preferred_element_type=F32)
        emb = jnp.where(row_id == 0, vec[b:b + 1], emb) + pos_ref[...].astype(F32)
        x_ref[b * chars:(b + 1) * chars] = emb
        n_ref[b * chars:(b + 1) * chars] = rms_rows(emb, gain_ref[0:1]).astype(BF)
    for j, dst in ((0, q_ref), (1, k_ref), (2, v_ref)):
        copies[j].wait()
        dst[...] = jnp.dot(n_ref[...], wq[j].reshape(width, width), preferred_element_type=F32).astype(BF)

    lane = lax.broadcasted_iota(jnp.int32, (chars, 128), 1)
    low = lane < 64
    causal = lax.broadcasted_iota(jnp.int32, (chars, chars), 0) >= lax.broadcasted_iota(jnp.int32, (chars, chars), 1)

    def attend(b, carry):
        rows = pl.ds(pl.multiple_of(b * chars, chars), chars)
        for h in range(width // 128):
            cols = slice(h * 128, (h + 1) * 128)
            q, k, v = q_ref[rows, cols], k_ref[rows, cols], v_ref[rows, cols]
            zero = jnp.zeros_like(k)
            kk = jnp.concatenate([jnp.where(low, k, zero), jnp.where(low, zero, k)], axis=0)
            vv = jnp.concatenate([jnp.where(low, v, zero), jnp.where(low, zero, v)], axis=0)
            s = lax.dot_general(q, kk, (((1,), (1,)), ((), ())), preferred_element_type=F32)
            probs = []
            for half in range(2):
                t = jnp.where(causal, s[:, half * chars:(half + 1) * chars], -1e30)
                e = jnp.exp((t - jnp.max(t, axis=-1, keepdims=True)) * 0.125)
                probs.append((e * (1.0 / jnp.sum(e, axis=-1, keepdims=True))).astype(BF))
            c_ref[rows, cols] = jnp.dot(jnp.concatenate(probs, axis=1), vv, preferred_element_type=F32).astype(BF)
        return carry

    lax.fori_loop(0, bars, attend, 0)
    copies[3].wait()
    hidden = x_ref[...] + jnp.dot(c_ref[...], wq[3].reshape(width, width), preferred_element_type=F32)
    x_ref[...] = hidden
    n_ref[...] = rms_rows(hidden, gain_ref[1:2]).astype(BF)
    for j in range(4):
        copies[4 + j].wait()
        mid_ref[...] = jax.nn.gelu(jnp.dot(n_ref[...], wup[j].reshape(width, width), preferred_element_type=F32)).astype(BF)
        copies[8 + j].wait()
        x_ref[...] += jnp.dot(mid_ref[...], wdn[32 * j:32 * j + 32].reshape(width, width), preferred_element_type=F32)
    last = rms_rows(x_ref[...], gain_ref[2:3]).astype(BF)
    logits = lax.dot_general(embed_ref[...], last, (((1,), (1,)), ((), ())), preferred_element_type=F32)
    top = jnp.max(logits, axis=0, keepdims=True)
    norm = top + jnp.log(jnp.sum(jnp.exp(logits - top), axis=0, keepdims=True))
    for b in range(bars):
        cols = slice(b * chars, (b + 1) * chars)
        hit = lax.broadcasted_iota(jnp.int32, (vocab, chars), 0) == ids_ref[b:b + 1, :]
        picked = jnp.sum(jnp.where(hit, logits[:, cols], 0.0), axis=0, keepdims=True) - norm[:, cols]
        live = lax.broadcasted_iota(jnp.int32, (1, chars), 1) < len_ref[b:b + 1, :]
        out_ref[b:b + 1, :] = jnp.where(live, picked, 0.0)


def char_decode(parts, ids, lengths, embed, pos, gain, pack):
    bars, chars = ids.shape
    width = embed.shape[1]
    tokens = bars * chars
    prev = jnp.concatenate([jnp.full((bars, 1), -1, jnp.int32), ids[:, :-1]], axis=1)
    vm = pl.BlockSpec(memory_space=pltpu.VMEM)
    t = lambda d: pltpu.VMEM((tokens, width), d)
    return pl.pallas_call(
        char_kernel,
        out_shape=jax.ShapeDtypeStruct((bars, chars), F32),
        in_specs=[vm] * 7 + [pl.BlockSpec(memory_space=pl.ANY)],
        out_specs=vm,
        scratch_shapes=[t(F32), t(BF), t(BF), t(BF), t(BF), t(BF), t(BF),
                        pltpu.VMEM((4, 128, 8, width), BF), pltpu.VMEM((4, 128, 8, width), BF),
                        pltpu.VMEM((128, 4, 8, width), BF), pltpu.SemaphoreType.DMA((12,))],
        compiler_params=pltpu.CompilerParams(vmem_limit_bytes=56 << 20),
        name="char_decode",
    )(parts, ids, prev, lengths[:, None], embed, pos, gain, pack)


GROUP = ("y", "x", "z", "c")


def section_kernel(copies, project, where_ref, x_ref, gain_ref, *refs):
    own, other = refs[:copies], refs[copies:2 * copies]
    refs = refs[2 * copies:]
    if project:
        proj_ref, refs = refs[0], refs[1:]
    out_ref, n_ref, w_ref, sems = refs
    blocks, rows, cols = x_ref.shape
    half = cols // 2
    which, core, chip = where_ref[0], where_ref[1], where_ref[2]
    first = pl.ds(pl.multiple_of(core * half, half), half)
    second = pl.ds(pl.multiple_of((1 - core) * half, half), half)
    for i in range(copies):
        @pl.when(which == i)
        def _():
            pltpu.make_async_copy(own[i], w_ref.at[:, first], sems.at[0]).start()
            pltpu.make_async_copy(other[i], w_ref.at[:, second], sems.at[1]).start()
    total = jnp.zeros((rows, cols), F32)
    for j in range(blocks):
        v = x_ref[j].astype(F32)
        total += v * v
    scale = lax.rsqrt(jnp.sum(total, axis=-1, keepdims=True) / (blocks * cols) + 1e-05)
    gain = gain_ref[which]
    for j in range(blocks):
        span = slice(j * cols, (j + 1) * cols)
        n_ref[:, span] = (x_ref[j].astype(F32) * scale * gain[:, span]).astype(BF)
    pltpu.make_async_copy(own[0], w_ref.at[:, first], sems.at[0]).wait()
    pltpu.make_async_copy(other[0], w_ref.at[:, second], sems.at[1]).wait()
    update = jax.nn.gelu(jnp.dot(n_ref[...], w_ref[...], preferred_element_type=F32))
    leaving = (x_ref[chip].astype(F32) + update).astype(BF)
    if project:
        partial = jnp.dot(leaving, proj_ref[...], preferred_element_type=F32)
        each = rows // blocks
        for j in range(blocks):
            out_ref[j] = partial[j * each:(j + 1) * each]
    else:
        each = out_ref.shape[1]
        for j in range(out_ref.shape[0]):
            out_ref[j] = leaving if each == rows else leaving[j * each:(j + 1) * each]


def section_step(where, x, gain, own, other, out_shape, proj=None):
    blocks, rows, cols = x.shape
    depth = blocks * cols
    vm = pl.BlockSpec(memory_space=pltpu.VMEM)
    hbm = pl.BlockSpec(memory_space=pl.ANY)
    extra = [] if proj is None else [proj]
    return pl.pallas_call(
        lambda *refs: section_kernel(len(own), proj is not None, *refs),
        out_shape=out_shape,
        in_specs=[pl.BlockSpec(memory_space=pltpu.SMEM), vm, vm] + [hbm] * (2 * len(own)) + [vm] * len(extra),
        out_specs=vm,
        scratch_shapes=[pltpu.VMEM((rows, depth), BF), pltpu.VMEM((depth, cols), BF), pltpu.SemaphoreType.DMA((2,))],
        compiler_params=pltpu.CompilerParams(vmem_limit_bytes=32 << 20),
        name="section",
    )(where, x, gain, *own, *other, *extra)


def body(bar_in, section_weight, section_gain, projection, char_ids, lengths, char_embed, char_pos,
         attn_in, attn_out, ffn_in, ffn_out, norm_gain):
    y, core = lax.axis_index("y"), lax.axis_index("c")
    chip = lax.axis_index("x") * 4 + lax.axis_index("z")
    width = char_embed.shape[1]

    def swap(v):
        return lax.ppermute(v, "c", [(0, 1), (1, 0)])

    def turn(v, by):
        return lax.ppermute(v, "y", [(i, (i + by) % 4) for i in range(4)])

    def ordered(mine, theirs, axis):
        return jnp.where(core == 0, jnp.concatenate([mine, theirs], axis), jnp.concatenate([theirs, mine], axis))

    def spread(v):
        return lax.all_to_all(v, ("x", "z"), 0, 0, tiled=True)

    pack = jnp.concatenate(
        [attn_in[:, i * width:(i + 1) * width] for i in range(3)] + [attn_out]
        + [ffn_in[:, i * width:(i + 1) * width] for i in range(4)] + [ffn_out], axis=0)
    pack = lax.all_gather(pack, GROUP, axis=0, tiled=True).reshape(128, 12, 8, width)

    own = [section_weight[0]]
    gains = [section_gain]
    for by in (1, 2, 3):
        own.append(turn(section_weight[0], by))
        gains.append(turn(section_gain, by))
    other = [swap(w) for w in own]
    proj = ordered(projection, swap(projection), 0)

    micro, bars, feats = bar_in.shape
    by_core = bar_in.reshape(micro, 16, 2, 4, feats).transpose(2, 0, 1, 3, 4).reshape(2, micro * 64, feats)
    mine = lax.dynamic_index_in_dim(by_core, core, 0, keepdims=False)
    theirs = swap(lax.dynamic_index_in_dim(by_core, 1 - core, 0, keepdims=False))
    block = ordered(mine, theirs, 1)
    x = spread(jnp.broadcast_to(block[None], (16,) + block.shape))

    def where(step):
        return jnp.stack([lax.rem(y - step + 4, 4) if step else jnp.int32(0), core, chip])

    first = section_step(where(0), x, section_gain[None], own[:1], other[:1],
                         jax.ShapeDtypeStruct((micro, 64, 2 * feats), BF))
    rows = lax.all_to_all(first, "y", 0, 0, tiled=True)[0]
    out = jnp.broadcast_to(rows[None], (16,) + rows.shape)
    gain = jnp.stack(gains)
    for step in (1, 2, 3):
        x = spread(out)
        shape = jax.ShapeDtypeStruct((16, 64, 2 * feats), BF) if step < 3 else jax.ShapeDtypeStruct((16, 4, width), F32)
        out = section_step(where(step), x, gain, own, other, shape, proj if step == 3 else None)
    parts = spread(out)
    return char_decode(parts, char_ids[0], lengths[0], char_embed, char_pos, norm_gain, pack)[None]


def solution(mesh):
    fine = jax.sharding.Mesh(mesh.devices.reshape(4, 4, 4, 2), GROUP)
    bar = ("x", "z", "c")
    in_specs = (
        P(None, None, bar),
        P("y", None, bar),
        P("y", None),
        P(bar, None),
        P("y", bar, None),
        P("y", bar),
        P(),
        P(),
        P(GROUP, None),
        P(GROUP, None),
        P(GROUP, None),
        P(GROUP, None),
        P(),
    )
    return jax.shard_map(body, mesh=fine, in_specs=in_specs, out_specs=P("y", bar, None), check_vma=False)
```

time: 675 us -> 216 us (0.32)
  waiting for transfers between devices: 383 us -> 99.5 us
  blocking collectives: 152 us -> 0 us
  matrix products: 49.2 us -> 0 us
  Pallas kernels: 0 us -> 39.9 us
  starting transfers between devices: 25.1 us -> 43.5 us
  other arithmetic: 20.7 us -> 2.39 us
  local copies, waits for them, and re-layouts: 28.2 us -> 15.3 us
    all_gather x11 -> x1, waiting for transfers between devices: 367 us -> 0.01 us  [body(): lax.all_gather(pack, GROUP, axis=0, tiled=True).reshape(128, 12, 8, width)]
    unnamed x1 -> x0, blocking collectives: 152 us -> none
    ppermute x6 -> x12, waiting for transfers between devices: 9.47 us -> 61.4 us  [the longest x6 58.5 us: turn(): return lax.ppermute(v, 'y', [(i, (i + by) % 4) for i in range(4)])]
    dot_general x17 -> x0, matrix products: 49.2 us -> none  [the longest x1 16.2 us: char_decoder(): jnp.dot(middle, ffn_out, preferred_element_type=jnp.float32)]
    pallas_call x0 -> x5, Pallas kernels: none -> 39.9 us  [the longest x1 25.3 us: char_decode(): pl.pallas_call(char_kernel, out_shape=jax.ShapeDtypeStruct((bars, chars),...]
    all_to_all x1 -> x6, waiting for transfers between devices: 3.75 us -> 38.1 us  [the longest x5 34.8 us: spread(): return lax.all_to_all(v, ('x', 'z'), 0, 0, tiled=True)]
    all_to_all x1 -> x6, starting transfers between devices: 4.3 us -> 32.2 us  [the longest x5 28.8 us: spread(): return lax.all_to_all(v, ('x', 'z'), 0, 0, tiled=True)]
    reduce_sum x10 -> x0, other arithmetic: 12.8 us -> none  [the longest x8 12.6 us: rms_scale(): jnp.mean(values * values, axis=-1, keepdims=True) + 1e-05]
  transfers between devices with their start and end apart: 18 -> 19, of which waited for: 15 -> 11; matrix products, arithmetic and copies ran while one was open for 8% -> 3% of each run, Pallas kernels for 0% -> 7%
where the time goes in v1:
time: 216 us; the launch traced here: 214 us
  waiting for transfers between devices  99.5 us (46%)
  starting transfers between devices  43.5 us (20%)
  Pallas kernels  39.9 us (18%)
  local copies, waits for them, and re-layouts  15.3 us (7%)
  between operations  13.6 us (6%)
  other arithmetic  2.39 us (1%)
    ppermute x6, waiting for transfers between devices, turn(): return lax.ppermute(v, 'y', [(i, (i + by) % 4) for i in range(4)])  58.5 us
    all_to_all x5, waiting for transfers between devices, spread(): return lax.all_to_all(v, ('x', 'z'), 0, 0, tiled=True)  34.8 us
    all_to_all x5, starting transfers between devices, spread(): return lax.all_to_all(v, ('x', 'z'), 0, 0, tiled=True)  28.8 us
    pallas_call x1, Pallas kernels, char_decode(): pl.pallas_call(char_kernel, out_shape=jax.ShapeDtypeStruct((bars, chars),...  25.3 us
    pallas_call x4, Pallas kernels, section_step(): pl.pallas_call(lambda *refs: section_kernel(len(own), proj is not None, *...  14.7 us
    ppermute x6, starting transfers between devices, turn(): return lax.ppermute(v, 'y', [(i, (i + by) % 4) for i in range(4)])  11.2 us
    unnamed x28, local copies, waits for them, and re-layouts  9.75 us
  transfers between devices with their start and end apart: 19, of which 11 were waited for; matrix products, arithmetic and copies ran while one was open for 3% of the time, Pallas kernels for 7%

profile of v1, /device:TPU:0, one launch (start us, length us, event | category | flops | bytes accessed | tf_op | source)
XLA Modules:
  0.0 214.3 jit_solution(11851988175265369784)
XLA Ops:
  6.5 0.7 constant_dynamic-update-slice_fusion.8
  7.3 0.7 constant_dynamic-update-slice_fusion.7
  8.0 0.7 constant_dynamic-update-slice_fusion.6
  8.7 0.7 constant_dynamic-update-slice_fusion.5
  9.4 0.7 constant_dynamic-update-slice_fusion.4
  10.1 0.7 constant_dynamic-update-slice_fusion.3
  10.9 0.7 constant_dynamic-update-slice_fusion.2
  11.6 0.7 constant_dynamic-update-slice_fusion.1
  12.3 0.8 constant_dynamic-update-slice_fusion
  13.1 0.7 copy-done.7
  13.8 1.0 copy.15
  14.9 1.2 collective-permute-done
  16.2 1.6 broadcast_in_dim.19
  17.8 8.1 %all-to-all-start = ((bf16[16,256,256]{2,1,0:T(8,128)(2,1)}), bf16[16,256,256]{2,1,0:T(8,128)(2,1)}, u32[]{:S(2)}, u32[]{:S(2)}) async-start(bf16[16,256,256]{2,1,0:T(8,128)(2,1)} %broadcast_in_dim.19), calls=%async_computation | async-start | bytes 4194304 | tf_op jit(solution)/shard_map/all_to_all | solution.py:180
  25.9 3.1 %collective-permute-start.7 = (bf16[4096,128]{1,0:T(8,128)(2,1)S(1)}, bf16[4096,128]{1,0:T(8,128)(2,1)S(1)}, u32[]{:S(2)}, u32[]{:S(2)}) collective-permute-start(bf16[4096,128]{1,0:T(8,128)(2,1)S(1)} %bitcast.25), channel_id=1, source_target_pairs={{0,96},{32,0},{64,32},{96,64},{1,97},{33,1},{65,33},{97,65},{2,98}... | collective-permute-start | bytes 3145736 | tf_op jit(solution)/shard_map/ppermute | solution.py:174
  29.0 2.2 %collective-permute-start.6 = (bf16[4096,128]{1,0:T(8,128)(2,1)S(1)}, bf16[4096,128]{1,0:T(8,128)(2,1)}, u32[]{:S(2)}, u32[]{:S(2)}) collective-permute-start(bf16[4096,128]{1,0:T(8,128)(2,1)S(1)} %bitcast.27), channel_id=1, source_target_pairs={{0,64},{32,96},{64,0},{96,32},{1,65},{33,97},{65,1},{97,33},{2,66}... | collective-permute-start | bytes 3145736 | tf_op jit(solution)/shard_map/ppermute | solution.py:174
  31.2 37.5 %collective-permute-done.7.refs_6_ = bf16[4096,128]{1,0:T(8,128)(2,1)S(1)} collective-permute-done((bf16[4096,128]{1,0:T(8,128)(2,1)S(1)}, bf16[4096,128]{1,0:T(8,128)(2,1)S(1)}, u32[]{:S(2)}, u32[]{:S(2)}) %collective-permute-start.7) | collective-permute-done | bytes 1048608 | tf_op jit(solution)/shard_map/ppermute | solution.py:174
  68.7 1.1 collective-permute-done.5.refs_4_
  69.8 17.1 %collective-permute-done.6.refs_5_ = bf16[4096,128]{1,0:T(8,128)(2,1)} collective-permute-done((bf16[4096,128]{1,0:T(8,128)(2,1)S(1)}, bf16[4096,128]{1,0:T(8,128)(2,1)}, u32[]{:S(2)}, u32[]{:S(2)}) %collective-permute-start.6) | collective-permute-done | bytes 1048608 | tf_op jit(solution)/shard_map/ppermute | solution.py:174
  87.0 4.3 %section.4 = bf16[4,64,256]{2,1,0:T(8,128)(2,1)} custom-call(s32[3]{0:T(128)S(1)} %add_add_fusion.3.refs_0_, bf16[16,256,256]{2,1,0:T(8,128)(2,1)} %all-to-all-done.refs_1_, f32[1,1,4096]{2,1,0:T(1,128)S(1)} %bitcast.33, bf16[4096,128]{1,0:T(8,128)(2,1)S(1)} %bitcast.29, bf16[4096,128]{1,0:T(8,128)(2,1)S(1)} %collective-permute-done.1.refs_4_.refs_7_), custom_call_target="tpu_custom_call" | custom-call | tf_op jit(solution)/shard_map/section/pallas_call | solution.py:153
  91.4 3.3 %all-to-all-start.1 = ((bf16[4,64,256]{2,1,0:T(8,128)(2,1)}), bf16[4,64,256]{2,1,0:T(8,128)(2,1)S(1)}, u32[]{:S(2)}, u32[]{:S(2)}) async-start(bf16[4,64,256]{2,1,0:T(8,128)(2,1)} %section.4), calls=%async_computation.1 | async-start | bytes 262144 | tf_op jit(solution)/shard_map/all_to_all | solution.py:207
  94.7 2.0 collective-permute-start.2
  96.7 2.7 %collective-permute-start.3 = (f32[1,4096]{1,0:T(1,128)S(1)}, f32[1,4096]{1,0:T(1,128)S(1)}, u32[]{:S(2)}, u32[]{:S(2)}) collective-permute-start(f32[1,4096]{1,0:T(1,128)S(1)} %copy-done.4), channel_id=1, source_target_pairs={{0,64},{32,96},{64,0},{96,32},{1,65},{33,97},{65,1},{97,33},{2,66}... | collective-permute-start | bytes 49160 | tf_op jit(solution)/shard_map/ppermute | solution.py:174
  99.4 3.3 %all-to-all-done.1 = bf16[4,64,256]{2,1,0:T(8,128)(2,1)S(1)} async-done(((bf16[4,64,256]{2,1,0:T(8,128)(2,1)}), bf16[4,64,256]{2,1,0:T(8,128)(2,1)S(1)}, u32[]{:S(2)}, u32[]{:S(2)}) %all-to-all-start.1) | async-done | bytes 131104 | tf_op jit(solution)/shard_map/all_to_all | solution.py:207
  102.6 0.8 broadcast_in_dim.22
  103.5 7.0 %all-to-all-start.2 = ((bf16[16,64,256]{2,1,0:T(8,128)(2,1)}), bf16[16,64,256]{2,1,0:T(8,128)(2,1)}, u32[]{:S(2)}, u32[]{:S(2)}) async-start(bf16[16,64,256]{2,1,0:T(8,128)(2,1)} %broadcast_in_dim.22), calls=%async_computation.2 | async-start | bytes 1048576 | tf_op jit(solution)/shard_map/all_to_all | solution.py:180
  110.5 1.2 collective-permute-start.4
  111.8 2.8 %collective-permute-done.4 = f32[1,4096]{1,0:T(1,128)S(1)} collective-permute-done((f32[1,4096]{1,0:T(1,128)S(1)}, f32[1,4096]{1,0:T(1,128)S(1)}, u32[]{:S(2)}, u32[]{:S(2)}) %collective-permute-start.4) | collective-permute-done | bytes 16416 | tf_op jit(solution)/shard_map/ppermute | solution.py:174
  114.7 11.5 %all-to-all-done.2.refs_1_ = bf16[16,64,256]{2,1,0:T(8,128)(2,1)} async-done(((bf16[16,64,256]{2,1,0:T(8,128)(2,1)}), bf16[16,64,256]{2,1,0:T(8,128)(2,1)}, u32[]{:S(2)}, u32[]{:S(2)}) %all-to-all-start.2) | async-done | bytes 524320 | tf_op jit(solution)/shard_map/all_to_all | solution.py:180
  126.2 3.1 %section.5 = bf16[16,64,256]{2,1,0:T(8,128)(2,1)S(1)} custom-call(s32[3]{0:T(128)S(1)} %add_add_fusion.2.refs_0_, bf16[16,64,256]{2,1,0:T(8,128)(2,1)} %all-to-all-done.2.refs_1_, f32[4,1,4096]{2,1,0:T(1,128)S(1)} %pad_maximum_fusion.refs_2_, bf16[4096,128]{1,0:T(8,128)(2,1)S(1)} %bitcast.30, bf16[4096,128]{1,0:T(8,128)(2,1)} %collective-permute-done.5.refs_4_, ...), custom_call_target="tpu_custom_call" | custom-call | tf_op jit(solution)/shard_map/section/pallas_call | solution.py:153
  129.3 0.8 copy-done.2
  130.1 5.8 %all-to-all-start.3 = ((bf16[16,64,256]{2,1,0:T(8,128)(2,1)}), bf16[16,64,256]{2,1,0:T(8,128)(2,1)}, u32[]{:S(2)}, u32[]{:S(2)}) async-start(bf16[16,64,256]{2,1,0:T(8,128)(2,1)} %copy-done.2), calls=%async_computation.3 | async-start | bytes 1048576 | tf_op jit(solution)/shard_map/all_to_all | solution.py:180
  135.9 10.1 %all-to-all-done.3.refs_1_ = bf16[16,64,256]{2,1,0:T(8,128)(2,1)} async-done(((bf16[16,64,256]{2,1,0:T(8,128)(2,1)}), bf16[16,64,256]{2,1,0:T(8,128)(2,1)}, u32[]{:S(2)}, u32[]{:S(2)}) %all-to-all-start.3) | async-done | bytes 524320 | tf_op jit(solution)/shard_map/all_to_all | solution.py:180
  146.0 3.2 %section.6 = bf16[16,64,256]{2,1,0:T(8,128)(2,1)S(1)} custom-call(s32[3]{0:T(128)S(1)} %add_add_fusion.1.refs_0_, bf16[16,64,256]{2,1,0:T(8,128)(2,1)} %all-to-all-done.3.refs_1_, f32[4,1,4096]{2,1,0:T(1,128)S(1)} %pad_maximum_fusion.refs_2_, bf16[4096,128]{1,0:T(8,128)(2,1)S(1)} %bitcast.31, bf16[4096,128]{1,0:T(8,128)(2,1)} %collective-permute-done.5.refs_4_, ...), custom_call_target="tpu_custom_call" | custom-call | tf_op jit(solution)/shard_map/section/pallas_call | solution.py:153
  149.2 0.8 copy-done.1
  149.9 4.2 %all-to-all-start.4 = ((bf16[16,64,256]{2,1,0:T(8,128)(2,1)}), bf16[16,64,256]{2,1,0:T(8,128)(2,1)}, u32[]{:S(2)}, u32[]{:S(2)}) async-start(bf16[16,64,256]{2,1,0:T(8,128)(2,1)} %copy-done.1), calls=%async_computation.4 | async-start | bytes 1048576 | tf_op jit(solution)/shard_map/all_to_all | solution.py:180
  154.2 0.1 collective-permute-start.11
  154.4 1.6 collective-permute-done.11
  155.9 2.0 maximum_select_fusion.refs_11_
  157.9 6.4 %all-to-all-done.4.refs_1_ = bf16[16,64,256]{2,1,0:T(8,128)(2,1)} async-done(((bf16[16,64,256]{2,1,0:T(8,128)(2,1)}), bf16[16,64,256]{2,1,0:T(8,128)(2,1)}, u32[]{:S(2)}, u32[]{:S(2)}) %all-to-all-start.4) | async-done | bytes 524320 | tf_op jit(solution)/shard_map/all_to_all | solution.py:180
  164.3 1.0 copy-done.3
  165.3 4.1 %section.7 = f32[16,4,1024]{2,1,0:T(4,128)} custom-call(s32[3]{0:T(128)S(1)} %add_add_fusion.refs_0_, bf16[16,64,256]{2,1,0:T(8,128)(2,1)} %all-to-all-done.4.refs_1_, f32[4,1,4096]{2,1,0:T(1,128)S(1)} %pad_maximum_fusion.refs_2_, bf16[4096,128]{1,0:T(8,128)(2,1)S(1)} %bitcast.32, bf16[4096,128]{1,0:T(8,128)(2,1)} %collective-permute-done.5.refs_4_, ...), custom_call_target="tpu_custom_call" | custom-call | tf_op jit(solution)/shard_map/section/pallas_call | solution.py:153
  169.5 3.7 %all-to-all-start.5 = ((f32[16,4,1024]{2,1,0:T(4,128)}), f32[16,4,1024]{2,1,0:T(4,128)S(1)}, u32[]{:S(2)}, u32[]{:S(2)}) async-start(f32[16,4,1024]{2,1,0:T(4,128)} %section.7), calls=%async_computation.5 | async-start | bytes 524288 | tf_op jit(solution)/shard_map/all_to_all | solution.py:180
  173.2 0.7 copy.16.len_ref
  173.9 0.7 concatenate.33.prev_ref
  174.5 6.9 %all-to-all-done.5.parts_ref = f32[16,4,1024]{2,1,0:T(4,128)S(1)} async-done(((f32[16,4,1024]{2,1,0:T(4,128)}), f32[16,4,1024]{2,1,0:T(4,128)S(1)}, u32[]{:S(2)}, u32[]{:S(2)}) %all-to-all-start.5) | async-done | bytes 262176 | tf_op jit(solution)/shard_map/all_to_all | solution.py:180
  181.5 0.7 copy-done.5
  182.2 25.3 %char_decode.1 = f32[4,128]{1,0:T(4,128)} custom-call(f32[16,4,1024]{2,1,0:T(4,128)} %copy-done.5, s32[4,128]{1,0:T(4,128)} %bitcast.41, s32[4,128]{1,0:T(4,128)} %concatenate.33.prev_ref, s32[4,1]{1,0:T(4,128)} %copy.16.len_ref, bf16[128,1024]{1,0:T(8,128)(2,1)} %embed_ref.1, bf16[128,1024]{1,0:T(8,128)(2,1)} %pos_ref.1, f32[3,1024]{1,0:T(4,128)} %gain_ref.1, ...), custom_call_target="tpu_custom_call" | custom-call | tf_op jit(solution)/shard_map/char_decode/pallas_call | solution.py:91
  (39 shorter events, 0.6 us)
Async XLA Ops:
  6.5 174.9 %all-gather.2.cloned.1.call-start = ((), (), s32[]{:S(2)}) async-start(), calls=%async_computation.6 | async-start | bytes 25362432 | tf_op jit(solution)/shard_map/all_gather | solution.py:185
  13.1 0.7 copy-start.7
  14.8 1.3 collective-permute-start
  17.8 8.2 %copy-start = (bf16[1,4096,128]{2,1,0:T(8,128)(2,1)S(1)}, bf16[1,4096,128]{2,1,0:T(8,128)(2,1)}, u32[]{:S(2)}) copy-start(bf16[1,4096,128]{2,1,0:T(8,128)(2,1)} %param.14) | copy-start | bytes 3145732
  17.8 69.3 %copy-start.4 = (f32[1,4096]{1,0:T(1,128)S(1)}, f32[1,4096]{1,0:T(1,128)}, u32[]{:S(2)}) copy-start(f32[1,4096]{1,0:T(1,128)} %param.15) | copy-start | bytes 49156
  17.8 69.3 %all-to-all-start = ((bf16[16,256,256]{2,1,0:T(8,128)(2,1)}), bf16[16,256,256]{2,1,0:T(8,128)(2,1)}, u32[]{:S(2)}, u32[]{:S(2)}) async-start(bf16[16,256,256]{2,1,0:T(8,128)(2,1)} %broadcast_in_dim.19), calls=%async_computation | async-start | bytes 4194304 | tf_op jit(solution)/shard_map/all_to_all | solution.py:180
  25.9 42.8 %collective-permute-start.7 = (bf16[4096,128]{1,0:T(8,128)(2,1)S(1)}, bf16[4096,128]{1,0:T(8,128)(2,1)S(1)}, u32[]{:S(2)}, u32[]{:S(2)}) collective-permute-start(bf16[4096,128]{1,0:T(8,128)(2,1)S(1)} %bitcast.25), channel_id=1, source_target_pairs={{0,96},{32,0},{64,32},{96,64},{1,97},{33,1},{65,33},{97,65},{2,98}... | collective-permute-start | bytes 3145736 | tf_op jit(solution)/shard_map/ppermute | solution.py:174
  29.0 40.8 %collective-permute-start.5 = (bf16[4096,128]{1,0:T(8,128)(2,1)S(1)}, bf16[4096,128]{1,0:T(8,128)(2,1)}, u32[]{:S(2)}, u32[]{:S(2)}) collective-permute-start(bf16[4096,128]{1,0:T(8,128)(2,1)S(1)} %bitcast.26), channel_id=1, source_target_pairs={{0,32},{32,64},{64,96},{96,0},{1,33},{33,65},{65,97},{97,1},{2,34}... | collective-permute-start | bytes 3145736 | tf_op jit(solution)/shard_map/ppermute | solution.py:174
  29.0 57.9 %collective-permute-start.6 = (bf16[4096,128]{1,0:T(8,128)(2,1)S(1)}, bf16[4096,128]{1,0:T(8,128)(2,1)}, u32[]{:S(2)}, u32[]{:S(2)}) collective-permute-start(bf16[4096,128]{1,0:T(8,128)(2,1)S(1)} %bitcast.27), channel_id=1, source_target_pairs={{0,64},{32,96},{64,0},{96,32},{1,65},{33,97},{65,1},{97,33},{2,66}... | collective-permute-start | bytes 3145736 | tf_op jit(solution)/shard_map/ppermute | solution.py:174
  31.2 55.8 %collective-permute-start.1 = (bf16[4096,128]{1,0:T(8,128)(2,1)S(1)}, bf16[4096,128]{1,0:T(8,128)(2,1)S(1)}, u32[]{:S(2)}, u32[]{:S(2)}) collective-permute-start(bf16[4096,128]{1,0:T(8,128)(2,1)S(1)} %bitcast.28), channel_id=1, source_target_pairs={{0,1},{1,0},{2,3},{3,2},{4,5},{5,4},{6,7},{7,6},{8,9},{9,8},{10,11... | collective-permute-start | bytes 3145736 | tf_op jit(solution)/shard_map/ppermute | solution.py:171
  68.7 46.0 %collective-permute-start.10 = (bf16[4096,128]{1,0:T(8,128)(2,1)S(1)}, bf16[4096,128]{1,0:T(8,128)(2,1)}, u32[]{:S(2)}, u32[]{:S(2)}) collective-permute-start(bf16[4096,128]{1,0:T(8,128)(2,1)S(1)} %collective-permute-done.7.refs_6_), channel_id=1, source_target_pairs={{0,1},{1,0},{2,3},{3,2},{4,5},{5,4},{6,7},{7,6},{8,9},{9,8},{10,11... | collective-permute-start | bytes 3145736 | tf_op jit(solution)/shard_map/ppermute | solution.py:171
  69.8 44.9 %collective-permute-start.8 = (bf16[4096,128]{1,0:T(8,128)(2,1)}, bf16[4096,128]{1,0:T(8,128)(2,1)}, u32[]{:S(2)}, u32[]{:S(2)}) collective-permute-start(bf16[4096,128]{1,0:T(8,128)(2,1)} %collective-permute-done.5.refs_4_), channel_id=1, source_target_pairs={{0,1},{1,0},{2,3},{3,2},{4,5},{5,4},{6,7},{7,6},{8,9},{9,8},{10,11... | collective-permute-start | bytes 3145736 | tf_op jit(solution)/shard_map/ppermute | solution.py:171
  86.9 27.7 %collective-permute-start.9 = (bf16[4096,128]{1,0:T(8,128)(2,1)}, bf16[4096,128]{1,0:T(8,128)(2,1)}, u32[]{:S(2)}, u32[]{:S(2)}) collective-permute-start(bf16[4096,128]{1,0:T(8,128)(2,1)} %collective-permute-done.6.refs_5_), channel_id=1, source_target_pairs={{0,1},{1,0},{2,3},{3,2},{4,5},{5,4},{6,7},{7,6},{8,9},{9,8},{10,11... | collective-permute-start | bytes 3145736 | tf_op jit(solution)/shard_map/ppermute | solution.py:171
  91.4 11.3 %all-to-all-start.1 = ((bf16[4,64,256]{2,1,0:T(8,128)(2,1)}), bf16[4,64,256]{2,1,0:T(8,128)(2,1)S(1)}, u32[]{:S(2)}, u32[]{:S(2)}) async-start(bf16[4,64,256]{2,1,0:T(8,128)(2,1)} %section.4), calls=%async_computation.1 | async-start | bytes 262144 | tf_op jit(solution)/shard_map/all_to_all | solution.py:207
  94.7 15.8 %collective-permute-start.2 = (f32[1,4096]{1,0:T(1,128)S(1)}, f32[1,4096]{1,0:T(1,128)S(1)}, u32[]{:S(2)}, u32[]{:S(2)}) collective-permute-start(f32[1,4096]{1,0:T(1,128)S(1)} %copy-done.4), channel_id=1, source_target_pairs={{0,32},{32,64},{64,96},{96,0},{1,33},{33,65},{65,97},{97,1},{2,34}... | collective-permute-start | bytes 49160 | tf_op jit(solution)/shard_map/ppermute | solution.py:174
  96.7 15.1 %collective-permute-start.3 = (f32[1,4096]{1,0:T(1,128)S(1)}, f32[1,4096]{1,0:T(1,128)S(1)}, u32[]{:S(2)}, u32[]{:S(2)}) collective-permute-start(f32[1,4096]{1,0:T(1,128)S(1)} %copy-done.4), channel_id=1, source_target_pairs={{0,64},{32,96},{64,0},{96,32},{1,65},{33,97},{65,1},{97,33},{2,66}... | collective-permute-start | bytes 49160 | tf_op jit(solution)/shard_map/ppermute | solution.py:174
  103.5 22.7 %all-to-all-start.2 = ((bf16[16,64,256]{2,1,0:T(8,128)(2,1)}), bf16[16,64,256]{2,1,0:T(8,128)(2,1)}, u32[]{:S(2)}, u32[]{:S(2)}) async-start(bf16[16,64,256]{2,1,0:T(8,128)(2,1)} %broadcast_in_dim.22), calls=%async_computation.2 | async-start | bytes 1048576 | tf_op jit(solution)/shard_map/all_to_all | solution.py:180
  110.5 4.1 %collective-permute-start.4 = (f32[1,4096]{1,0:T(1,128)S(1)}, f32[1,4096]{1,0:T(1,128)S(1)}, u32[]{:S(2)}, u32[]{:S(2)}) collective-permute-start(f32[1,4096]{1,0:T(1,128)S(1)} %copy-done.4), channel_id=1, source_target_pairs={{0,96},{32,0},{64,32},{96,64},{1,97},{33,1},{65,33},{97,65},{2,98}... | collective-permute-start | bytes 49160 | tf_op jit(solution)/shard_map/ppermute | solution.py:174
  129.3 0.8 copy-start.2
  130.1 15.9 %all-to-all-start.3 = ((bf16[16,64,256]{2,1,0:T(8,128)(2,1)}), bf16[16,64,256]{2,1,0:T(8,128)(2,1)}, u32[]{:S(2)}, u32[]{:S(2)}) async-start(bf16[16,64,256]{2,1,0:T(8,128)(2,1)} %copy-done.2), calls=%async_computation.3 | async-start | bytes 1048576 | tf_op jit(solution)/shard_map/all_to_all | solution.py:180
  135.9 18.3 %copy-start.6 = (bf16[128,1024]{1,0:T(8,128)(2,1)S(1)}, bf16[128,1024]{1,0:T(8,128)(2,1)}, u32[]{:S(2)}) copy-start(bf16[128,1024]{1,0:T(8,128)(2,1)} %param.16) | copy-start | bytes 786436
  149.1 0.8 copy-start.1
  149.9 14.4 %all-to-all-start.4 = ((bf16[16,64,256]{2,1,0:T(8,128)(2,1)}), bf16[16,64,256]{2,1,0:T(8,128)(2,1)}, u32[]{:S(2)}, u32[]{:S(2)}) async-start(bf16[16,64,256]{2,1,0:T(8,128)(2,1)} %copy-done.1), calls=%async_computation.4 | async-start | bytes 1048576 | tf_op jit(solution)/shard_map/all_to_all | solution.py:180
  154.2 1.7 collective-permute-start.11
  164.3 1.0 copy-start.3
  165.3 7.9 %copy-start.9 = (s32[1,4]{1,0:T(1,128)S(1)}, s32[1,4]{1,0:T(1,128)}, u32[]{:S(2)}) copy-start(s32[1,4]{1,0:T(1,128)} %param.18) | copy-start | bytes 52
  165.3 8.6 %copy-start.8 = (s32[1,4,128]{2,1,0:T(4,128)S(1)}, s32[1,4,128]{2,1,0:T(4,128)}, u32[]{:S(2)}) copy-start(s32[1,4,128]{2,1,0:T(4,128)} %param.17) | copy-start | bytes 6148
  169.5 12.0 %all-to-all-start.5 = ((f32[16,4,1024]{2,1,0:T(4,128)}), f32[16,4,1024]{2,1,0:T(4,128)S(1)}, u32[]{:S(2)}, u32[]{:S(2)}) async-start(f32[16,4,1024]{2,1,0:T(4,128)} %section.7), calls=%async_computation.5 | async-start | bytes 524288 | tf_op jit(solution)/shard_map/all_to_all | solution.py:180
  181.4 0.7 copy-start.5
Sparse Core Ops, SparseCore 0:
  14.0 125.8 all-gather.1

commit v2 on v1

--- a/solution.py
+++ b/solution.py
@@ -104,61 +104,118 @@
 GROUP = ("y", "x", "z", "c")
 
 
-def section_kernel(copies, project, where_ref, x_ref, gain_ref, *refs):
-    own, other = refs[:copies], refs[copies:2 * copies]
-    refs = refs[2 * copies:]
+def section_kernel(project, where_ref, x_ref, *refs):
+    own, other, refs = refs[:4], refs[4:8], refs[8:]
     if project:
-        proj_ref, refs = refs[0], refs[1:]
-    out_ref, n_ref, w_ref, sems = refs
+        proj_own, proj_other, out_ref, w_ref, sems, p_ref, p_sems = refs
+    else:
+        out_ref, w_ref, sems, row_ref, out_sems = refs
     blocks, rows, cols = x_ref.shape
-    half = cols // 2
+    side, depth = cols // 2, blocks * cols
+    half = depth // 2
     which, core, chip = where_ref[0], where_ref[1], where_ref[2]
-    first = pl.ds(pl.multiple_of(core * half, half), half)
-    second = pl.ds(pl.multiple_of((1 - core) * half, half), half)
-    for i in range(copies):
+    for i in range(4):
         @pl.when(which == i)
         def _():
-            pltpu.make_async_copy(own[i], w_ref.at[:, first], sems.at[0]).start()
-            pltpu.make_async_copy(other[i], w_ref.at[:, second], sems.at[1]).start()
+            for sources, at, sem in ((own, core, 0), (other, 1 - core, 1)):
+                lanes = pl.ds(pl.multiple_of(at * side, side), side)
+                for part in range(2):
+                    span = pl.ds(part * half, half)
+                    pltpu.make_async_copy(
+                        sources[i].at[span], w_ref.at[span, lanes], sems.at[2 * sem + part]
+                    ).start()
+    if project:
+        deep = proj_own.shape[0]
+        loads = [
+            pltpu.make_async_copy(source, p_ref.at[pl.ds(pl.multiple_of(at * deep, deep), deep)], p_sems.at[i])
+            for i, (source, at) in enumerate(((proj_own, core), (proj_other, 1 - core)))
+        ]
+        for load in loads:
+            load.start()
     total = jnp.zeros((rows, cols), F32)
     for j in range(blocks):
         v = x_ref[j].astype(F32)
         total += v * v
-    scale = lax.rsqrt(jnp.sum(total, axis=-1, keepdims=True) / (blocks * cols) + 1e-05)
-    gain = gain_ref[which]
-    for j in range(blocks):
-        span = slice(j * cols, (j + 1) * cols)
-        n_ref[:, span] = (x_ref[j].astype(F32) * scale * gain[:, span]).astype(BF)
-    pltpu.make_async_copy(own[0], w_ref.at[:, first], sems.at[0]).wait()
-    pltpu.make_async_copy(other[0], w_ref.at[:, second], sems.at[1]).wait()
-    update = jax.nn.gelu(jnp.dot(n_ref[...], w_ref[...], preferred_element_type=F32))
+    scale = lax.rsqrt(jnp.sum(total, axis=-1, keepdims=True) / depth + 1e-05)
+    for i in range(4):
+        span = pl.ds(i % 2 * half, half)
+        pltpu.make_async_copy(own[0].at[span], w_ref.at[span, pl.ds(i // 2 * side, side)], sems.at[i]).wait()
+    wide = jnp.concatenate([x_ref[j] for j in range(blocks)], axis=1)
+    update = jax.nn.gelu(jnp.dot(wide, w_ref[...], preferred_element_type=F32) * scale)
     leaving = (x_ref[chip].astype(F32) + update).astype(BF)
     if project:
-        partial = jnp.dot(leaving, proj_ref[...], preferred_element_type=F32)
+        for load in loads:
+            load.wait()
+        partial = jnp.dot(leaving, p_ref[...], preferred_element_type=F32)
         each = rows // blocks
         for j in range(blocks):
             out_ref[j] = partial[j * each:(j + 1) * each]
     else:
-        each = out_ref.shape[1]
-        for j in range(out_ref.shape[0]):
-            out_ref[j] = leaving if each == rows else leaving[j * each:(j + 1) * each]
-
-
-def section_step(where, x, gain, own, other, out_shape, proj=None):
+        row_ref[...] = leaving
+        sends = [pltpu.make_async_copy(row_ref, out_ref.at[j], out_sems.at[j]) for j in range(blocks)]
+        for send in sends:
+            send.start()
+        for send in sends:
+            send.wait()
+
+
+def section_step(where, x, own, other, proj=None):
     blocks, rows, cols = x.shape
-    depth = blocks * cols
     vm = pl.BlockSpec(memory_space=pltpu.VMEM)
     hbm = pl.BlockSpec(memory_space=pl.ANY)
-    extra = [] if proj is None else [proj]
+    scratch = [pltpu.VMEM((blocks * cols, cols), BF), pltpu.SemaphoreType.DMA((4,))]
+    if proj is None:
+        proj, out, out_spec = [], jax.ShapeDtypeStruct(x.shape, BF), hbm
+        scratch += [pltpu.VMEM((rows, cols), BF), pltpu.SemaphoreType.DMA((blocks,))]
+    else:
+        width = proj[0].shape[1]
+        out, out_spec = jax.ShapeDtypeStruct((blocks, rows // blocks, width), F32), vm
+        scratch += [pltpu.VMEM((cols, width), BF), pltpu.SemaphoreType.DMA((2,))]
     return pl.pallas_call(
-        lambda *refs: section_kernel(len(own), proj is not None, *refs),
-        out_shape=out_shape,
-        in_specs=[pl.BlockSpec(memory_space=pltpu.SMEM), vm, vm] + [hbm] * (2 * len(own)) + [vm] * len(extra),
-        out_specs=vm,
-        scratch_shapes=[pltpu.VMEM((rows, depth), BF), pltpu.VMEM((depth, cols), BF), pltpu.SemaphoreType.DMA((2,))],
-        compiler_params=pltpu.CompilerParams(vmem_limit_bytes=32 << 20),
+        lambda *refs: section_kernel(len(proj) > 0, *refs),
+        out_shape=out,
+        in_specs=[pl.BlockSpec(memory_space=pltpu.SMEM), vm] + [hbm] * (8 + len(proj)),
+        out_specs=out_spec,
+        scratch_shapes=scratch,
+        compiler_params=pltpu.CompilerParams(vmem_limit_bytes=16 << 20),
+        cost_estimate=pl.CostEstimate(flops=1, bytes_accessed=1, transcendentals=0),
         name="section",
-    )(where, x, gain, *own, *other, *extra)
+    )(where, x, *own, *other, *proj)
+
+
+def gain_kernel(w_ref, gain_ref, out_ref):
+    for i in range(gain_ref.shape[0]):
+        span = slice(i * 128, (i + 1) * 128)
+        column = jnp.transpose(jnp.broadcast_to(gain_ref[i:i + 1, :], (128, 128)))
+        out_ref[span, :] = (w_ref[span, :].astype(F32) * column).astype(BF)
+
+
+def pack_kernel(a_ref, o_ref, u_ref, d_ref, out_ref):
+    width = o_ref.shape[1]
+    for i in range(3):
+        out_ref[i] = a_ref[:, i * width:(i + 1) * width]
+    out_ref[3] = o_ref[...]
+    for i in range(4):
+        out_ref[4 + i] = u_ref[:, i * width:(i + 1) * width]
+        out_ref[8 + i] = d_ref[8 * i:8 * i + 8]
+
+
+def after_kernel(*refs):
+    pass
+
+
+def after(first, arrays):
+    hbm = pl.BlockSpec(memory_space=pl.ANY)
+    return pl.pallas_call(
+        after_kernel,
+        out_shape=[jax.ShapeDtypeStruct(v.shape, v.dtype) for v in arrays],
+        in_specs=[hbm] * (len(first) + len(arrays)),
+        out_specs=[hbm] * len(arrays),
+        input_output_aliases={i + len(first): i for i in range(len(arrays))},
+        compiler_params=pltpu.CompilerParams(vmem_limit_bytes=1 << 20),
+        cost_estimate=pl.CostEstimate(flops=1, bytes_accessed=1, transcendentals=0),
+        name="after",
+    )(*first, *arrays)
 
 
 def body(bar_in, section_weight, section_gain, projection, char_ids, lengths, char_embed, char_pos,
@@ -179,38 +236,33 @@
     def spread(v):
         return lax.all_to_all(v, ("x", "z"), 0, 0, tiled=True)
 
-    pack = jnp.concatenate(
-        [attn_in[:, i * width:(i + 1) * width] for i in range(3)] + [attn_out]
-        + [ffn_in[:, i * width:(i + 1) * width] for i in range(4)] + [ffn_out], axis=0)
-    pack = lax.all_gather(pack, GROUP, axis=0, tiled=True).reshape(128, 12, 8, width)
-
-    own = [section_weight[0]]
-    gains = [section_gain]
-    for by in (1, 2, 3):
-        own.append(turn(section_weight[0], by))
-        gains.append(turn(section_gain, by))
-    other = [swap(w) for w in own]
-    proj = ordered(projection, swap(projection), 0)
-
-    micro, bars, feats = bar_in.shape
-    by_core = bar_in.reshape(micro, 16, 2, 4, feats).transpose(2, 0, 1, 3, 4).reshape(2, micro * 64, feats)
+    pack = pl.pallas_call(
+        pack_kernel, out_shape=jax.ShapeDtypeStruct((12, 8, width), BF), name="pack",
+    )(attn_in, attn_out, ffn_in, ffn_out)
+    pack = lax.all_gather(pack.reshape(96, width), GROUP, axis=0, tiled=True).reshape(128, 12, 8, width)
+
+    feats = bar_in.shape[2]
+    weight = pl.pallas_call(
+        gain_kernel, out_shape=jax.ShapeDtypeStruct(section_weight.shape[1:], BF),
+        compiler_params=pltpu.CompilerParams(vmem_limit_bytes=8 << 20), name="gain",
+    )(section_weight[0], section_gain.reshape(-1, 128))
+
+    by_core = lax.dynamic_index_in_dim(bar_in, y, 0, keepdims=False).reshape(16, 2, 4, feats)
+    by_core = by_core.transpose(1, 0, 2, 3).reshape(2, 64, feats)
     mine = lax.dynamic_index_in_dim(by_core, core, 0, keepdims=False)
     theirs = swap(lax.dynamic_index_in_dim(by_core, 1 - core, 0, keepdims=False))
     block = ordered(mine, theirs, 1)
-    x = spread(jnp.broadcast_to(block[None], (16,) + block.shape))
-
-    def where(step):
-        return jnp.stack([lax.rem(y - step + 4, 4) if step else jnp.int32(0), core, chip])
-
-    first = section_step(where(0), x, section_gain[None], own[:1], other[:1],
-                         jax.ShapeDtypeStruct((micro, 64, 2 * feats), BF))
-    rows = lax.all_to_all(first, "y", 0, 0, tiled=True)[0]
-    out = jnp.broadcast_to(rows[None], (16,) + rows.shape)
-    gain = jnp.stack(gains)
-    for step in (1, 2, 3):
-        x = spread(out)
-        shape = jax.ShapeDtypeStruct((16, 64, 2 * feats), BF) if step < 3 else jax.ShapeDtypeStruct((16, 4, width), F32)
-        out = section_step(where(step), x, gain, own, other, shape, proj if step == 3 else None)
+
+    out = jnp.broadcast_to(block[None], (16,) + block.shape)
+    x = spread(out)
+    own = [weight, *after([x], [turn(weight, by) for by in (1, 2, 3)])]
+    other = [swap(w) for w in own]
+    proj = [projection, swap(projection)]
+    for step in range(4):
+        if step:
+            x = spread(out)
+        where = jnp.stack([lax.rem(y - step + 4, 4), core, chip])
+        out = section_step(where, x, own, other, proj if step == 3 else None)
     parts = spread(out)
     return char_decode(parts, char_ids[0], lengths[0], char_embed, char_pos, norm_gain, pack)[None]
 

time: 216 us -> 197 us (0.912)
  waiting for transfers between devices: 99.5 us -> 90.8 us
  local copies, waits for them, and re-layouts: 15.3 us -> 9.27 us
  starting transfers between devices: 43.5 us -> 38.3 us
  Pallas kernels: 39.9 us -> 43.3 us
    ppermute x6 -> x3, waiting for transfers between devices: 58.5 us -> 21 us  [turn(): return lax.ppermute(v, 'y', [(i, (i + by) % 4) for i in range(4)])]
    all_to_all x5, waiting for transfers between devices: 34.8 us -> 61.4 us  [spread(): return lax.all_to_all(v, ('x', 'z'), 0, 0, tiled=True)]
    ppermute x6, waiting for transfers between devices: 2.82 us -> 8.43 us  [swap(): return lax.ppermute(v, 'c', [(0, 1), (1, 0)])]
    ppermute x6 -> x3, starting transfers between devices: 11.2 us -> 5.98 us  [turn(): return lax.ppermute(v, 'y', [(i, (i + by) % 4) for i in range(4)])]
    unnamed x28 -> x20, local copies, waits for them, and re-layouts: 9.75 us -> 5.12 us
    all_to_all x1 -> x0, starting transfers between devices: 3.33 us -> none  [body(): rows = lax.all_to_all(first, 'y', 0, 0, tiled=True)[0]]
    pallas_call x4 -> x7, Pallas kernels: 14.7 us -> 18 us  [the longest x4 15.7 us: section_step(): pl.pallas_call(lambda *refs: section_kernel(len(proj) > 0, *refs), out_sh...]
    all_to_all x1 -> x0, waiting for transfers between devices: 3.28 us -> none  [body(): rows = lax.all_to_all(first, 'y', 0, 0, tiled=True)[0]]
  transfers between devices with their start and end apart: 19 -> 15, of which waited for: 11 -> 11; matrix products, arithmetic and copies ran while one was open for 3% -> 3% of each run, Pallas kernels for 7% -> 8%
where the time goes in v2:
time: 197 us; the launch traced here: 196 us
  waiting for transfers between devices  90.8 us (46%)
  Pallas kernels  43.3 us (22%)
  starting transfers between devices  38.3 us (19%)
  between operations  13.6 us (7%)
  local copies, waits for them, and re-layouts  9.27 us (5%)
    all_to_all x5, waiting for transfers between devices, spread(): return lax.all_to_all(v, ('x', 'z'), 0, 0, tiled=True)  61.4 us
    all_to_all x5, starting transfers between devices, spread(): return lax.all_to_all(v, ('x', 'z'), 0, 0, tiled=True)  31.6 us
    pallas_call x1, Pallas kernels, char_decode(): pl.pallas_call(char_kernel, out_shape=jax.ShapeDtypeStruct((bars, chars),...  25.3 us
    ppermute x3, waiting for transfers between devices, turn(): return lax.ppermute(v, 'y', [(i, (i + by) % 4) for i in range(4)])  21 us
    pallas_call x4, Pallas kernels, section_step(): pl.pallas_call(lambda *refs: section_kernel(len(proj) > 0, *refs), out_sh...  15.7 us
    ppermute x6, waiting for transfers between devices, swap(): return lax.ppermute(v, 'c', [(0, 1), (1, 0)])  8.43 us
    ppermute x3, starting transfers between devices, turn(): return lax.ppermute(v, 'y', [(i, (i + by) % 4) for i in range(4)])  5.98 us
    unnamed x20, local copies, waits for them, and re-layouts  5.12 us
  transfers between devices with their start and end apart: 15, of which 11 were waited for; matrix products, arithmetic and copies ran while one was open for 3% of the time, Pallas kernels for 8%

profile of v2, /device:TPU:0, one launch (start us, length us, event | category | flops | bytes accessed | tf_op | source)
XLA Modules:
  0.0 196.3 jit_solution(8589137754355840271)
XLA Ops:
  6.5 1.7 pack.1
  8.2 0.0 all-gather.2.cloned.1.call-update
  8.2 0.0 copy-start.4
  8.2 1.2 copy-done.4
  9.5 0.7 copy-done.6
  10.2 0.6 gain.1.refs_2_
  10.8 1.7 collective-permute-start.1
  12.5 2.9 %collective-permute-start.2 = (bf16[4096,128]{1,0:T(8,128)(2,1)S(1)}, bf16[4096,128]{1,0:T(8,128)(2,1)S(1)}, u32[]{:S(2)}, u32[]{:S(2)}) collective-permute-start(bf16[4096,128]{1,0:T(8,128)(2,1)S(1)} %gain.1.refs_2_), channel_id=1, source_target_pairs={{0,64},{32,96},{64,0},{96,32},{1,65},{33,97},{65,1},{97,33},{2,66}... | collective-permute-start | bytes 3145736 | tf_op jit(solution)/shard_map/ppermute | solution.py:231
  15.4 1.3 collective-permute-start.3
  16.8 0.6 copy.19
  17.4 1.3 dynamic-slice_bitcast_fusion.1
  18.7 1.5 collective-permute-done
  20.2 0.8 maximum_select_fusion
  21.1 0.8 broadcast_in_dim.4
  21.9 7.9 %all-to-all-start = ((bf16[16,64,256]{2,1,0:T(8,128)(2,1)}), bf16[16,64,256]{2,1,0:T(8,128)(2,1)}, u32[]{:S(2)}, u32[]{:S(2)}) async-start(bf16[16,64,256]{2,1,0:T(8,128)(2,1)} %broadcast_in_dim.4), calls=%async_computation | async-start | bytes 1048576 | tf_op jit(solution)/shard_map/all_to_all | solution.py:237
  29.9 0.1 collective-permute-start.4
  30.0 12.0 %all-to-all-done.refs_0_.refs_1_ = bf16[16,64,256]{2,1,0:T(8,128)(2,1)} async-done(((bf16[16,64,256]{2,1,0:T(8,128)(2,1)}), bf16[16,64,256]{2,1,0:T(8,128)(2,1)}, u32[]{:S(2)}, u32[]{:S(2)}) %all-to-all-start) | async-done | bytes 524320 | tf_op jit(solution)/shard_map/all_to_all | solution.py:237
  42.0 21.0 %collective-permute-done.2.refs_2_ = bf16[4096,128]{1,0:T(8,128)(2,1)S(1)} collective-permute-done((bf16[4096,128]{1,0:T(8,128)(2,1)S(1)}, bf16[4096,128]{1,0:T(8,128)(2,1)S(1)}, u32[]{:S(2)}, u32[]{:S(2)}) %collective-permute-start.2) | collective-permute-done | bytes 1048608 | tf_op jit(solution)/shard_map/ppermute | solution.py:231
  63.0 0.5 collective-permute-start.6
  63.5 0.1 collective-permute-start.7
  63.6 0.1 add_add_fusion.3.refs_0_
  63.6 2.1 %collective-permute-done.5.refs_7_ = bf16[4096,128]{1,0:T(8,128)(2,1)} collective-permute-done((bf16[4096,128]{1,0:T(8,128)(2,1)S(1)}, bf16[4096,128]{1,0:T(8,128)(2,1)}, u32[]{:S(2)}, u32[]{:S(2)}) %collective-permute-start.5) | collective-permute-done | bytes 1048608 | tf_op jit(solution)/shard_map/ppermute | solution.py:228
  65.8 3.0 %collective-permute-done.6.refs_8_ = bf16[4096,128]{1,0:T(8,128)(2,1)} collective-permute-done((bf16[4096,128]{1,0:T(8,128)(2,1)S(1)}, bf16[4096,128]{1,0:T(8,128)(2,1)}, u32[]{:S(2)}, u32[]{:S(2)}) %collective-permute-start.6) | collective-permute-done | bytes 1048608 | tf_op jit(solution)/shard_map/ppermute | solution.py:228
  68.8 0.2 collective-permute-done.7.refs_9_
  69.0 3.8 %section.4 = bf16[16,64,256]{2,1,0:T(8,128)(2,1)S(1)} custom-call(s32[3]{0:T(128)S(1)} %add_add_fusion.3.refs_0_, bf16[16,64,256]{2,1,0:T(8,128)(2,1)} %all-to-all-done.refs_0_.refs_1_, bf16[4096,128]{1,0:T(8,128)(2,1)S(1)} %gain.1.refs_2_, bf16[4096,128]{1,0:T(8,128)(2,1)S(1)} %get-tuple-element.8.refs_3_, bf16[4096,128]{1,0:T(8,128)(2,1)S(1)} %get-tuple-element.9.refs_4_, ...), custom_call_target="tpu_custom_call" | custom-call | flops 1 | bytes 1 | tf_op jit(solution)/shard_map/section/pallas_call | solution.py:174
  72.8 0.8 copy-done.3
  73.6 8.1 %all-to-all-start.1 = ((bf16[16,64,256]{2,1,0:T(8,128)(2,1)}), bf16[16,64,256]{2,1,0:T(8,128)(2,1)}, u32[]{:S(2)}, u32[]{:S(2)}) async-start(bf16[16,64,256]{2,1,0:T(8,128)(2,1)} %copy-done.3), calls=%async_computation.1 | async-start | bytes 1048576 | tf_op jit(solution)/shard_map/all_to_all | solution.py:237
  81.8 0.1 add_add_fusion.2.refs_0_
  81.9 13.0 %all-to-all-done.1.refs_1_ = bf16[16,64,256]{2,1,0:T(8,128)(2,1)} async-done(((bf16[16,64,256]{2,1,0:T(8,128)(2,1)}), bf16[16,64,256]{2,1,0:T(8,128)(2,1)}, u32[]{:S(2)}, u32[]{:S(2)}) %all-to-all-start.1) | async-done | bytes 524320 | tf_op jit(solution)/shard_map/all_to_all | solution.py:237
  94.8 4.0 %section.5 = bf16[16,64,256]{2,1,0:T(8,128)(2,1)S(1)} custom-call(s32[3]{0:T(128)S(1)} %add_add_fusion.2.refs_0_, bf16[16,64,256]{2,1,0:T(8,128)(2,1)} %all-to-all-done.1.refs_1_, bf16[4096,128]{1,0:T(8,128)(2,1)S(1)} %gain.1.refs_2_, bf16[4096,128]{1,0:T(8,128)(2,1)S(1)} %get-tuple-element.8.refs_3_, bf16[4096,128]{1,0:T(8,128)(2,1)S(1)} %get-tuple-element.9.refs_4_, ...), custom_call_target="tpu_custom_call" | custom-call | flops 1 | bytes 1 | tf_op jit(solution)/shard_map/section/pallas_call | solution.py:174
  98.8 0.8 copy-done.2
  99.6 4.2 %all-to-all-start.2 = ((bf16[16,64,256]{2,1,0:T(8,128)(2,1)}), bf16[16,64,256]{2,1,0:T(8,128)(2,1)}, u32[]{:S(2)}, u32[]{:S(2)}) async-start(bf16[16,64,256]{2,1,0:T(8,128)(2,1)} %copy-done.2), calls=%async_computation.2 | async-start | bytes 1048576 | tf_op jit(solution)/shard_map/all_to_all | solution.py:237
  103.9 0.1 add_add_fusion.1.refs_0_
  103.9 15.6 %all-to-all-done.2.refs_1_ = bf16[16,64,256]{2,1,0:T(8,128)(2,1)} async-done(((bf16[16,64,256]{2,1,0:T(8,128)(2,1)}), bf16[16,64,256]{2,1,0:T(8,128)(2,1)}, u32[]{:S(2)}, u32[]{:S(2)}) %all-to-all-start.2) | async-done | bytes 524320 | tf_op jit(solution)/shard_map/all_to_all | solution.py:237
  119.5 3.9 %section.6 = bf16[16,64,256]{2,1,0:T(8,128)(2,1)S(1)} custom-call(s32[3]{0:T(128)S(1)} %add_add_fusion.1.refs_0_, bf16[16,64,256]{2,1,0:T(8,128)(2,1)} %all-to-all-done.2.refs_1_, bf16[4096,128]{1,0:T(8,128)(2,1)S(1)} %gain.1.refs_2_, bf16[4096,128]{1,0:T(8,128)(2,1)S(1)} %get-tuple-element.8.refs_3_, bf16[4096,128]{1,0:T(8,128)(2,1)S(1)} %get-tuple-element.9.refs_4_, ...), custom_call_target="tpu_custom_call" | custom-call | flops 1 | bytes 1 | tf_op jit(solution)/shard_map/section/pallas_call | solution.py:174
  123.4 0.8 copy-done.1
  124.3 5.7 %all-to-all-start.3 = ((bf16[16,64,256]{2,1,0:T(8,128)(2,1)}), bf16[16,64,256]{2,1,0:T(8,128)(2,1)}, u32[]{:S(2)}, u32[]{:S(2)}) async-start(bf16[16,64,256]{2,1,0:T(8,128)(2,1)} %copy-done.1), calls=%async_computation.3 | async-start | bytes 1048576 | tf_op jit(solution)/shard_map/all_to_all | solution.py:237
  129.9 0.1 collective-permute-start.8
  130.0 0.1 add_add_fusion.refs_0_
  130.1 1.6 collective-permute-done.8.refs_11_
  131.7 13.7 %all-to-all-done.3.refs_1_ = bf16[16,64,256]{2,1,0:T(8,128)(2,1)} async-done(((bf16[16,64,256]{2,1,0:T(8,128)(2,1)}), bf16[16,64,256]{2,1,0:T(8,128)(2,1)}, u32[]{:S(2)}, u32[]{:S(2)}) %all-to-all-start.3) | async-done | bytes 524320 | tf_op jit(solution)/shard_map/all_to_all | solution.py:237
  145.4 4.0 %section.7 = f32[16,4,1024]{2,1,0:T(4,128)} custom-call(s32[3]{0:T(128)S(1)} %add_add_fusion.refs_0_, bf16[16,64,256]{2,1,0:T(8,128)(2,1)} %all-to-all-done.3.refs_1_, bf16[4096,128]{1,0:T(8,128)(2,1)S(1)} %gain.1.refs_2_, bf16[4096,128]{1,0:T(8,128)(2,1)S(1)} %get-tuple-element.8.refs_3_, bf16[4096,128]{1,0:T(8,128)(2,1)S(1)} %get-tuple-element.9.refs_4_, ...), custom_call_target="tpu_custom_call" | custom-call | flops 1 | bytes 1 | tf_op jit(solution)/shard_map/section/pallas_call | solution.py:174
  149.4 5.6 %all-to-all-start.4 = ((f32[16,4,1024]{2,1,0:T(4,128)}), f32[16,4,1024]{2,1,0:T(4,128)S(1)}, u32[]{:S(2)}, u32[]{:S(2)}) async-start(f32[16,4,1024]{2,1,0:T(4,128)} %section.7), calls=%async_computation.4 | async-start | bytes 524288 | tf_op jit(solution)/shard_map/all_to_all | solution.py:237
  155.0 0.7 copy.20.len_ref
  155.7 0.7 concatenate.22.prev_ref
  156.4 7.1 %all-to-all-done.4.parts_ref = f32[16,4,1024]{2,1,0:T(4,128)S(1)} async-done(((f32[16,4,1024]{2,1,0:T(4,128)}), f32[16,4,1024]{2,1,0:T(4,128)S(1)}, u32[]{:S(2)}, u32[]{:S(2)}) %all-to-all-start.4) | async-done | bytes 262176 | tf_op jit(solution)/shard_map/all_to_all | solution.py:237
  163.5 0.7 copy-done.7
  164.2 25.3 %char_decode.1 = f32[4,128]{1,0:T(4,128)} custom-call(f32[16,4,1024]{2,1,0:T(4,128)} %copy-done.7, s32[4,128]{1,0:T(4,128)} %bitcast.28, s32[4,128]{1,0:T(4,128)} %concatenate.22.prev_ref, s32[4,1]{1,0:T(4,128)} %copy.20.len_ref, bf16[128,1024]{1,0:T(8,128)(2,1)} %embed_ref.1, bf16[128,1024]{1,0:T(8,128)(2,1)} %pos_ref.1, f32[3,1024]{1,0:T(4,128)} %gain_ref.1, ...), custom_call_target="tpu_custom_call" | custom-call | tf_op jit(solution)/shard_map/char_decode/pallas_call | solution.py:91
  (22 shorter events, 0.1 us)
Async XLA Ops:
  6.5 10.2 %copy-start = (bf16[4,128,128]{2,1,0:T(8,128)(2,1)S(1)}, bf16[4,128,128]{2,1,0:T(8,128)(2,1)}, u32[]{:S(2)}) copy-start(bf16[4,128,128]{2,1,0:T(8,128)(2,1)} %param.13) | copy-start | bytes 393220
  6.5 123.4 %copy-start.5 = (bf16[128,1024]{1,0:T(8,128)(2,1)S(1)}, bf16[128,1024]{1,0:T(8,128)(2,1)}, u32[]{:S(2)}) copy-start(bf16[128,1024]{1,0:T(8,128)(2,1)} %refs_10_.1) | copy-start | bytes 786436
  6.5 156.9 %all-gather.2.cloned.1.call-start = ((), (), s32[]{:S(2)}) async-start(), calls=%async_computation.5 | async-start | bytes 25362432 | tf_op jit(solution)/shard_map/all_gather | solution.py:242
  8.2 1.2 copy-start.4
  9.5 0.7 copy-start.6
  10.8 31.2 %collective-permute-start.1 = (bf16[4096,128]{1,0:T(8,128)(2,1)S(1)}, bf16[4096,128]{1,0:T(8,128)(2,1)S(1)}, u32[]{:S(2)}, u32[]{:S(2)}) collective-permute-start(bf16[4096,128]{1,0:T(8,128)(2,1)S(1)} %gain.1.refs_2_), channel_id=1, source_target_pairs={{0,32},{32,64},{64,96},{96,0},{1,33},{33,65},{65,97},{97,1},{2,34}... | collective-permute-start | bytes 3145736 | tf_op jit(solution)/shard_map/ppermute | solution.py:231
  12.5 50.4 %collective-permute-start.2 = (bf16[4096,128]{1,0:T(8,128)(2,1)S(1)}, bf16[4096,128]{1,0:T(8,128)(2,1)S(1)}, u32[]{:S(2)}, u32[]{:S(2)}) collective-permute-start(bf16[4096,128]{1,0:T(8,128)(2,1)S(1)} %gain.1.refs_2_), channel_id=1, source_target_pairs={{0,64},{32,96},{64,0},{96,32},{1,65},{33,97},{65,1},{97,33},{2,66}... | collective-permute-start | bytes 3145736 | tf_op jit(solution)/shard_map/ppermute | solution.py:231
  15.4 47.5 %collective-permute-start.3 = (bf16[4096,128]{1,0:T(8,128)(2,1)S(1)}, bf16[4096,128]{1,0:T(8,128)(2,1)}, u32[]{:S(2)}, u32[]{:S(2)}) collective-permute-start(bf16[4096,128]{1,0:T(8,128)(2,1)S(1)} %gain.1.refs_2_), channel_id=1, source_target_pairs={{0,96},{32,0},{64,32},{96,64},{1,97},{33,1},{65,33},{97,65},{2,98}... | collective-permute-start | bytes 3145736 | tf_op jit(solution)/shard_map/ppermute | solution.py:231
  18.7 1.5 collective-permute-start
  21.1 134.0 %copy-start.9 = (s32[1,4]{1,0:T(1,128)S(1)}, s32[1,4]{1,0:T(1,128)}, u32[]{:S(2)}) copy-start(s32[1,4]{1,0:T(1,128)} %param.18) | copy-start | bytes 52
  21.1 134.6 %copy-start.8 = (s32[1,4,128]{2,1,0:T(4,128)S(1)}, s32[1,4,128]{2,1,0:T(4,128)}, u32[]{:S(2)}) copy-start(s32[1,4,128]{2,1,0:T(4,128)} %param.17) | copy-start | bytes 6148
  21.9 20.1 %all-to-all-start = ((bf16[16,64,256]{2,1,0:T(8,128)(2,1)}), bf16[16,64,256]{2,1,0:T(8,128)(2,1)}, u32[]{:S(2)}, u32[]{:S(2)}) async-start(bf16[16,64,256]{2,1,0:T(8,128)(2,1)} %broadcast_in_dim.4), calls=%async_computation | async-start | bytes 1048576 | tf_op jit(solution)/shard_map/all_to_all | solution.py:237
  29.9 33.8 %collective-permute-start.4 = (bf16[4096,128]{1,0:T(8,128)(2,1)S(1)}, bf16[4096,128]{1,0:T(8,128)(2,1)}, u32[]{:S(2)}, u32[]{:S(2)}) collective-permute-start(bf16[4096,128]{1,0:T(8,128)(2,1)S(1)} %gain.1.refs_2_), channel_id=1, source_target_pairs={{0,1},{1,0},{2,3},{3,2},{4,5},{5,4},{6,7},{7,6},{8,9},{9,8},{10,11... | collective-permute-start | bytes 3145736 | tf_op jit(solution)/shard_map/ppermute | solution.py:228
  63.0 2.8 %collective-permute-start.5 = (bf16[4096,128]{1,0:T(8,128)(2,1)S(1)}, bf16[4096,128]{1,0:T(8,128)(2,1)}, u32[]{:S(2)}, u32[]{:S(2)}) collective-permute-start(bf16[4096,128]{1,0:T(8,128)(2,1)S(1)} %get-tuple-element.8.refs_3_), channel_id=1, source_target_pairs={{0,1},{1,0},{2,3},{3,2},{4,5},{5,4},{6,7},{7,6},{8,9},{9,8},{10,11... | collective-permute-start | bytes 3145736 | tf_op jit(solution)/shard_map/ppermute | solution.py:228
  63.0 5.8 %collective-permute-start.6 = (bf16[4096,128]{1,0:T(8,128)(2,1)S(1)}, bf16[4096,128]{1,0:T(8,128)(2,1)}, u32[]{:S(2)}, u32[]{:S(2)}) collective-permute-start(bf16[4096,128]{1,0:T(8,128)(2,1)S(1)} %get-tuple-element.9.refs_4_), channel_id=1, source_target_pairs={{0,1},{1,0},{2,3},{3,2},{4,5},{5,4},{6,7},{7,6},{8,9},{9,8},{10,11... | collective-permute-start | bytes 3145736 | tf_op jit(solution)/shard_map/ppermute | solution.py:228
  63.5 5.5 %collective-permute-start.7 = (bf16[4096,128]{1,0:T(8,128)(2,1)}, bf16[4096,128]{1,0:T(8,128)(2,1)}, u32[]{:S(2)}, u32[]{:S(2)}) collective-permute-start(bf16[4096,128]{1,0:T(8,128)(2,1)} %get-tuple-element.10.refs_5_), channel_id=1, source_target_pairs={{0,1},{1,0},{2,3},{3,2},{4,5},{5,4},{6,7},{7,6},{8,9},{9,8},{10,11... | collective-permute-start | bytes 3145736 | tf_op jit(solution)/shard_map/ppermute | solution.py:228
  72.8 0.8 copy-start.3
  73.6 21.2 %all-to-all-start.1 = ((bf16[16,64,256]{2,1,0:T(8,128)(2,1)}), bf16[16,64,256]{2,1,0:T(8,128)(2,1)}, u32[]{:S(2)}, u32[]{:S(2)}) async-start(bf16[16,64,256]{2,1,0:T(8,128)(2,1)} %copy-done.3), calls=%async_computation.1 | async-start | bytes 1048576 | tf_op jit(solution)/shard_map/all_to_all | solution.py:237
  98.8 0.8 copy-start.2
  99.6 19.9 %all-to-all-start.2 = ((bf16[16,64,256]{2,1,0:T(8,128)(2,1)}), bf16[16,64,256]{2,1,0:T(8,128)(2,1)}, u32[]{:S(2)}, u32[]{:S(2)}) async-start(bf16[16,64,256]{2,1,0:T(8,128)(2,1)} %copy-done.2), calls=%async_computation.2 | async-start | bytes 1048576 | tf_op jit(solution)/shard_map/all_to_all | solution.py:237
  123.4 0.8 copy-start.1
  124.3 21.1 %all-to-all-start.3 = ((bf16[16,64,256]{2,1,0:T(8,128)(2,1)}), bf16[16,64,256]{2,1,0:T(8,128)(2,1)}, u32[]{:S(2)}, u32[]{:S(2)}) async-start(bf16[16,64,256]{2,1,0:T(8,128)(2,1)} %copy-done.1), calls=%async_computation.3 | async-start | bytes 1048576 | tf_op jit(solution)/shard_map/all_to_all | solution.py:237
  129.9 1.7 collective-permute-start.8
  149.4 14.0 %all-to-all-start.4 = ((f32[16,4,1024]{2,1,0:T(4,128)}), f32[16,4,1024]{2,1,0:T(4,128)S(1)}, u32[]{:S(2)}, u32[]{:S(2)}) async-start(f32[16,4,1024]{2,1,0:T(4,128)} %section.7), calls=%async_computation.4 | async-start | bytes 524288 | tf_op jit(solution)/shard_map/all_to_all | solution.py:237
  163.5 0.7 copy-start.7
Sparse Core Ops, SparseCore 0:
  10.4 139.3 all-gather.1

commit v3 on v2

v3 whole, which is shorter than its diff:
```python
import functools
import jax, jax.numpy as jnp
from jax import lax
from jax.sharding import PartitionSpec as P
from jax.experimental import pallas as pl
from jax.experimental.pallas import tpu as pltpu

BF=jnp.bfloat16
F32=jnp.float32

def rms_rows(v, g):
    return v * lax.rsqrt(jnp.mean(v * v, axis=-1, keepdims=True) + 1e-05) * g


HEADS = 16
VMEM_BYTES = 63_000_000


def embedded(prev, embed_ref, pos_ref):
    one_hot = (lax.broadcasted_iota(jnp.int32, (embed_ref.shape[0], prev.shape[1]), 0) == prev).astype(BF)
    rows = lax.dot_general(one_hot, embed_ref[...], (((0,), (0,)), ((), ())), preferred_element_type=F32)
    return rows + pos_ref[...].astype(F32)


def fetched(sources, refs, sems):
    copies = [pltpu.make_async_copy(source, to, sems.at[i]) for i, (source, to) in enumerate(zip(sources, refs))]
    for copy in copies:
        copy.start()
    return copies


def early_kernel(gate_ref, prev_in, embed_in, pos_in, gain_in, pack_ref, q_out, acc_out, top_out, sum_out,
                 prev_ref, embed_ref, pos_ref, gain_ref, n_ref, k_ref, v_ref, wq, sems, small_sems):
    bars, chars = prev_ref.shape
    vocab, width = embed_ref.shape
    small = fetched((prev_in, embed_in, pos_in, gain_in), (prev_ref, embed_ref, pos_ref, gain_ref), small_sems)
    copies = [pltpu.make_async_copy(pack_ref.at[:, j], wq.at[j], sems.at[j]) for j in range(3)]
    for copy in small:
        copy.wait()
    copies[0].start()
    for b in range(bars):
        emb = embedded(prev_ref[b:b + 1, :], embed_ref, pos_ref)
        n_ref[b * chars:(b + 1) * chars] = rms_rows(emb, gain_ref[0:1]).astype(BF)
    for j, dst in ((0, q_out), (1, k_ref), (2, v_ref)):
        copies[j].wait()
        if j < 2:
            copies[j + 1].start()
        dst[...] = jnp.dot(n_ref[...], wq[j].reshape(width, width), preferred_element_type=F32).astype(BF)
    low = lax.broadcasted_iota(jnp.int32, (chars, 128), 1) < 64
    query = lax.broadcasted_iota(jnp.int32, (chars, chars), 0)
    key = lax.broadcasted_iota(jnp.int32, (chars, chars), 1)
    seen = (query >= key) & (key > 0)
    head = lax.broadcasted_iota(jnp.int32, (chars, HEADS), 1)

    def attend(b, carry):
        rows = pl.ds(pl.multiple_of(b * chars, chars), chars)
        tops = jnp.full((chars, HEADS), -1e30, F32)
        sums = jnp.zeros((chars, HEADS), F32)
        for h in range(width // 128):
            cols = slice(h * 128, (h + 1) * 128)
            q, k, v = q_out[rows, cols], k_ref[rows, cols], v_ref[rows, cols]
            zero = jnp.zeros_like(k)
            kk = jnp.concatenate([jnp.where(low, k, zero), jnp.where(low, zero, k)], axis=0)
            vv = jnp.concatenate([jnp.where(low, v, zero), jnp.where(low, zero, v)], axis=0)
            s = lax.dot_general(q, kk, (((1,), (1,)), ((), ())), preferred_element_type=F32)
            probs = []
            for half in range(2):
                t = jnp.where(seen, s[:, half * chars:(half + 1) * chars], -1e30)
                top = jnp.max(t, axis=-1, keepdims=True)
                e = jnp.where(seen, jnp.exp((t - top) * 0.125), 0.0)
                tops = jnp.where(head == 2 * h + half, top, tops)
                sums = jnp.where(head == 2 * h + half, jnp.sum(e, axis=-1, keepdims=True), sums)
                probs.append(e.astype(BF))
            acc_out[rows, cols] = jnp.dot(jnp.concatenate(probs, axis=1), vv, preferred_element_type=F32)
        top_out[rows] = tops
        sum_out[rows] = sums
        return carry

    lax.fori_loop(0, bars, attend, 0)


def early_decode(gate, prev, embed, pos, gain, pack):
    bars, chars = prev.shape
    width = embed.shape[1]
    tokens = bars * chars
    t = lambda d, w=width: jax.ShapeDtypeStruct((tokens, w), d)
    return pl.pallas_call(
        early_kernel,
        out_shape=[t(BF), t(F32), t(F32, HEADS), t(F32, HEADS)],
        in_specs=[pl.BlockSpec(memory_space=pl.ANY)] * 6,
        out_specs=[pl.BlockSpec(memory_space=pltpu.VMEM)] * 4,
        scratch_shapes=[pltpu.VMEM(v.shape, v.dtype) for v in (prev, embed, pos, gain)]
        + [pltpu.VMEM((tokens, width), BF)] * 3
        + [pltpu.VMEM((3, 128, 8, width), BF), pltpu.SemaphoreType.DMA((3,)), pltpu.SemaphoreType.DMA((4,))],
        compiler_params=pltpu.CompilerParams(vmem_limit_bytes=VMEM_BYTES),
        cost_estimate=pl.CostEstimate(flops=8 << 30, bytes_accessed=16 << 20, transcendentals=1 << 20),
        name="early",
    )(gate, prev, embed, pos, gain, pack)


def late_kernel(*refs):
    pack_ref, out_ref, refs, sources = refs[11], refs[12], refs[13:], refs[:11]
    held, (x_ref, n_ref, c_ref, mid_ref, wk, wo, wup, wdn, sems, loads) = refs[:11], refs[11:]
    parts_ref, ids_ref, prev_ref, len_ref, embed_ref, pos_ref, gain_ref, top_in, sum_in, q_ref, acc_ref = held
    bars, chars = ids_ref.shape
    vocab, width = embed_ref.shape
    copies = [pltpu.make_async_copy(pack_ref.at[:, 1 + j], wk.at[j], sems.at[j]) for j in range(2)]
    copies.append(pltpu.make_async_copy(pack_ref.at[:, 3], wo, sems.at[2]))
    for j in range(4):
        copies.append(pltpu.make_async_copy(pack_ref.at[:, 4 + j], wup.at[j], sems.at[3 + j]))
    for j in range(4):
        rows = pl.ds(32 * j, 32)
        copies.append(pltpu.make_async_copy(pack_ref.at[rows, 8:12], wdn.at[rows], sems.at[7 + j]))
    small = [pltpu.make_async_copy(source, to, loads.at[i]) for i, (source, to) in enumerate(zip(sources, held))]
    for copy in small[:7] + copies[:2]:
        copy.start()
    for copy in small[:7]:
        copy.wait()
    for b in range(bars):
        x_ref[b * chars:(b + 1) * chars] = embedded(prev_ref[b:b + 1, :], embed_ref, pos_ref)
    vec = jnp.sum(parts_ref[...], axis=0).astype(BF).astype(F32)
    first = vec + pos_ref[0:1].astype(F32)
    normed = rms_rows(first, gain_ref[0:1]).astype(BF)
    kv = []
    for j in range(2):
        copies[j].wait()
        if j == 0:
            for copy in small[7:]:
                copy.start()
        kv.append(jnp.dot(normed, wk[j].reshape(width, width), preferred_element_type=F32).astype(BF).astype(F32))
    member = (lax.broadcasted_iota(jnp.int32, (HEADS, width), 1) // 64
              == lax.broadcasted_iota(jnp.int32, (HEADS, width), 0))
    expand = member.astype(BF)

    for copy in small[7:]:
        copy.wait()
    copies[2].start()
    copies[3].start()

    def widen(v):
        high = v.astype(BF)
        rest = (v - high.astype(F32)).astype(BF)
        both = jnp.concatenate([high, rest], axis=1)
        return jnp.dot(both, jnp.concatenate([expand, expand], axis=0), preferred_element_type=F32)

    for b in range(bars):
        rows = slice(b * chars, (b + 1) * chars)
        key = jnp.where(member, kv[0][b:b + 1], 0.0).astype(BF)
        score = lax.dot_general(q_ref[rows, :], key, (((1,), (1,)), ((), ())), preferred_element_type=F32)
        start = lax.broadcasted_iota(jnp.int32, (chars, HEADS), 0) == 0
        before = jnp.where(start, -1e30, top_in[rows, :])
        score = jnp.where(start, 0.0, score)
        top = jnp.maximum(before, score)
        old = jnp.exp((before - top) * 0.125)
        new = jnp.exp((score - top) * 0.125)
        inverse = 1.0 / (old * sum_in[rows, :] + new)
        mixed = acc_ref[rows, :] * widen(old * inverse) + kv[1][b:b + 1] * widen(new * inverse)
        c_ref[rows, :] = mixed.astype(BF)
        x_ref[b * chars:b * chars + 1, :] = first[b:b + 1]
    copies[2].wait()
    copies[7].start()
    copies[4].start()
    hidden = x_ref[...] + jnp.dot(c_ref[...], wo[...].reshape(width, width), preferred_element_type=F32)
    x_ref[...] = hidden
    n_ref[...] = rms_rows(hidden, gain_ref[1:2]).astype(BF)
    for j in range(4):
        copies[3 + j].wait()
        if j < 3:
            copies[8 + j].start()
        if j < 2:
            copies[5 + j].start()
        mid_ref[...] = jax.nn.gelu(jnp.dot(n_ref[...], wup[j].reshape(width, width), preferred_element_type=F32)).astype(BF)
        copies[7 + j].wait()
        x_ref[...] += jnp.dot(mid_ref[...], wdn[32 * j:32 * j + 32].reshape(width, width), preferred_element_type=F32)
    last = rms_rows(x_ref[...], gain_ref[2:3]).astype(BF)
    logits = lax.dot_general(embed_ref[...], last, (((1,), (1,)), ((), ())), preferred_element_type=F32)
    top = jnp.max(logits, axis=0, keepdims=True)
    norm = top + jnp.log(jnp.sum(jnp.exp(logits - top), axis=0, keepdims=True))
    for b in range(bars):
        cols = slice(b * chars, (b + 1) * chars)
        hit = lax.broadcasted_iota(jnp.int32, (vocab, chars), 0) == ids_ref[b:b + 1, :]
        picked = jnp.sum(jnp.where(hit, logits[:, cols], 0.0), axis=0, keepdims=True) - norm[:, cols]
        live = lax.broadcasted_iota(jnp.int32, (1, chars), 1) < len_ref[b:b + 1, :]
        out_ref[b:b + 1, :] = jnp.where(live, picked, 0.0)


def late_decode(parts, early, ids, prev, lengths, embed, pos, gain, pack):
    bars, chars = ids.shape
    width = embed.shape[1]
    tokens = bars * chars
    sources = (parts, ids, prev, lengths, embed, pos, gain, early[2], early[3], early[0], early[1])
    t = lambda d: pltpu.VMEM((tokens, width), d)
    return pl.pallas_call(
        late_kernel,
        out_shape=jax.ShapeDtypeStruct((bars, chars), F32),
        in_specs=[pl.BlockSpec(memory_space=pl.ANY)] * 12,
        out_specs=pl.BlockSpec(memory_space=pltpu.VMEM),
        scratch_shapes=[pltpu.VMEM(v.shape, v.dtype) for v in sources] + [t(F32), t(BF), t(BF), t(BF),
                        pltpu.VMEM((2, 128, 8, width), BF), pltpu.VMEM((128, 8, width), BF),
                        pltpu.VMEM((4, 128, 8, width), BF), pltpu.VMEM((128, 4, 8, width), BF),
                        pltpu.SemaphoreType.DMA((11,)), pltpu.SemaphoreType.DMA((11,))],
        compiler_params=pltpu.CompilerParams(vmem_limit_bytes=VMEM_BYTES),
        cost_estimate=pl.CostEstimate(flops=10 << 30, bytes_accessed=24 << 20, transcendentals=4 << 20),
        name="late",
    )(*sources, pack)


def shifted(ids):
    return jnp.concatenate([jnp.full((ids.shape[0], 1), -1, jnp.int32), ids[:, :-1]], axis=1)


GROUP = ("y", "x", "z", "c")


def section_kernel(step, project, x_in, *refs):
    own, other, refs = refs[:8], refs[8:16], refs[16:]
    if project:
        proj_own, proj_other, _, out_ref, x_ref, w_ref, sems, p_ref, p_sems = refs
    else:
        out_ref, x_ref, w_ref, sems, row_ref, out_sems = refs
    blocks, rows, cols = x_ref.shape
    side, depth = cols // 2, blocks * cols
    half = depth // 2
    core = lax.axis_index("c")
    which = lax.rem(lax.axis_index("y") - step + 4, 4)
    chip = lax.axis_index("x") * 4 + lax.axis_index("z")
    load_x = pltpu.make_async_copy(x_in, x_ref, sems.at[4])
    load_x.start()
    for i in range(4):
        @pl.when(which == i)
        def _():
            for part in range(2):
                for sources, at, sem in ((own, core, 0), (other, 1 - core, 1)):
                    lanes = pl.ds(pl.multiple_of(at * side, side), side)
                    pltpu.make_async_copy(
                        sources[2 * i + part], w_ref.at[pl.ds(part * half, half), lanes], sems.at[2 * part + sem]
                    ).start()
    if project:
        deep = proj_own.shape[0]
        loads = [
            pltpu.make_async_copy(source, p_ref.at[pl.ds(pl.multiple_of(at * deep, deep), deep)], p_sems.at[i])
            for i, (source, at) in enumerate(((proj_own, core), (proj_other, 1 - core)))
        ]
        for load in loads:
            load.start()
    load_x.wait()
    total = jnp.zeros((rows, cols), F32)
    for j in range(blocks):
        v = x_ref[j].astype(F32)
        total += v * v
    scale = lax.rsqrt(jnp.sum(total, axis=-1, keepdims=True) / depth + 1e-05)
    update = jnp.zeros((rows, cols), F32)
    for part in range(2):
        span = pl.ds(part * half, half)
        for sem in range(2):
            at = w_ref.at[span, pl.ds(sem * side, side)]
            pltpu.make_async_copy(own[0], at, sems.at[2 * part + sem]).wait()
        wide = jnp.concatenate([x_ref[part * blocks // 2 + j] for j in range(blocks // 2)], axis=1)
        update += jnp.dot(wide, w_ref[span, :], preferred_element_type=F32)
    leaving = (x_ref[chip].astype(F32) + jax.nn.gelu(update * scale)).astype(BF)
    if project:
        for load in loads:
            load.wait()
        partial = jnp.dot(leaving, p_ref[...], preferred_element_type=F32)
        each = rows // blocks
        for j in range(blocks):
            out_ref[j] = partial[j * each:(j + 1) * each]
    else:
        row_ref[...] = leaving
        sends = [pltpu.make_async_copy(row_ref, out_ref.at[j], out_sems.at[j]) for j in range(blocks)]
        for send in sends:
            send.start()
        for send in sends:
            send.wait()


def section_step(step, x, own, other, proj=()):
    blocks, rows, cols = x.shape
    vm = pl.BlockSpec(memory_space=pltpu.VMEM)
    hbm = pl.BlockSpec(memory_space=pl.ANY)
    scratch = [pltpu.VMEM(x.shape, BF), pltpu.VMEM((blocks * cols, cols), BF), pltpu.SemaphoreType.DMA((5,))]
    if not proj:
        out = jax.ShapeDtypeStruct(x.shape, BF)
        scratch += [pltpu.VMEM((rows, cols), BF), pltpu.SemaphoreType.DMA((blocks,))]
    else:
        width = proj[0].shape[1]
        out = jax.ShapeDtypeStruct((blocks, rows // blocks, width), F32)
        scratch += [pltpu.VMEM((cols, width), BF), pltpu.SemaphoreType.DMA((2,))]
    return pl.pallas_call(
        lambda *refs: section_kernel(step, len(proj) > 0, *refs),
        out_shape=out,
        in_specs=[hbm] * (17 + len(proj)),
        out_specs=vm if proj else hbm,
        scratch_shapes=scratch,
        compiler_params=pltpu.CompilerParams(vmem_limit_bytes=VMEM_BYTES),
        cost_estimate=pl.CostEstimate(flops=1, bytes_accessed=1, transcendentals=0),
        name="section",
    )(x, *own, *other, *proj)


def prepare_kernel(*refs):
    sources, outs, scratch = refs[:6], refs[6:9], refs[9:]
    held, (pack_ref, sems, out_sem) = scratch[:6], scratch[6:]
    loads = [pltpu.make_async_copy(source, to, sems.at[i]) for i, (source, to) in enumerate(zip(sources, held))]
    for load in loads:
        load.start()
    a_ref, o_ref, u_ref, d_ref, w_ref, gain_ref = held
    width = o_ref.shape[1]
    for load in loads[:4]:
        load.wait()
    for i in range(3):
        pack_ref[i] = a_ref[:, i * width:(i + 1) * width]
    pack_ref[3] = o_ref[...]
    for i in range(4):
        pack_ref[4 + i] = u_ref[:, i * width:(i + 1) * width]
        pack_ref[8 + i] = d_ref[8 * i:8 * i + 8]
    store = pltpu.make_async_copy(pack_ref, outs[0], out_sem)
    store.start()
    loads[4].wait()
    loads[5].wait()
    rows = outs[1].shape[0]
    for i in range(gain_ref.shape[0]):
        span = slice(i * 128, (i + 1) * 128)
        column = jnp.transpose(jnp.broadcast_to(gain_ref[i:i + 1, :], (128, 128)))
        first = i * 128 % rows
        outs[1 + i * 128 // rows][first:first + 128] = (w_ref[span, :].astype(F32) * column).astype(BF)
    store.wait()


def prepare(*sources):
    depth, cols = sources[4].shape
    width = sources[1].shape[1]
    hbm = pl.BlockSpec(memory_space=pl.ANY)
    vm = pl.BlockSpec(memory_space=pltpu.VMEM)
    half = jax.ShapeDtypeStruct((depth // 2, cols), BF)
    return pl.pallas_call(
        prepare_kernel,
        out_shape=[jax.ShapeDtypeStruct((12, 8, width), BF), half, half],
        in_specs=[hbm] * 6,
        out_specs=[hbm, vm, vm],
        scratch_shapes=[pltpu.VMEM(v.shape, v.dtype) for v in sources]
        + [pltpu.VMEM((12, 8, width), BF), pltpu.SemaphoreType.DMA((6,)), pltpu.SemaphoreType.DMA],
        compiler_params=pltpu.CompilerParams(vmem_limit_bytes=VMEM_BYTES),
        name="prepare",
    )(*sources)


def after_kernel(*refs):
    pass


def after(first, arrays):
    hbm = pl.BlockSpec(memory_space=pl.ANY)
    return pl.pallas_call(
        after_kernel,
        out_shape=[jax.ShapeDtypeStruct(v.shape, v.dtype) for v in arrays],
        in_specs=[hbm] * (len(first) + len(arrays)),
        out_specs=[hbm] * len(arrays),
        input_output_aliases={i + len(first): i for i in range(len(arrays))},
        compiler_params=pltpu.CompilerParams(vmem_limit_bytes=1 << 20),
        cost_estimate=pl.CostEstimate(flops=1, bytes_accessed=1, transcendentals=0),
        name="after",
    )(*first, *arrays)


def body(bar_in, section_weight, section_gain, projection, char_ids, lengths, char_embed, char_pos,
         attn_in, attn_out, ffn_in, ffn_out, norm_gain):
    y, core = lax.axis_index("y"), lax.axis_index("c")
    width = char_embed.shape[1]

    def swap(v):
        return lax.ppermute(v, "c", [(0, 1), (1, 0)])

    def turn(v, by):
        return lax.ppermute(v, "y", [(i, (i + by) % 4) for i in range(4)])

    def ordered(mine, theirs, axis):
        return jnp.where(core == 0, jnp.concatenate([mine, theirs], axis), jnp.concatenate([theirs, mine], axis))

    feats = bar_in.shape[2]
    pack, low, high = prepare(
        attn_in, attn_out, ffn_in, ffn_out, section_weight[0], section_gain.reshape(-1, 128))
    pack = lax.all_gather(pack.reshape(96, width), GROUP, axis=0, tiled=True).reshape(128, 12, 8, width)

    by_core = lax.dynamic_index_in_dim(bar_in, y, 0, keepdims=False).reshape(16, 2, 4, feats)
    by_core = by_core.transpose(1, 0, 2, 3).reshape(2, 64, feats)
    mine = lax.dynamic_index_in_dim(by_core, core, 0, keepdims=False)
    theirs = swap(lax.dynamic_index_in_dim(by_core, 1 - core, 0, keepdims=False))
    block = ordered(mine, theirs, 1)

    def spread(v):
        return lax.all_to_all(v, ("x", "z"), 0, 0, tiled=True)

    x = spread(jnp.broadcast_to(block[None], (16,) + block.shape))
    below_low, above_high, below_high, above_low = after(
        [x], [turn(low, 1), turn(high, 3), turn(high, 1), turn(low, 3)])
    own = [low, high, below_low, below_high, turn(below_low, 1), turn(above_high, 3), above_low, above_high]
    other = [swap(w) for w in own]
    proj = [projection, swap(projection)]
    for step in range(4):
        if step:
            x = spread(out)
        out = section_step(step, x, own, other, [*proj, early[2]] if step == 3 else ())
        if step == 2:
            ids, prev = char_ids[0], shifted(char_ids[0])
            early = early_decode(out, prev, char_embed, char_pos, norm_gain, pack)
    parts = spread(out)
    return late_decode(parts, early, ids, prev, lengths[0][:, None], char_embed, char_pos, norm_gain, pack)[None]


def solution(mesh):
    fine = jax.sharding.Mesh(mesh.devices.reshape(4, 4, 4, 2), GROUP)
    bar = ("x", "z", "c")
    in_specs = (
        P(None, None, bar),
        P("y", None, bar),
        P("y", None),
        P(bar, None),
        P("y", bar, None),
        P("y", bar),
        P(),
        P(),
        P(GROUP, None),
        P(GROUP, None),
        P(GROUP, None),
        P(GROUP, None),
        P(),
    )
    return jax.shard_map(body, mesh=fine, in_specs=in_specs, out_specs=P("y", bar, None), check_vma=False)
```

time: 197 us -> 193 us (0.980)
  waiting for transfers between devices: 90.8 us -> 61.9 us
  blocking collectives: 0 us -> 24.2 us
  Pallas kernels: 43.3 us -> 48.7 us
  local copies, waits for them, and re-layouts: 9.27 us -> 5.42 us
    all_to_all x5 -> x4, waiting for transfers between devices: 61.4 us -> 22.7 us  [spread(): return lax.all_to_all(v, ('x', 'z'), 0, 0, tiled=True)]
    all_to_all x0 -> x1, blocking collectives: none -> 24.2 us  [spread(): return lax.all_to_all(v, ('x', 'z'), 0, 0, tiled=True)]
    ppermute x3 -> x6, waiting for transfers between devices: 21 us -> 36.4 us  [turn(): return lax.ppermute(v, 'y', [(i, (i + by) % 4) for i in range(4)])]
    ppermute x6 -> x10, waiting for transfers between devices: 8.43 us -> 2.78 us  [swap(): return lax.ppermute(v, 'c', [(0, 1), (1, 0)])]
    pallas_call x7, Pallas kernels: 43.3 us -> 48.7 us  [the longest x1 20.4 us: late_decode(): pl.pallas_call(late_kernel, out_shape=jax.ShapeDtypeStruct((bars, chars),...]
    all_to_all x5 -> x4, starting transfers between devices: 31.6 us -> 26.7 us  [spread(): return lax.all_to_all(v, ('x', 'z'), 0, 0, tiled=True)]
    ppermute x3 -> x6, starting transfers between devices: 5.98 us -> 9.73 us  [turn(): return lax.ppermute(v, 'y', [(i, (i + by) % 4) for i in range(4)])]
    unnamed x20 -> x42, local copies, waits for them, and re-layouts: 5.12 us -> 3.22 us
  transfers between devices with their start and end apart: 15 -> 21, of which waited for: 11 -> 6; matrix products, arithmetic and copies ran while one was open for 3% -> 1% of each run, Pallas kernels for 8% -> 11%
where the time goes in v3:
time: 193 us; the launch traced here: 192 us
  waiting for transfers between devices  61.9 us (32%)
  Pallas kernels  48.7 us (25%)
  starting transfers between devices  37.9 us (20%)
  blocking collectives  24.2 us (13%)
  between operations  13.8 us (7%)
  local copies, waits for them, and re-layouts  5.42 us (3%)
    ppermute x6, waiting for transfers between devices, turn(): return lax.ppermute(v, 'y', [(i, (i + by) % 4) for i in range(4)])  36.4 us
    all_to_all x4, starting transfers between devices, spread(): return lax.all_to_all(v, ('x', 'z'), 0, 0, tiled=True)  26.7 us
    all_to_all x1, blocking collectives, spread(): return lax.all_to_all(v, ('x', 'z'), 0, 0, tiled=True)  24.2 us
    all_to_all x4, waiting for transfers between devices, spread(): return lax.all_to_all(v, ('x', 'z'), 0, 0, tiled=True)  22.7 us
    pallas_call x1, Pallas kernels, late_decode(): pl.pallas_call(late_kernel, out_shape=jax.ShapeDtypeStruct((bars, chars),...  20.4 us
    pallas_call x4, Pallas kernels, section_step(): pl.pallas_call(lambda *refs: section_kernel(step, len(proj) > 0, *refs),...  12.8 us
    pallas_call x1, Pallas kernels, early_decode(): pl.pallas_call(early_kernel, out_shape=[t(BF), t(F32), t(F32, HEADS), t(F...  12.5 us
    ppermute x6, starting transfers between devices, turn(): return lax.ppermute(v, 'y', [(i, (i + by) % 4) for i in range(4)])  9.73 us
  transfers between devices with their start and end apart: 21, of which 6 were waited for; matrix products, arithmetic and copies ran while one was open for 1% of the time, Pallas kernels for 11%

profile of v3, /device:TPU:0, one launch (start us, length us, event | category | flops | bytes accessed | tf_op | source)
XLA Modules:
  0.0 192.0 jit_solution(2739990457241114401)
XLA Ops:
  6.5 3.1 %prepare.1 = (bf16[12,8,1024]{2,1,0:T(8,128)(2,1)}, bf16[2048,128]{1,0:T(8,128)(2,1)}, bf16[2048,128]{1,0:T(8,128)(2,1)}) custom-call(bf16[8,3072]{1,0:T(8,128)(2,1)} %refs_0_.1, bf16[8,1024]{1,0:T(8,128)(2,1)} %refs_1_.1, bf16[8,4096]{1,0:T(8,128)(2,1)} %refs_2_.1, bf16[32,1024]{1,0:T(8,128)(2,1)} %refs_3_.1, bf16[4096,128]{1,0:T(8,128)(2,1)} %bitcast.16, ...), custom_call_target="tpu_custom_call" | custom-call | tf_op jit(solution)/shard_map/prepare/pallas_call | solution.py:336
  9.7 0.0 all-gather.2.cloned.1.call-update
  9.8 0.1 collective-permute-start
  9.8 3.2 %collective-permute-start.2 = (bf16[2048,128]{1,0:T(8,128)(2,1)}, bf16[2048,128]{1,0:T(8,128)(2,1)S(1)}, u32[]{:S(2)}, u32[]{:S(2)}) collective-permute-start(bf16[2048,128]{1,0:T(8,128)(2,1)} %get-tuple-element.17.refs_2_), channel_id=1, source_target_pairs={{0,96},{32,0},{64,32},{96,64},{1,97},{33,1},{65,33},{97,65},{2,98}... | collective-permute-start | bytes 1572872 | tf_op jit(solution)/shard_map/ppermute | solution.py:375
  13.0 0.0 collective-permute-start.3
  13.0 0.6 collective-permute-start.1
  13.6 2.7 %collective-permute-start.4 = (bf16[2048,128]{1,0:T(8,128)(2,1)}, bf16[2048,128]{1,0:T(8,128)(2,1)S(1)}, u32[]{:S(2)}, u32[]{:S(2)}) collective-permute-start(bf16[2048,128]{1,0:T(8,128)(2,1)} %get-tuple-element.16.refs_1_), channel_id=1, source_target_pairs={{0,96},{32,0},{64,32},{96,64},{1,97},{33,1},{65,33},{97,65},{2,98}... | collective-permute-start | bytes 1572872 | tf_op jit(solution)/shard_map/ppermute | solution.py:375
  16.3 0.0 collective-permute-done
  16.3 0.9 broadcast_in_dim.4
  17.2 7.9 %all-to-all-start = ((bf16[16,64,256]{2,1,0:T(8,128)(2,1)}), bf16[16,64,256]{2,1,0:T(8,128)(2,1)S(1)}, u32[]{:S(2)}, u32[]{:S(2)}) async-start(bf16[16,64,256]{2,1,0:T(8,128)(2,1)} %broadcast_in_dim.4), calls=%async_computation | async-start | bytes 1048576 | tf_op jit(solution)/shard_map/all_to_all | solution.py:392
  25.1 0.1 collective-permute-start.7
  25.1 16.6 %collective-permute-done.1.refs_1_ = bf16[2048,128]{1,0:T(8,128)(2,1)S(1)} collective-permute-done((bf16[2048,128]{1,0:T(8,128)(2,1)}, bf16[2048,128]{1,0:T(8,128)(2,1)S(1)}, u32[]{:S(2)}, u32[]{:S(2)}) %collective-permute-start.1) | collective-permute-done | bytes 524320 | tf_op jit(solution)/shard_map/ppermute | solution.py:375
  41.8 0.0 collective-permute-start.8
  41.8 0.0 all-to-all-done.refs_0_
  41.8 0.0 collective-permute-done.2.refs_2_
  41.9 0.1 collective-permute-start.5
  41.9 3.2 %collective-permute-start.6 = (bf16[2048,128]{1,0:T(8,128)(2,1)S(1)}, bf16[2048,128]{1,0:T(8,128)(2,1)S(1)}, u32[]{:S(2)}, u32[]{:S(2)}) collective-permute-start(bf16[2048,128]{1,0:T(8,128)(2,1)S(1)} %get-tuple-element.20.refs_8_), channel_id=1, source_target_pairs={{0,96},{32,0},{64,32},{96,64},{1,97},{33,1},{65,33},{97,65},{2,98}... | collective-permute-start | bytes 1572872 | tf_op jit(solution)/shard_map/ppermute | solution.py:375
  45.2 0.0 collective-permute-start.10
  45.2 0.5 collective-permute-start.14
  45.7 0.1 collective-permute-start.9
  45.8 19.8 %collective-permute-done.5.refs_5_ = bf16[2048,128]{1,0:T(8,128)(2,1)S(1)} collective-permute-done((bf16[2048,128]{1,0:T(8,128)(2,1)S(1)}, bf16[2048,128]{1,0:T(8,128)(2,1)S(1)}, u32[]{:S(2)}, u32[]{:S(2)}) %collective-permute-start.5) | collective-permute-done | bytes 524320 | tf_op jit(solution)/shard_map/ppermute | solution.py:375
  65.6 0.5 collective-permute-start.11
  66.1 0.1 collective-permute-start.12
  66.2 1.3 collective-permute-done.13.refs_15_
  67.5 1.5 collective-permute-done.11.refs_13_
  69.0 0.8 copy-done.13
  69.8 0.0 collective-permute-done.12.refs_14_
  69.9 3.2 %section.4 = bf16[16,64,256]{2,1,0:T(8,128)(2,1)} custom-call(bf16[16,64,256]{2,1,0:T(8,128)(2,1)} %copy-done.5, bf16[2048,128]{1,0:T(8,128)(2,1)} %get-tuple-element.16.refs_1_, bf16[2048,128]{1,0:T(8,128)(2,1)} %get-tuple-element.17.refs_2_, bf16[2048,128]{1,0:T(8,128)(2,1)} %copy-done.3, bf16[2048,128]{1,0:T(8,128)(2,1)} %copy-done.2, ...), custom_call_target="tpu_custom_call" | custom-call | flops 1 | bytes 1 | tf_op jit(solution)/shard_map/section/pallas_call | solution.py:289
  73.0 24.2 %all_to_all.25.refs_0_ = bf16[16,64,256]{2,1,0:T(8,128)(2,1)} all-to-all(bf16[16,64,256]{2,1,0:T(8,128)(2,1)} %section.4), channel_id=1, replica_groups=mesh['y'=4,'x'=4,'z'=4,'c'=2] {'x','z'}, dimensions={0} | all-to-all | bytes 1048576 | tf_op jit(solution)/shard_map/all_to_all | solution.py:392
  97.2 3.2 %section.5 = bf16[16,64,256]{2,1,0:T(8,128)(2,1)} custom-call(bf16[16,64,256]{2,1,0:T(8,128)(2,1)} %all_to_all.25.refs_0_, bf16[2048,128]{1,0:T(8,128)(2,1)} %get-tuple-element.16.refs_1_, bf16[2048,128]{1,0:T(8,128)(2,1)} %get-tuple-element.17.refs_2_, bf16[2048,128]{1,0:T(8,128)(2,1)} %copy-done.3, bf16[2048,128]{1,0:T(8,128)(2,1)} %copy-done.2, ...), custom_call_target="tpu_custom_call" | custom-call | flops 1 | bytes 1 | tf_op jit(solution)/shard_map/section/pallas_call | solution.py:289
  100.4 5.8 %all-to-all-start.2 = ((bf16[16,64,256]{2,1,0:T(8,128)(2,1)}), bf16[16,64,256]{2,1,0:T(8,128)(2,1)S(1)}, u32[]{:S(2)}, u32[]{:S(2)}) async-start(bf16[16,64,256]{2,1,0:T(8,128)(2,1)} %section.5), calls=%async_computation.2 | async-start | bytes 1048576 | tf_op jit(solution)/shard_map/all_to_all | solution.py:392
  106.2 0.1 collective-permute-start.15
  106.3 0.7 concatenate.22.prev_in.refs_2_
  107.0 14.8 %all-to-all-done.2.refs_0_ = bf16[16,64,256]{2,1,0:T(8,128)(2,1)S(1)} async-done(((bf16[16,64,256]{2,1,0:T(8,128)(2,1)}), bf16[16,64,256]{2,1,0:T(8,128)(2,1)S(1)}, u32[]{:S(2)}, u32[]{:S(2)}) %all-to-all-start.2) | async-done | bytes 524320 | tf_op jit(solution)/shard_map/all_to_all | solution.py:392
  121.8 0.8 copy-done.15
  122.6 3.2 %section.6.gate_ref = bf16[16,64,256]{2,1,0:T(8,128)(2,1)} custom-call(bf16[16,64,256]{2,1,0:T(8,128)(2,1)} %copy-done.15, bf16[2048,128]{1,0:T(8,128)(2,1)} %get-tuple-element.16.refs_1_, bf16[2048,128]{1,0:T(8,128)(2,1)} %get-tuple-element.17.refs_2_, bf16[2048,128]{1,0:T(8,128)(2,1)} %copy-done.3, bf16[2048,128]{1,0:T(8,128)(2,1)} %copy-done.2, ...), custom_call_target="tpu_custom_call" | custom-call | flops 1 | bytes 1 | tf_op jit(solution)/shard_map/section/pallas_call | solution.py:289
  125.8 5.8 %all-to-all-start.3 = ((bf16[16,64,256]{2,1,0:T(8,128)(2,1)}), bf16[16,64,256]{2,1,0:T(8,128)(2,1)S(1)}, u32[]{:S(2)}, u32[]{:S(2)}) async-start(bf16[16,64,256]{2,1,0:T(8,128)(2,1)} %section.6.gate_ref), calls=%async_computation.3 | async-start | bytes 1048576 | tf_op jit(solution)/shard_map/all_to_all | solution.py:392
  131.6 0.0 all-gather.2.cloned.1.call-done
  131.6 12.5 %early.1 = (bf16[512,1024]{1,0:T(8,128)(2,1)}, f32[512,1024]{1,0:T(8,128)}, f32[512,16]{1,0:T(8,128)}, f32[512,16]{1,0:T(8,128)}) custom-call(bf16[16,64,256]{2,1,0:T(8,128)(2,1)} %section.6.gate_ref, s32[4,128]{1,0:T(4,128)} %concatenate.22.prev_in.refs_2_, bf16[128,1024]{1,0:T(8,128)(2,1)} %refs_4_.1, bf16[128,1024]{1,0:T(8,128)(2,1)} %refs_5_.1, ...), custom_call_target="tpu_custom_call" | custom-call | flops 8589934592 | bytes 16777216 | tf_op jit(solution)/shard_map/early/pallas_call | solution.py:87
  144.1 0.0 collective-permute-done.15.refs_18_
  144.2 0.7 copy-done.17
  144.9 0.2 copy-done.14
  145.0 3.3 %section.7 = f32[16,4,1024]{2,1,0:T(4,128)} custom-call(bf16[16,64,256]{2,1,0:T(8,128)(2,1)} %copy-done.14, bf16[2048,128]{1,0:T(8,128)(2,1)} %get-tuple-element.16.refs_1_, bf16[2048,128]{1,0:T(8,128)(2,1)} %get-tuple-element.17.refs_2_, bf16[2048,128]{1,0:T(8,128)(2,1)} %copy-done.3, bf16[2048,128]{1,0:T(8,128)(2,1)} %copy-done.2, ...), custom_call_target="tpu_custom_call" | custom-call | flops 1 | bytes 1 | tf_op jit(solution)/shard_map/section/pallas_call | solution.py:289
  148.3 7.2 %all-to-all-start.4 = ((f32[16,4,1024]{2,1,0:T(4,128)}), f32[16,4,1024]{2,1,0:T(4,128)S(1)}, u32[]{:S(2)}, u32[]{:S(2)}) async-start(f32[16,4,1024]{2,1,0:T(4,128)} %section.7), calls=%async_computation.4 | async-start | bytes 524288 | tf_op jit(solution)/shard_map/all_to_all | solution.py:392
  155.6 0.6 copy.21.refs_3_
  156.2 7.8 %all-to-all-done.4.refs_0_ = f32[16,4,1024]{2,1,0:T(4,128)S(1)} async-done(((f32[16,4,1024]{2,1,0:T(4,128)}), f32[16,4,1024]{2,1,0:T(4,128)S(1)}, u32[]{:S(2)}, u32[]{:S(2)}) %all-to-all-start.4) | async-done | bytes 262176 | tf_op jit(solution)/shard_map/all_to_all | solution.py:392
  164.0 0.7 copy-done.18
  164.7 20.4 %late.1 = f32[4,128]{1,0:T(4,128)} custom-call(f32[16,4,1024]{2,1,0:T(4,128)} %copy-done.18, s32[4,128]{1,0:T(4,128)} %bitcast.21, s32[4,128]{1,0:T(4,128)} %concatenate.22.prev_in.refs_2_, s32[4,1]{1,0:T(4,128)} %copy.21.refs_3_, bf16[128,1024]{1,0:T(8,128)(2,1)} %refs_4_.1, bf16[128,1024]{1,0:T(8,128)(2,1)} %refs_5_.1, f32[3,1024]{1,0:T(4,128)} %refs_6_.1, ...), custom_call_target="tpu_custom_call" | custom-call | flops 10737418240 | bytes 25165824 | tf_op jit(solution)/shard_map/late/pallas_call | solution.py:193
  (53 shorter events, 0.1 us)
Async XLA Ops:
  6.5 3.1 %copy-start = (bf16[4,128,128]{2,1,0:T(8,128)(2,1)S(1)}, bf16[4,128,128]{2,1,0:T(8,128)(2,1)}, u32[]{:S(2)}) copy-start(bf16[4,128,128]{2,1,0:T(8,128)(2,1)} %param.13) | copy-start | bytes 393220
  6.5 99.7 %copy-start.16 = (bf16[128,1024]{1,0:T(8,128)(2,1)S(1)}, bf16[128,1024]{1,0:T(8,128)(2,1)}, u32[]{:S(2)}) copy-start(bf16[128,1024]{1,0:T(8,128)(2,1)} %refs_17_.1) | copy-start | bytes 786436
  6.5 99.8 %copy-start.19 = (s32[1,4,128]{2,1,0:T(4,128)S(1)}, s32[1,4,128]{2,1,0:T(4,128)}, u32[]{:S(2)}) copy-start(s32[1,4,128]{2,1,0:T(4,128)} %param.17) | copy-start | bytes 6148
  6.5 125.1 %all-gather.2.cloned.1.call-start = ((), (), s32[]{:S(2)}) async-start(), calls=%async_computation.5 | async-start | bytes 25362432 | tf_op jit(solution)/shard_map/all_gather | solution.py:383
  9.8 6.5 %collective-permute-start = (bf16[64,128]{1,0:T(8,128)(2,1)S(1)}, bf16[64,128]{1,0:T(8,128)(2,1)S(1)}, u32[]{:S(2)}, u32[]{:S(2)}) collective-permute-start(bf16[64,128]{1,0:T(8,128)(2,1)S(1)} %get-tuple-element.28), channel_id=1, source_target_pairs={{0,1},{1,0},{2,3},{3,2},{4,5},{5,4},{6,7},{7,6},{8,9},{9,8},{10,11... | collective-permute-start | bytes 49160 | tf_op jit(solution)/shard_map/ppermute | solution.py:372
  9.8 31.9 %collective-permute-start.2 = (bf16[2048,128]{1,0:T(8,128)(2,1)}, bf16[2048,128]{1,0:T(8,128)(2,1)S(1)}, u32[]{:S(2)}, u32[]{:S(2)}) collective-permute-start(bf16[2048,128]{1,0:T(8,128)(2,1)} %get-tuple-element.17.refs_2_), channel_id=1, source_target_pairs={{0,96},{32,0},{64,32},{96,64},{1,97},{33,1},{65,33},{97,65},{2,98}... | collective-permute-start | bytes 1572872 | tf_op jit(solution)/shard_map/ppermute | solution.py:375
  13.0 28.8 %collective-permute-start.3 = (bf16[2048,128]{1,0:T(8,128)(2,1)}, bf16[2048,128]{1,0:T(8,128)(2,1)S(1)}, u32[]{:S(2)}, u32[]{:S(2)}) collective-permute-start(bf16[2048,128]{1,0:T(8,128)(2,1)} %get-tuple-element.17.refs_2_), channel_id=1, source_target_pairs={{0,32},{32,64},{64,96},{96,0},{1,33},{33,65},{65,97},{97,1},{2,34}... | collective-permute-start | bytes 1572872 | tf_op jit(solution)/shard_map/ppermute | solution.py:375
  13.0 28.8 %collective-permute-start.1 = (bf16[2048,128]{1,0:T(8,128)(2,1)}, bf16[2048,128]{1,0:T(8,128)(2,1)S(1)}, u32[]{:S(2)}, u32[]{:S(2)}) collective-permute-start(bf16[2048,128]{1,0:T(8,128)(2,1)} %get-tuple-element.16.refs_1_), channel_id=1, source_target_pairs={{0,32},{32,64},{64,96},{96,0},{1,33},{33,65},{65,97},{97,1},{2,34}... | collective-permute-start | bytes 1572872 | tf_op jit(solution)/shard_map/ppermute | solution.py:375
  13.6 28.2 %collective-permute-start.4 = (bf16[2048,128]{1,0:T(8,128)(2,1)}, bf16[2048,128]{1,0:T(8,128)(2,1)S(1)}, u32[]{:S(2)}, u32[]{:S(2)}) collective-permute-start(bf16[2048,128]{1,0:T(8,128)(2,1)} %get-tuple-element.16.refs_1_), channel_id=1, source_target_pairs={{0,96},{32,0},{64,32},{96,64},{1,97},{33,1},{65,33},{97,65},{2,98}... | collective-permute-start | bytes 1572872 | tf_op jit(solution)/shard_map/ppermute | solution.py:375
  17.2 24.6 %all-to-all-start = ((bf16[16,64,256]{2,1,0:T(8,128)(2,1)}), bf16[16,64,256]{2,1,0:T(8,128)(2,1)S(1)}, u32[]{:S(2)}, u32[]{:S(2)}) async-start(bf16[16,64,256]{2,1,0:T(8,128)(2,1)} %broadcast_in_dim.4), calls=%async_computation | async-start | bytes 1048576 | tf_op jit(solution)/shard_map/all_to_all | solution.py:392
  25.1 20.1 %collective-permute-start.7 = (bf16[2048,128]{1,0:T(8,128)(2,1)}, bf16[2048,128]{1,0:T(8,128)(2,1)S(1)}, u32[]{:S(2)}, u32[]{:S(2)}) collective-permute-start(bf16[2048,128]{1,0:T(8,128)(2,1)} %get-tuple-element.16.refs_1_), channel_id=1, source_target_pairs={{0,1},{1,0},{2,3},{3,2},{4,5},{5,4},{6,7},{7,6},{8,9},{9,8},{10,11... | collective-permute-start | bytes 1572872 | tf_op jit(solution)/shard_map/ppermute | solution.py:372
  41.8 3.9 %collective-permute-start.8 = (bf16[2048,128]{1,0:T(8,128)(2,1)}, bf16[2048,128]{1,0:T(8,128)(2,1)}, u32[]{:S(2)}, u32[]{:S(2)}) collective-permute-start(bf16[2048,128]{1,0:T(8,128)(2,1)} %get-tuple-element.17.refs_2_), channel_id=1, source_target_pairs={{0,1},{1,0},{2,3},{3,2},{4,5},{5,4},{6,7},{7,6},{8,9},{9,8},{10,11... | collective-permute-start | bytes 1572872 | tf_op jit(solution)/shard_map/ppermute | solution.py:372
  41.8 28.0 %copy-start.5 = (bf16[16,64,256]{2,1,0:T(8,128)(2,1)}, bf16[16,64,256]{2,1,0:T(8,128)(2,1)S(1)}, u32[]{:S(2)}) copy-start(bf16[16,64,256]{2,1,0:T(8,128)(2,1)S(1)} %all-to-all-done.refs_0_) | copy-start | bytes 1572868
  41.8 28.0 %copy-start.1 = (bf16[2048,128]{1,0:T(8,128)(2,1)}, bf16[2048,128]{1,0:T(8,128)(2,1)S(1)}, u32[]{:S(2)}) copy-start(bf16[2048,128]{1,0:T(8,128)(2,1)S(1)} %get-tuple-element.20.refs_8_) | copy-start | bytes 1572868
  41.8 28.0 %copy-start.2 = (bf16[2048,128]{1,0:T(8,128)(2,1)}, bf16[2048,128]{1,0:T(8,128)(2,1)S(1)}, u32[]{:S(2)}) copy-start(bf16[2048,128]{1,0:T(8,128)(2,1)S(1)} %get-tuple-element.19.refs_4_) | copy-start | bytes 1572868
  41.8 28.0 %copy-start.3 = (bf16[2048,128]{1,0:T(8,128)(2,1)}, bf16[2048,128]{1,0:T(8,128)(2,1)S(1)}, u32[]{:S(2)}) copy-start(bf16[2048,128]{1,0:T(8,128)(2,1)S(1)} %get-tuple-element.18.refs_3_) | copy-start | bytes 1572868
  41.8 28.0 %copy-start.4 = (bf16[2048,128]{1,0:T(8,128)(2,1)}, bf16[2048,128]{1,0:T(8,128)(2,1)S(1)}, u32[]{:S(2)}) copy-start(bf16[2048,128]{1,0:T(8,128)(2,1)S(1)} %get-tuple-element.21.refs_7_) | copy-start | bytes 1572868
  41.9 23.7 %collective-permute-start.5 = (bf16[2048,128]{1,0:T(8,128)(2,1)S(1)}, bf16[2048,128]{1,0:T(8,128)(2,1)S(1)}, u32[]{:S(2)}, u32[]{:S(2)}) collective-permute-start(bf16[2048,128]{1,0:T(8,128)(2,1)S(1)} %get-tuple-element.18.refs_3_), channel_id=1, source_target_pairs={{0,32},{32,64},{64,96},{96,0},{1,33},{33,65},{65,97},{97,1},{2,34}... | collective-permute-start | bytes 1572872 | tf_op jit(solution)/shard_map/ppermute | solution.py:375
  41.9 23.6 %collective-permute-start.6 = (bf16[2048,128]{1,0:T(8,128)(2,1)S(1)}, bf16[2048,128]{1,0:T(8,128)(2,1)S(1)}, u32[]{:S(2)}, u32[]{:S(2)}) collective-permute-start(bf16[2048,128]{1,0:T(8,128)(2,1)S(1)} %get-tuple-element.20.refs_8_), channel_id=1, source_target_pairs={{0,96},{32,0},{64,32},{96,64},{1,97},{33,1},{65,33},{97,65},{2,98}... | collective-permute-start | bytes 1572872 | tf_op jit(solution)/shard_map/ppermute | solution.py:375
  45.2 20.9 %collective-permute-start.10 = (bf16[2048,128]{1,0:T(8,128)(2,1)S(1)}, bf16[2048,128]{1,0:T(8,128)(2,1)S(1)}, u32[]{:S(2)}, u32[]{:S(2)}) collective-permute-start(bf16[2048,128]{1,0:T(8,128)(2,1)S(1)} %get-tuple-element.19.refs_4_), channel_id=1, source_target_pairs={{0,1},{1,0},{2,3},{3,2},{4,5},{5,4},{6,7},{7,6},{8,9},{9,8},{10,11... | collective-permute-start | bytes 1572872 | tf_op jit(solution)/shard_map/ppermute | solution.py:372
  45.2 24.7 %copy-start.6 = (bf16[2048,128]{1,0:T(8,128)(2,1)}, bf16[2048,128]{1,0:T(8,128)(2,1)S(1)}, u32[]{:S(2)}) copy-start(bf16[2048,128]{1,0:T(8,128)(2,1)S(1)} %collective-permute-done.7.refs_9_) | copy-start | bytes 1572868
  45.2 22.3 %collective-permute-start.14 = (bf16[2048,128]{1,0:T(8,128)(2,1)S(1)}, bf16[2048,128]{1,0:T(8,128)(2,1)S(1)}, u32[]{:S(2)}, u32[]{:S(2)}) collective-permute-start(bf16[2048,128]{1,0:T(8,128)(2,1)S(1)} %get-tuple-element.20.refs_8_), channel_id=1, source_target_pairs={{0,1},{1,0},{2,3},{3,2},{4,5},{5,4},{6,7},{7,6},{8,9},{9,8},{10,11... | collective-permute-start | bytes 1572872 | tf_op jit(solution)/shard_map/ppermute | solution.py:372
  45.7 21.8 %collective-permute-start.9 = (bf16[2048,128]{1,0:T(8,128)(2,1)S(1)}, bf16[2048,128]{1,0:T(8,128)(2,1)S(1)}, u32[]{:S(2)}, u32[]{:S(2)}) collective-permute-start(bf16[2048,128]{1,0:T(8,128)(2,1)S(1)} %get-tuple-element.18.refs_3_), channel_id=1, source_target_pairs={{0,1},{1,0},{2,3},{3,2},{4,5},{5,4},{6,7},{7,6},{8,9},{9,8},{10,11... | collective-permute-start | bytes 1572872 | tf_op jit(solution)/shard_map/ppermute | solution.py:372
  65.6 1.9 %copy-start.7 = (bf16[2048,128]{1,0:T(8,128)(2,1)}, bf16[2048,128]{1,0:T(8,128)(2,1)S(1)}, u32[]{:S(2)}) copy-start(bf16[2048,128]{1,0:T(8,128)(2,1)S(1)} %collective-permute-done.5.refs_5_) | copy-start | bytes 1572868
  65.6 1.9 collective-permute-start.13
  65.6 3.4 %copy-start.8 = (bf16[2048,128]{1,0:T(8,128)(2,1)}, bf16[2048,128]{1,0:T(8,128)(2,1)S(1)}, u32[]{:S(2)}) copy-start(bf16[2048,128]{1,0:T(8,128)(2,1)S(1)} %collective-permute-done.6.refs_6_) | copy-start | bytes 1572868
  65.6 3.4 %collective-permute-start.11 = (bf16[2048,128]{1,0:T(8,128)(2,1)S(1)}, bf16[2048,128]{1,0:T(8,128)(2,1)S(1)}, u32[]{:S(2)}, u32[]{:S(2)}) collective-permute-start(bf16[2048,128]{1,0:T(8,128)(2,1)S(1)} %collective-permute-done.5.refs_5_), channel_id=1, source_target_pairs={{0,1},{1,0},{2,3},{3,2},{4,5},{5,4},{6,7},{7,6},{8,9},{9,8},{10,11... | collective-permute-start | bytes 1572872 | tf_op jit(solution)/shard_map/ppermute | solution.py:372
  66.1 2.9 %copy-start.9 = (bf16[2048,128]{1,0:T(8,128)(2,1)}, bf16[2048,128]{1,0:T(8,128)(2,1)S(1)}, u32[]{:S(2)}) copy-start(bf16[2048,128]{1,0:T(8,128)(2,1)S(1)} %collective-permute-done.10.refs_12_) | copy-start | bytes 1572868
  66.1 3.7 %collective-permute-start.12 = (bf16[2048,128]{1,0:T(8,128)(2,1)S(1)}, bf16[2048,128]{1,0:T(8,128)(2,1)}, u32[]{:S(2)}, u32[]{:S(2)}) collective-permute-start(bf16[2048,128]{1,0:T(8,128)(2,1)S(1)} %collective-permute-done.6.refs_6_), channel_id=1, source_target_pairs={{0,1},{1,0},{2,3},{3,2},{4,5},{5,4},{6,7},{7,6},{8,9},{9,8},{10,11... | collective-permute-start | bytes 1572872 | tf_op jit(solution)/shard_map/ppermute | solution.py:372
  67.5 1.5 copy-start.12
  67.5 1.5 copy-start.10
  67.5 1.5 copy-start.11
  69.0 0.8 copy-start.13
  100.4 21.4 %all-to-all-start.2 = ((bf16[16,64,256]{2,1,0:T(8,128)(2,1)}), bf16[16,64,256]{2,1,0:T(8,128)(2,1)S(1)}, u32[]{:S(2)}, u32[]{:S(2)}) async-start(bf16[16,64,256]{2,1,0:T(8,128)(2,1)} %section.5), calls=%async_computation.2 | async-start | bytes 1048576 | tf_op jit(solution)/shard_map/all_to_all | solution.py:392
  106.2 37.9 %collective-permute-start.15 = (bf16[128,1024]{1,0:T(8,128)(2,1)S(1)}, bf16[128,1024]{1,0:T(8,128)(2,1)S(1)}, u32[]{:S(2)}, u32[]{:S(2)}) collective-permute-start(bf16[128,1024]{1,0:T(8,128)(2,1)S(1)} %copy-done.16), channel_id=1, source_target_pairs={{0,1},{1,0},{2,3},{3,2},{4,5},{5,4},{6,7},{7,6},{8,9},{9,8},{10,11... | collective-permute-start | bytes 786440 | tf_op jit(solution)/shard_map/ppermute | solution.py:372
  107.0 48.6 %copy-start.20 = (s32[1,4]{1,0:T(1,128)S(1)}, s32[1,4]{1,0:T(1,128)}, u32[]{:S(2)}) copy-start(s32[1,4]{1,0:T(1,128)} %param.18) | copy-start | bytes 52
  121.8 0.8 copy-start.15
  125.8 18.3 %all-to-all-start.3 = ((bf16[16,64,256]{2,1,0:T(8,128)(2,1)}), bf16[16,64,256]{2,1,0:T(8,128)(2,1)S(1)}, u32[]{:S(2)}, u32[]{:S(2)}) async-start(bf16[16,64,256]{2,1,0:T(8,128)(2,1)} %section.6.gate_ref), calls=%async_computation.3 | async-start | bytes 1048576 | tf_op jit(solution)/shard_map/all_to_all | solution.py:392
  144.2 0.7 copy-start.17
  144.2 0.9 copy-start.14
  148.3 15.7 %all-to-all-start.4 = ((f32[16,4,1024]{2,1,0:T(4,128)}), f32[16,4,1024]{2,1,0:T(4,128)S(1)}, u32[]{:S(2)}, u32[]{:S(2)}) async-start(f32[16,4,1024]{2,1,0:T(4,128)} %section.7), calls=%async_computation.4 | async-start | bytes 524288 | tf_op jit(solution)/shard_map/all_to_all | solution.py:392
  164.0 0.7 copy-start.18
Sparse Core Ops, SparseCore 0:
  10.4 115.2 all-gather.1

commit v4 on v3

--- a/solution.py
+++ b/solution.py
@@ -29,73 +29,107 @@
     return copies
 
 
-def early_kernel(gate_ref, prev_in, embed_in, pos_in, gain_in, pack_ref, q_out, acc_out, top_out, sum_out,
-                 prev_ref, embed_ref, pos_ref, gain_ref, n_ref, k_ref, v_ref, wq, sems, small_sems):
+def embed_kernel(prev_ref, embed_ref, pos_ref, gain_ref, out_ref):
     bars, chars = prev_ref.shape
-    vocab, width = embed_ref.shape
-    small = fetched((prev_in, embed_in, pos_in, gain_in), (prev_ref, embed_ref, pos_ref, gain_ref), small_sems)
-    copies = [pltpu.make_async_copy(pack_ref.at[:, j], wq.at[j], sems.at[j]) for j in range(3)]
-    for copy in small:
-        copy.wait()
-    copies[0].start()
     for b in range(bars):
         emb = embedded(prev_ref[b:b + 1, :], embed_ref, pos_ref)
-        n_ref[b * chars:(b + 1) * chars] = rms_rows(emb, gain_ref[0:1]).astype(BF)
-    for j, dst in ((0, q_out), (1, k_ref), (2, v_ref)):
+        out_ref[b * chars:(b + 1) * chars] = rms_rows(emb, gain_ref[0:1]).astype(BF)
+
+
+def embed_chars(prev, embed, pos, gain):
+    vm = pl.BlockSpec(memory_space=pltpu.VMEM)
+    return pl.pallas_call(
+        embed_kernel,
+        out_shape=jax.ShapeDtypeStruct((prev.size, embed.shape[1]), BF),
+        in_specs=[vm] * 4,
+        out_specs=vm,
+        compiler_params=pltpu.CompilerParams(vmem_limit_bytes=VMEM_BYTES),
+        name="embed",
+    )(prev, embed, pos, gain)
+
+
+def early_kernel(gate_ref, n_in, pack_ref, q_out, acc_out, top_out, sum_out,
+                 q_ref, acc_ref, top_ref, sum_ref, n_ref, k_ref, v_ref, wq, sems, out_sems):
+    tokens, width = n_ref.shape
+    chars = 128
+    bars = tokens // chars
+    copies = [pltpu.make_async_copy(pack_ref.at[:, j], wq.at[j], sems.at[j]) for j in range(3)]
+    load = pltpu.make_async_copy(n_in, n_ref, sems.at[3])
+    load.start()
+    copies[0].start()
+    load.wait()
+    q_store = pltpu.make_async_copy(q_ref, q_out, out_sems.at[3 * bars])
+    for j, dst in ((0, q_ref), (1, k_ref), (2, v_ref)):
         copies[j].wait()
         if j < 2:
             copies[j + 1].start()
-        dst[...] = jnp.dot(n_ref[...], wq[j].reshape(width, width), preferred_element_type=F32).astype(BF)
+        made = jnp.dot(n_ref[...], wq[j].reshape(width, width), preferred_element_type=F32).astype(BF)
+        dst[...] = made * BF(0.125) if j == 0 else made
+        if j == 0:
+            q_store.start()
+
+    def stores(b):
+        rows = pl.ds(pl.multiple_of(b * chars, chars), chars)
+        return [pltpu.make_async_copy(source.at[rows], to.at[rows], out_sems.at[3 * b + i])
+                for i, (source, to) in enumerate(((acc_ref, acc_out), (top_ref, top_out), (sum_ref, sum_out)))]
+
     low = lax.broadcasted_iota(jnp.int32, (chars, 128), 1) < 64
     query = lax.broadcasted_iota(jnp.int32, (chars, chars), 0)
     key = lax.broadcasted_iota(jnp.int32, (chars, chars), 1)
     seen = (query >= key) & (key > 0)
-    head = lax.broadcasted_iota(jnp.int32, (chars, HEADS), 1)
+    second = lax.broadcasted_iota(jnp.int32, (2 * chars, 128), 0) // chars
+    column = lax.broadcasted_iota(jnp.int32, (2 * chars, 128), 1)
 
     def attend(b, carry):
         rows = pl.ds(pl.multiple_of(b * chars, chars), chars)
-        tops = jnp.full((chars, HEADS), -1e30, F32)
-        sums = jnp.zeros((chars, HEADS), F32)
+        tops = jnp.full((chars, 128), -1e30, F32)
+        sums = jnp.zeros((chars, 128), F32)
         for h in range(width // 128):
             cols = slice(h * 128, (h + 1) * 128)
-            q, k, v = q_out[rows, cols], k_ref[rows, cols], v_ref[rows, cols]
+            q, k, v = q_ref[rows, cols], k_ref[rows, cols], v_ref[rows, cols]
             zero = jnp.zeros_like(k)
             kk = jnp.concatenate([jnp.where(low, k, zero), jnp.where(low, zero, k)], axis=0)
             vv = jnp.concatenate([jnp.where(low, v, zero), jnp.where(low, zero, v)], axis=0)
+            ones = (column == 2 * h + second).astype(F32).astype(BF)
             s = lax.dot_general(q, kk, (((1,), (1,)), ((), ())), preferred_element_type=F32)
             probs = []
             for half in range(2):
                 t = jnp.where(seen, s[:, half * chars:(half + 1) * chars], -1e30)
                 top = jnp.max(t, axis=-1, keepdims=True)
-                e = jnp.where(seen, jnp.exp((t - top) * 0.125), 0.0)
-                tops = jnp.where(head == 2 * h + half, top, tops)
-                sums = jnp.where(head == 2 * h + half, jnp.sum(e, axis=-1, keepdims=True), sums)
-                probs.append(e.astype(BF))
-            acc_out[rows, cols] = jnp.dot(jnp.concatenate(probs, axis=1), vv, preferred_element_type=F32)
-        top_out[rows] = tops
-        sum_out[rows] = sums
+                tops = jnp.where(key == 2 * h + half, top, tops)
+                probs.append(jnp.exp(t - top).astype(BF))
+            both = jnp.dot(jnp.concatenate(probs, axis=1), jnp.concatenate([vv, ones], axis=1), preferred_element_type=F32)
+            acc_ref[rows, cols] = both[:, :128]
+            sums += both[:, 128:]
+        top_ref[rows] = tops
+        sum_ref[rows] = sums
+        for store in stores(b):
+            store.start()
         return carry
 
     lax.fori_loop(0, bars, attend, 0)
-
-
-def early_decode(gate, prev, embed, pos, gain, pack):
-    bars, chars = prev.shape
-    width = embed.shape[1]
-    tokens = bars * chars
-    t = lambda d, w=width: jax.ShapeDtypeStruct((tokens, w), d)
+    q_store.wait()
+    for b in range(bars):
+        for store in stores(b):
+            store.wait()
+
+
+def early_decode(gate, normed, pack):
+    tokens, width = normed.shape
+    hbm = pl.BlockSpec(memory_space=pl.ANY)
+    shapes = ((width, BF), (width, F32), (128, F32), (128, F32))
     return pl.pallas_call(
         early_kernel,
-        out_shape=[t(BF), t(F32), t(F32, HEADS), t(F32, HEADS)],
-        in_specs=[pl.BlockSpec(memory_space=pl.ANY)] * 6,
-        out_specs=[pl.BlockSpec(memory_space=pltpu.VMEM)] * 4,
-        scratch_shapes=[pltpu.VMEM(v.shape, v.dtype) for v in (prev, embed, pos, gain)]
+        out_shape=[jax.ShapeDtypeStruct((tokens, w), d) for w, d in shapes],
+        in_specs=[hbm] * 3,
+        out_specs=[hbm] * 4,
+        scratch_shapes=[pltpu.VMEM((tokens, w), d) for w, d in shapes]
         + [pltpu.VMEM((tokens, width), BF)] * 3
-        + [pltpu.VMEM((3, 128, 8, width), BF), pltpu.SemaphoreType.DMA((3,)), pltpu.SemaphoreType.DMA((4,))],
+        + [pltpu.VMEM((3, 128, 8, width), BF), pltpu.SemaphoreType.DMA((4,)), pltpu.SemaphoreType.DMA((13,))],
         compiler_params=pltpu.CompilerParams(vmem_limit_bytes=VMEM_BYTES),
         cost_estimate=pl.CostEstimate(flops=8 << 30, bytes_accessed=16 << 20, transcendentals=1 << 20),
         name="early",
-    )(gate, prev, embed, pos, gain, pack)
+    )(gate, normed, pack)
 
 
 def late_kernel(*refs):
@@ -116,6 +150,8 @@
         copy.start()
     for copy in small[:7]:
         copy.wait()
+    for copy in small[7:]:
+        copy.start()
     for b in range(bars):
         x_ref[b * chars:(b + 1) * chars] = embedded(prev_ref[b:b + 1, :], embed_ref, pos_ref)
     vec = jnp.sum(parts_ref[...], axis=0).astype(BF).astype(F32)
@@ -124,9 +160,8 @@
     kv = []
     for j in range(2):
         copies[j].wait()
-        if j == 0:
-            for copy in small[7:]:
-                copy.start()
+        if j == 1:
+            copies[2].start()
         kv.append(jnp.dot(normed, wk[j].reshape(width, width), preferred_element_type=F32).astype(BF).astype(F32))
     member = (lax.broadcasted_iota(jnp.int32, (HEADS, width), 1) // 64
               == lax.broadcasted_iota(jnp.int32, (HEADS, width), 0))
@@ -134,8 +169,8 @@
 
     for copy in small[7:]:
         copy.wait()
-    copies[2].start()
     copies[3].start()
+    copies[7].start()
 
     def widen(v):
         high = v.astype(BF)
@@ -148,17 +183,16 @@
         key = jnp.where(member, kv[0][b:b + 1], 0.0).astype(BF)
         score = lax.dot_general(q_ref[rows, :], key, (((1,), (1,)), ((), ())), preferred_element_type=F32)
         start = lax.broadcasted_iota(jnp.int32, (chars, HEADS), 0) == 0
-        before = jnp.where(start, -1e30, top_in[rows, :])
+        before = jnp.where(start, -1e30, top_in[rows, :HEADS])
         score = jnp.where(start, 0.0, score)
         top = jnp.maximum(before, score)
-        old = jnp.exp((before - top) * 0.125)
-        new = jnp.exp((score - top) * 0.125)
-        inverse = 1.0 / (old * sum_in[rows, :] + new)
+        old = jnp.exp(before - top)
+        new = jnp.exp(score - top)
+        inverse = 1.0 / (old * sum_in[rows, :HEADS] + new)
         mixed = acc_ref[rows, :] * widen(old * inverse) + kv[1][b:b + 1] * widen(new * inverse)
         c_ref[rows, :] = mixed.astype(BF)
         x_ref[b * chars:b * chars + 1, :] = first[b:b + 1]
     copies[2].wait()
-    copies[7].start()
     copies[4].start()
     hidden = x_ref[...] + jnp.dot(c_ref[...], wo[...].reshape(width, width), preferred_element_type=F32)
     x_ref[...] = hidden
@@ -213,28 +247,33 @@
 
 
 def section_kernel(step, project, x_in, *refs):
-    own, other, refs = refs[:8], refs[8:16], refs[16:]
+    kept = 8 if project else 6 if step == 0 else 5
+    weights, refs = refs[:-kept], refs[-kept:]
     if project:
-        proj_own, proj_other, _, out_ref, x_ref, w_ref, sems, p_ref, p_sems = refs
+        proj_own, proj_other, out_ref, x_ref, w_ref, sems, p_ref, p_sems = refs
+    elif step == 0:
+        out_ref, row_ref, x_ref, w_ref, sems, _ = refs
     else:
-        out_ref, x_ref, w_ref, sems, row_ref, out_sems = refs
+        out_ref, x_ref, w_ref, sems, row_ref = refs
     blocks, rows, cols = x_ref.shape
     side, depth = cols // 2, blocks * cols
     half = depth // 2
-    core = lax.axis_index("c")
-    which = lax.rem(lax.axis_index("y") - step + 4, 4)
+    y, core = lax.axis_index("y"), lax.axis_index("c")
+    which = jnp.where(y < 2, (y, 1 - y, 3 - y, 2 + y)[step], (y - 2, y, y - 2, 3 - y)[step])
     chip = lax.axis_index("x") * 4 + lax.axis_index("z")
     load_x = pltpu.make_async_copy(x_in, x_ref, sems.at[4])
     load_x.start()
-    for i in range(4):
+    held = [(weights[i], weights[i + 1]) for i in range(0, min(len(weights), 6), 2)]
+    held += [(weights[6:8], weights[8:])] if len(weights) > 6 else []
+    for i, pair in enumerate(held):
         @pl.when(which == i)
         def _():
             for part in range(2):
-                for sources, at, sem in ((own, core, 0), (other, 1 - core, 1)):
+                span = pl.ds(part * half, half)
+                for sem, at in ((0, core), (1, 1 - core)):
                     lanes = pl.ds(pl.multiple_of(at * side, side), side)
-                    pltpu.make_async_copy(
-                        sources[2 * i + part], w_ref.at[pl.ds(part * half, half), lanes], sems.at[2 * part + sem]
-                    ).start()
+                    source = pair[sem].at[span] if i < 3 else pair[sem][part]
+                    pltpu.make_async_copy(source, w_ref.at[span, lanes], sems.at[2 * part + sem]).start()
     if project:
         deep = proj_own.shape[0]
         loads = [
@@ -254,7 +293,7 @@
         span = pl.ds(part * half, half)
         for sem in range(2):
             at = w_ref.at[span, pl.ds(sem * side, side)]
-            pltpu.make_async_copy(own[0], at, sems.at[2 * part + sem]).wait()
+            pltpu.make_async_copy(weights[0].at[span], at, sems.at[2 * part + sem]).wait()
         wide = jnp.concatenate([x_ref[part * blocks // 2 + j] for j in range(blocks // 2)], axis=1)
         update += jnp.dot(wide, w_ref[span, :], preferred_element_type=F32)
     leaving = (x_ref[chip].astype(F32) + jax.nn.gelu(update * scale)).astype(BF)
@@ -265,23 +304,26 @@
         each = rows // blocks
         for j in range(blocks):
             out_ref[j] = partial[j * each:(j + 1) * each]
+    elif step == 0:
+        out_ref[...] = leaving[:rows // 2]
+        row_ref[...] = leaving[rows // 2:]
     else:
         row_ref[...] = leaving
-        sends = [pltpu.make_async_copy(row_ref, out_ref.at[j], out_sems.at[j]) for j in range(blocks)]
+        sends = [pltpu.make_async_copy(row_ref, out_ref.at[j], sems.at[5 + j]) for j in range(blocks)]
         for send in sends:
             send.start()
         for send in sends:
             send.wait()
 
 
-def section_step(step, x, own, other, proj=()):
+def section_step(step, x, weights, proj=()):
     blocks, rows, cols = x.shape
     vm = pl.BlockSpec(memory_space=pltpu.VMEM)
     hbm = pl.BlockSpec(memory_space=pl.ANY)
-    scratch = [pltpu.VMEM(x.shape, BF), pltpu.VMEM((blocks * cols, cols), BF), pltpu.SemaphoreType.DMA((5,))]
+    scratch = [pltpu.VMEM(x.shape, BF), pltpu.VMEM((blocks * cols, cols), BF), pltpu.SemaphoreType.DMA((5 + blocks,))]
     if not proj:
-        out = jax.ShapeDtypeStruct(x.shape, BF)
-        scratch += [pltpu.VMEM((rows, cols), BF), pltpu.SemaphoreType.DMA((blocks,))]
+        out = [jax.ShapeDtypeStruct((rows // 2, cols), BF)] * 2 if step == 0 else jax.ShapeDtypeStruct(x.shape, BF)
+        scratch += [pltpu.VMEM((rows, cols), BF)]
     else:
         width = proj[0].shape[1]
         out = jax.ShapeDtypeStruct((blocks, rows // blocks, width), F32)
@@ -289,17 +331,17 @@
     return pl.pallas_call(
         lambda *refs: section_kernel(step, len(proj) > 0, *refs),
         out_shape=out,
-        in_specs=[hbm] * (17 + len(proj)),
-        out_specs=vm if proj else hbm,
+        in_specs=[hbm] * (1 + len(weights) + len(proj)),
+        out_specs=[vm, vm] if step == 0 else vm if proj else hbm,
         scratch_shapes=scratch,
         compiler_params=pltpu.CompilerParams(vmem_limit_bytes=VMEM_BYTES),
         cost_estimate=pl.CostEstimate(flops=1, bytes_accessed=1, transcendentals=0),
         name="section",
-    )(x, *own, *other, *proj)
+    )(x, *weights, *proj)
 
 
 def prepare_kernel(*refs):
-    sources, outs, scratch = refs[:6], refs[6:9], refs[9:]
+    sources, outs, scratch = refs[:6], refs[6:8], refs[8:]
     held, (pack_ref, sems, out_sem) = scratch[:6], scratch[6:]
     loads = [pltpu.make_async_copy(source, to, sems.at[i]) for i, (source, to) in enumerate(zip(sources, held))]
     for load in loads:
@@ -318,12 +360,10 @@
     store.start()
     loads[4].wait()
     loads[5].wait()
-    rows = outs[1].shape[0]
     for i in range(gain_ref.shape[0]):
         span = slice(i * 128, (i + 1) * 128)
         column = jnp.transpose(jnp.broadcast_to(gain_ref[i:i + 1, :], (128, 128)))
-        first = i * 128 % rows
-        outs[1 + i * 128 // rows][first:first + 128] = (w_ref[span, :].astype(F32) * column).astype(BF)
+        outs[1][span, :] = (w_ref[span, :].astype(F32) * column).astype(BF)
     store.wait()
 
 
@@ -332,12 +372,11 @@
     width = sources[1].shape[1]
     hbm = pl.BlockSpec(memory_space=pl.ANY)
     vm = pl.BlockSpec(memory_space=pltpu.VMEM)
-    half = jax.ShapeDtypeStruct((depth // 2, cols), BF)
     return pl.pallas_call(
         prepare_kernel,
-        out_shape=[jax.ShapeDtypeStruct((12, 8, width), BF), half, half],
+        out_shape=[jax.ShapeDtypeStruct((12, 8, width), BF), jax.ShapeDtypeStruct((depth, cols), BF)],
         in_specs=[hbm] * 6,
-        out_specs=[hbm, vm, vm],
+        out_specs=[hbm, vm],
         scratch_shapes=[pltpu.VMEM(v.shape, v.dtype) for v in sources]
         + [pltpu.VMEM((12, 8, width), BF), pltpu.SemaphoreType.DMA((6,)), pltpu.SemaphoreType.DMA],
         compiler_params=pltpu.CompilerParams(vmem_limit_bytes=VMEM_BYTES),
@@ -371,41 +410,47 @@
     def swap(v):
         return lax.ppermute(v, "c", [(0, 1), (1, 0)])
 
-    def turn(v, by):
-        return lax.ppermute(v, "y", [(i, (i + by) % 4) for i in range(4)])
+    def across(v, *pairs):
+        return lax.ppermute(v, "y", pairs)
 
     def ordered(mine, theirs, axis):
         return jnp.where(core == 0, jnp.concatenate([mine, theirs], axis), jnp.concatenate([theirs, mine], axis))
 
     feats = bar_in.shape[2]
-    pack, low, high = prepare(
+    pack, weight = prepare(
         attn_in, attn_out, ffn_in, ffn_out, section_weight[0], section_gain.reshape(-1, 128))
     pack = lax.all_gather(pack.reshape(96, width), GROUP, axis=0, tiled=True).reshape(128, 12, 8, width)
 
-    by_core = lax.dynamic_index_in_dim(bar_in, y, 0, keepdims=False).reshape(16, 2, 4, feats)
-    by_core = by_core.transpose(1, 0, 2, 3).reshape(2, 64, feats)
+    pair = jnp.stack([jnp.minimum(y, 3 - y), jnp.maximum(y, 3 - y)])
+    by_core = jnp.concatenate([lax.dynamic_slice_in_dim(bar_in, pair[i], 1, 0) for i in range(2)])
+    by_core = by_core.reshape(2, 16, 2, 4, feats).transpose(2, 0, 1, 3, 4).reshape(2, 128, feats)
     mine = lax.dynamic_index_in_dim(by_core, core, 0, keepdims=False)
     theirs = swap(lax.dynamic_index_in_dim(by_core, 1 - core, 0, keepdims=False))
-    block = ordered(mine, theirs, 1)
 
     def spread(v):
         return lax.all_to_all(v, ("x", "z"), 0, 0, tiled=True)
 
-    x = spread(jnp.broadcast_to(block[None], (16,) + block.shape))
-    below_low, above_high, below_high, above_low = after(
-        [x], [turn(low, 1), turn(high, 3), turn(high, 1), turn(low, 3)])
-    own = [low, high, below_low, below_high, turn(below_low, 1), turn(above_high, 3), above_low, above_high]
-    other = [swap(w) for w in own]
-    proj = [projection, swap(projection)]
-    for step in range(4):
-        if step:
-            x = spread(out)
-        out = section_step(step, x, own, other, [*proj, early[2]] if step == 3 else ())
-        if step == 2:
-            ids, prev = char_ids[0], shifted(char_ids[0])
-            early = early_decode(out, prev, char_embed, char_pos, norm_gain, pack)
+    def copies(v):
+        return jnp.broadcast_to(v[None], (16,) + v.shape)
+
+    x = spread(copies(ordered(mine, theirs, 1)))
+    near, far = after([x], [across(weight, (0, 1), (1, 0), (2, 3), (3, 2)), across(weight, (1, 2), (2, 1), (3, 0))])
+    weights = [weight, swap(weight), near, swap(near)]
+    half = near.shape[0] // 2
+    farther = [across(far[:half], (0, 1), (1, 0), (2, 3)), across(near[half:], (0, 3), (3, 0), (2, 1))]
+    far_other = swap(far)
+    here, there = section_step(0, x, weights)
+    there = across(after([far_other], [there])[0], (0, 3), (1, 2))
+    x = spread(copies(jnp.where(y < 2, here, there)))
+    farther = after([x], farther)
+    weights += [far, far_other, *farther, *[swap(w) for w in farther]]
+    normed = embed_chars(shifted(char_ids[0]), char_embed, char_pos, norm_gain)
+    x = spread(section_step(1, x, weights))
+    x = spread(section_step(2, x, weights))
+    out = section_step(3, x, weights, [projection, swap(projection)])
+    early = early_decode(out, normed, pack)
     parts = spread(out)
-    return late_decode(parts, early, ids, prev, lengths[0][:, None], char_embed, char_pos, norm_gain, pack)[None]
+    return late_decode(parts, early, char_ids[0], shifted(char_ids[0]), lengths[0][:, None], char_embed, char_pos, norm_gain, pack)[None]
 
 
 def solution(mesh):

time: 193 us -> 177 us (0.917)
  waiting for transfers between devices: 61.9 us -> 41.8 us
  local copies, waits for them, and re-layouts: 5.42 us -> 11.3 us
  blocking collectives: 24.2 us -> 22.2 us
    ppermute x6 -> x5, waiting for transfers between devices: 36.4 us -> 7.79 us  [across(): return lax.ppermute(v, 'y', pairs)]
    all_to_all x4, waiting for transfers between devices: 22.7 us -> 30.4 us  [spread(): return lax.all_to_all(v, ('x', 'z'), 0, 0, tiled=True)]
    all_to_all x4, starting transfers between devices: 26.7 us -> 23.8 us  [spread(): return lax.all_to_all(v, ('x', 'z'), 0, 0, tiled=True)]
    slice x0 -> x2, local copies, waits for them, and re-layouts: none -> 2.77 us  [the longest x1 1.89 us: body(): near[half:]]
    ppermute x6 -> x5, starting transfers between devices: 9.73 us -> 12.3 us  [across(): return lax.ppermute(v, 'y', pairs)]
    all_to_all x1, blocking collectives: 24.2 us -> 22.2 us  [spread(): return lax.all_to_all(v, ('x', 'z'), 0, 0, tiled=True)]
    unnamed x42 -> x30, local copies, waits for them, and re-layouts: 3.22 us -> 4.45 us
    pallas_call x1 -> x2, Pallas kernels: 12.5 us -> 12.9 us  [the longest x1 10.1 us: early_decode(): pl.pallas_call(early_kernel, out_shape=[jax.ShapeDtypeStruct((tokens, w),...]
  transfers between devices with their start and end apart: 21 -> 17, of which waited for: 6 -> 8; matrix products, arithmetic and copies ran while one was open for 1% -> 4% of each run, Pallas kernels for 11% -> 15%
where the time goes in v4:
time: 177 us; the launch traced here: 176 us
  Pallas kernels  48.8 us (28%)
  waiting for transfers between devices  41.8 us (24%)
  starting transfers between devices  36.9 us (21%)
  blocking collectives  22.2 us (13%)
  between operations  13.7 us (8%)
  local copies, waits for them, and re-layouts  11.3 us (6%)
    all_to_all x4, waiting for transfers between devices, spread(): return lax.all_to_all(v, ('x', 'z'), 0, 0, tiled=True)  30.4 us
    all_to_all x4, starting transfers between devices, spread(): return lax.all_to_all(v, ('x', 'z'), 0, 0, tiled=True)  23.8 us
    all_to_all x1, blocking collectives, spread(): return lax.all_to_all(v, ('x', 'z'), 0, 0, tiled=True)  22.2 us
    pallas_call x1, Pallas kernels, late_decode(): pl.pallas_call(late_kernel, out_shape=jax.ShapeDtypeStruct((bars, chars),...  19.9 us
    pallas_call x4, Pallas kernels, section_step(): pl.pallas_call(lambda *refs: section_kernel(step, len(proj) > 0, *refs),...  12.9 us
    ppermute x5, starting transfers between devices, across(): return lax.ppermute(v, 'y', pairs)  12.3 us
    pallas_call x1, Pallas kernels, early_decode(): pl.pallas_call(early_kernel, out_shape=[jax.ShapeDtypeStruct((tokens, w),...  10.1 us
    ppermute x5, waiting for transfers between devices, across(): return lax.ppermute(v, 'y', pairs)  7.79 us
  transfers between devices with their start and end apart: 17, of which 8 were waited for; matrix products, arithmetic and copies ran while one was open for 4% of the time, Pallas kernels for 15%

profile of v4, /device:TPU:0, one launch (start us, length us, event | category | flops | bytes accessed | tf_op | source)
XLA Modules:
  0.0 175.5 jit_solution(14124635514442277188)
XLA Ops:
  6.5 3.0 %prepare.1 = (bf16[12,8,1024]{2,1,0:T(8,128)(2,1)}, bf16[4096,128]{1,0:T(8,128)(2,1)}) custom-call(bf16[8,3072]{1,0:T(8,128)(2,1)} %refs_0_.1, bf16[8,1024]{1,0:T(8,128)(2,1)} %refs_1_.1, bf16[8,4096]{1,0:T(8,128)(2,1)} %refs_2_.1, bf16[32,1024]{1,0:T(8,128)(2,1)} %refs_3_.1, bf16[4096,128]{1,0:T(8,128)(2,1)} %bitcast.16, f32[32,128]{1,0:T(8,128)} %bitcast.20), custom_call_target="tpu_custom_call" | custom-call | tf_op jit(solution)/shard_map/prepare/pallas_call | solution.py:375
  9.6 0.0 all-gather.2.cloned.1.call-update
  9.6 0.8 constant_dynamic-slice_fusion.1
  10.5 0.1 collective-permute-start
  10.6 1.7 collective-permute-start.2
  12.3 1.3 collective-permute-start.3
  13.6 1.1 broadcast_in_dim.6
  14.7 7.9 %all-to-all-start = ((bf16[16,128,256]{2,1,0:T(8,128)(2,1)}), bf16[16,128,256]{2,1,0:T(8,128)(2,1)S(1)}, u32[]{:S(2)}, u32[]{:S(2)}) async-start(bf16[16,128,256]{2,1,0:T(8,128)(2,1)} %broadcast_in_dim.6), calls=%async_computation | async-start | bytes 2097152 | tf_op jit(solution)/shard_map/all_to_all | solution.py:431
  22.6 0.1 collective-permute-start.1
  22.7 20.0 %all-to-all-done.refs_0_ = bf16[16,128,256]{2,1,0:T(8,128)(2,1)S(1)} async-done(((bf16[16,128,256]{2,1,0:T(8,128)(2,1)}), bf16[16,128,256]{2,1,0:T(8,128)(2,1)S(1)}, u32[]{:S(2)}, u32[]{:S(2)}) %all-to-all-start) | async-done | bytes 1048608 | tf_op jit(solution)/shard_map/all_to_all | solution.py:431
  42.7 0.0 collective-permute-done.2.refs_1_
  42.7 0.2 collective-permute-done.3.refs_2_
  42.9 0.7 copy-done.3
  43.7 2.1 %collective-permute-done.4.refs_4_ = bf16[4096,128]{1,0:T(8,128)(2,1)} collective-permute-done((bf16[4096,128]{1,0:T(8,128)(2,1)S(1)}, bf16[4096,128]{1,0:T(8,128)(2,1)}, u32[]{:S(2)}, u32[]{:S(2)}) %collective-permute-start.4) | collective-permute-done | bytes 1048608 | tf_op jit(solution)/shard_map/ppermute | solution.py:411
  45.7 3.1 %section.4 = (bf16[64,256]{1,0:T(8,128)(2,1)}, bf16[64,256]{1,0:T(8,128)(2,1)}) custom-call(bf16[16,128,256]{2,1,0:T(8,128)(2,1)} %copy-done.3, bf16[4096,128]{1,0:T(8,128)(2,1)} %get-tuple-element.17.refs_1_, bf16[4096,128]{1,0:T(8,128)(2,1)} %collective-permute-done.1.refs_2_, bf16[4096,128]{1,0:T(8,128)(2,1)} %copy-done, ...), custom_call_target="tpu_custom_call" | custom-call | flops 1 | bytes 1 | tf_op jit(solution)/shard_map/section/pallas_call | solution.py:331
  48.9 0.8 copy-done.6
  49.7 0.6 copy-done.7
  50.3 5.5 %collective-permute-start.6 = (bf16[64,256]{1,0:T(8,128)(2,1)}, bf16[64,256]{1,0:T(8,128)(2,1)S(1)}, u32[]{:S(2)}, u32[]{:S(2)}) collective-permute-start(bf16[64,256]{1,0:T(8,128)(2,1)} %copy-done.7), channel_id=1, source_target_pairs={{0,96},{32,64},{1,97},{33,65},{2,98},{34,66},{3,99},{35,67},{4,100... | collective-permute-start | bytes 98312 | tf_op jit(solution)/shard_map/ppermute | solution.py:414
  55.7 0.9 slice.10
  56.6 1.9 %slice.11 = bf16[2048,128]{1,0:T(8,128)(2,1)} slice(bf16[4096,128]{1,0:T(8,128)(2,1)} %copy-done), slice={[2048:4096], [0:128]} | slice | bytes 1048576 | tf_op jit(solution)/shard_map/slice | solution.py:440
  58.5 1.9 %collective-permute-start.7 = (bf16[2048,128]{1,0:T(8,128)(2,1)}, bf16[2048,128]{1,0:T(8,128)(2,1)S(1)}, u32[]{:S(2)}, u32[]{:S(2)}) collective-permute-start(bf16[2048,128]{1,0:T(8,128)(2,1)} %slice.10), channel_id=1, source_target_pairs={{0,32},{32,0},{64,96},{1,33},{33,1},{65,97},{2,34},{34,2},{66,98},... | collective-permute-start | bytes 1572872 | tf_op jit(solution)/shard_map/ppermute | solution.py:414
  60.4 1.9 %collective-permute-start.8 = (bf16[2048,128]{1,0:T(8,128)(2,1)}, bf16[2048,128]{1,0:T(8,128)(2,1)S(1)}, u32[]{:S(2)}, u32[]{:S(2)}) collective-permute-start(bf16[2048,128]{1,0:T(8,128)(2,1)} %slice.11), channel_id=1, source_target_pairs={{0,96},{96,0},{64,32},{1,97},{97,1},{65,33},{2,98},{98,2},{66,34},... | collective-permute-start | bytes 1572872 | tf_op jit(solution)/shard_map/ppermute | solution.py:414
  62.4 0.8 broadcast_select_fusion
  63.1 0.9 broadcast_in_dim.7
  64.0 6.6 %all-to-all-start.1 = ((bf16[16,64,256]{2,1,0:T(8,128)(2,1)}), bf16[16,64,256]{2,1,0:T(8,128)(2,1)}, u32[]{:S(2)}, u32[]{:S(2)}) async-start(bf16[16,64,256]{2,1,0:T(8,128)(2,1)} %broadcast_in_dim.7), calls=%async_computation.1 | async-start | bytes 1048576 | tf_op jit(solution)/shard_map/all_to_all | solution.py:431
  70.6 5.5 %collective-permute-done.7.refs_1_ = bf16[2048,128]{1,0:T(8,128)(2,1)S(1)} collective-permute-done((bf16[2048,128]{1,0:T(8,128)(2,1)}, bf16[2048,128]{1,0:T(8,128)(2,1)S(1)}, u32[]{:S(2)}, u32[]{:S(2)}) %collective-permute-start.7) | collective-permute-done | bytes 524320 | tf_op jit(solution)/shard_map/ppermute | solution.py:414
  76.1 2.1 %collective-permute-done.8.refs_2_ = bf16[2048,128]{1,0:T(8,128)(2,1)S(1)} collective-permute-done((bf16[2048,128]{1,0:T(8,128)(2,1)}, bf16[2048,128]{1,0:T(8,128)(2,1)S(1)}, u32[]{:S(2)}, u32[]{:S(2)}) %collective-permute-start.8) | collective-permute-done | bytes 524320 | tf_op jit(solution)/shard_map/ppermute | solution.py:414
  78.1 4.0 %all-to-all-done.1.refs_0_ = bf16[16,64,256]{2,1,0:T(8,128)(2,1)} async-done(((bf16[16,64,256]{2,1,0:T(8,128)(2,1)}), bf16[16,64,256]{2,1,0:T(8,128)(2,1)}, u32[]{:S(2)}, u32[]{:S(2)}) %all-to-all-start.1) | async-done | bytes 524320 | tf_op jit(solution)/shard_map/all_to_all | solution.py:431
  82.2 0.5 collective-permute-start.9
  82.7 1.4 collective-permute-done.10.refs_10_
  84.1 0.8 copy-done.8
  84.9 0.1 collective-permute-done.9.refs_9_
  85.0 3.3 %section.5 = bf16[16,64,256]{2,1,0:T(8,128)(2,1)} custom-call(bf16[16,64,256]{2,1,0:T(8,128)(2,1)} %all-to-all-done.1.refs_0_, bf16[4096,128]{1,0:T(8,128)(2,1)} %get-tuple-element.17.refs_1_, bf16[4096,128]{1,0:T(8,128)(2,1)} %collective-permute-done.1.refs_2_, bf16[4096,128]{1,0:T(8,128)(2,1)} %copy-done, ...), custom_call_target="tpu_custom_call" | custom-call | flops 1 | bytes 1 | tf_op jit(solution)/shard_map/section/pallas_call | solution.py:331
  88.3 22.2 %all_to_all.25.refs_0_ = bf16[16,64,256]{2,1,0:T(8,128)(2,1)} all-to-all(bf16[16,64,256]{2,1,0:T(8,128)(2,1)} %section.5), channel_id=1, replica_groups=mesh['y'=4,'x'=4,'z'=4,'c'=2] {'x','z'}, dimensions={0} | all-to-all | bytes 1048576 | tf_op jit(solution)/shard_map/all_to_all | solution.py:431
  110.5 3.1 %section.6 = bf16[16,64,256]{2,1,0:T(8,128)(2,1)} custom-call(bf16[16,64,256]{2,1,0:T(8,128)(2,1)} %all_to_all.25.refs_0_, bf16[4096,128]{1,0:T(8,128)(2,1)} %get-tuple-element.17.refs_1_, bf16[4096,128]{1,0:T(8,128)(2,1)} %collective-permute-done.1.refs_2_, bf16[4096,128]{1,0:T(8,128)(2,1)} %copy-done, bf16[4096,128]{1,0:T(8,128)(2,1)} %collective-permute-done.4.refs_4_, ...), custom_call_target="tpu_custom_call" | custom-call | flops 1 | bytes 1 | tf_op jit(solution)/shard_map/section/pallas_call | solution.py:331
  113.6 5.9 %all-to-all-start.3 = ((bf16[16,64,256]{2,1,0:T(8,128)(2,1)}), bf16[16,64,256]{2,1,0:T(8,128)(2,1)S(1)}, u32[]{:S(2)}, u32[]{:S(2)}) async-start(bf16[16,64,256]{2,1,0:T(8,128)(2,1)} %section.6), calls=%async_computation.3 | async-start | bytes 1048576 | tf_op jit(solution)/shard_map/all_to_all | solution.py:431
  119.5 0.1 collective-permute-start.11
  119.6 0.7 copy.21.refs_3_
  120.3 0.7 concatenate.27.prev_ref.refs_2_
  120.9 2.8 %embed.1.n_in = bf16[512,1024]{1,0:T(8,128)(2,1)} custom-call(s32[4,128]{1,0:T(4,128)} %concatenate.27.prev_ref.refs_2_, bf16[128,1024]{1,0:T(8,128)(2,1)} %refs_4_.1, bf16[128,1024]{1,0:T(8,128)(2,1)} %refs_5_.1, f32[3,1024]{1,0:T(4,128)} %refs_6_.1), custom_call_target="tpu_custom_call" | custom-call | tf_op jit(solution)/shard_map/embed/pallas_call | solution.py:41
  123.7 6.4 %all-to-all-done.3.refs_0_ = bf16[16,64,256]{2,1,0:T(8,128)(2,1)S(1)} async-done(((bf16[16,64,256]{2,1,0:T(8,128)(2,1)}), bf16[16,64,256]{2,1,0:T(8,128)(2,1)S(1)}, u32[]{:S(2)}, u32[]{:S(2)}) %all-to-all-start.3) | async-done | bytes 524320 | tf_op jit(solution)/shard_map/all_to_all | solution.py:431
  130.1 0.8 copy-done.9
  130.9 3.4 %section.7.gate_ref = f32[16,4,1024]{2,1,0:T(4,128)} custom-call(bf16[16,64,256]{2,1,0:T(8,128)(2,1)} %copy-done.9, bf16[4096,128]{1,0:T(8,128)(2,1)} %get-tuple-element.17.refs_1_, bf16[4096,128]{1,0:T(8,128)(2,1)} %collective-permute-done.1.refs_2_, bf16[4096,128]{1,0:T(8,128)(2,1)} %copy-done, bf16[4096,128]{1,0:T(8,128)(2,1)} %collective-permute-done.4.refs_4_, ...), custom_call_target="tpu_custom_call" | custom-call | flops 1 | bytes 1 | tf_op jit(solution)/shard_map/section/pallas_call | solution.py:331
  134.3 3.5 %all-to-all-start.4 = ((f32[16,4,1024]{2,1,0:T(4,128)}), f32[16,4,1024]{2,1,0:T(4,128)S(1)}, u32[]{:S(2)}, u32[]{:S(2)}) async-start(f32[16,4,1024]{2,1,0:T(4,128)} %section.7.gate_ref), calls=%async_computation.4 | async-start | bytes 524288 | tf_op jit(solution)/shard_map/all_to_all | solution.py:431
  137.8 0.0 all-gather.2.cloned.1.call-done
  137.9 10.1 %early.1 = (bf16[512,1024]{1,0:T(8,128)(2,1)}, f32[512,1024]{1,0:T(8,128)}, f32[512,128]{1,0:T(8,128)}, f32[512,128]{1,0:T(8,128)}) custom-call(f32[16,4,1024]{2,1,0:T(4,128)} %section.7.gate_ref, bf16[512,1024]{1,0:T(8,128)(2,1)} %embed.1.n_in, bf16[128,12,8,1024]{3,2,1,0:T(8,128)(2,1)} %bitcast.24), custom_call_target="tpu_custom_call" | custom-call | flops 8589934592 | bytes 16777216 | tf_op jit(solution)/shard_map/early/pallas_call | solution.py:121
  148.0 0.7 copy-done.12
  148.7 19.9 %late.1 = f32[4,128]{1,0:T(4,128)} custom-call(f32[16,4,1024]{2,1,0:T(4,128)} %copy-done.12, s32[4,128]{1,0:T(4,128)} %bitcast.21, s32[4,128]{1,0:T(4,128)} %concatenate.27.prev_ref.refs_2_, s32[4,1]{1,0:T(4,128)} %copy.21.refs_3_, bf16[128,1024]{1,0:T(8,128)(2,1)} %refs_4_.1, bf16[128,1024]{1,0:T(8,128)(2,1)} %refs_5_.1, f32[3,1024]{1,0:T(4,128)} %refs_6_.1, ...), custom_call_target="tpu_custom_call" | custom-call | flops 10737418240 | bytes 25165824 | tf_op jit(solution)/shard_map/late/pallas_call | solution.py:227
  (41 shorter events, 0.1 us)
Async XLA Ops:
  6.5 112.9 %copy-start.10 = (bf16[128,1024]{1,0:T(8,128)(2,1)S(1)}, bf16[128,1024]{1,0:T(8,128)(2,1)}, u32[]{:S(2)}) copy-start(bf16[128,1024]{1,0:T(8,128)(2,1)} %refs_11_.1) | copy-start | bytes 786436
  6.5 113.0 %copy-start.14 = (s32[1,4]{1,0:T(1,128)S(1)}, s32[1,4]{1,0:T(1,128)}, u32[]{:S(2)}) copy-start(s32[1,4]{1,0:T(1,128)} %param.18) | copy-start | bytes 52
  6.5 113.7 %copy-start.13 = (s32[1,4,128]{2,1,0:T(4,128)S(1)}, s32[1,4,128]{2,1,0:T(4,128)}, u32[]{:S(2)}) copy-start(s32[1,4,128]{2,1,0:T(4,128)} %param.17) | copy-start | bytes 6148
  6.5 131.3 %all-gather.2.cloned.1.call-start = ((), (), s32[]{:S(2)}) async-start(), calls=%async_computation.5 | async-start | bytes 25362432 | tf_op jit(solution)/shard_map/all_gather | solution.py:422
  10.5 3.1 %collective-permute-start = (bf16[128,128]{1,0:T(8,128)(2,1)S(1)}, bf16[128,128]{1,0:T(8,128)(2,1)S(1)}, u32[]{:S(2)}, u32[]{:S(2)}) collective-permute-start(bf16[128,128]{1,0:T(8,128)(2,1)S(1)} %get-tuple-element.32), channel_id=1, source_target_pairs={{0,1},{1,0},{2,3},{3,2},{4,5},{5,4},{6,7},{7,6},{8,9},{9,8},{10,11... | collective-permute-start | bytes 98312 | tf_op jit(solution)/shard_map/ppermute | solution.py:411
  10.6 32.1 %collective-permute-start.2 = (bf16[4096,128]{1,0:T(8,128)(2,1)}, bf16[4096,128]{1,0:T(8,128)(2,1)S(1)}, u32[]{:S(2)}, u32[]{:S(2)}) collective-permute-start(bf16[4096,128]{1,0:T(8,128)(2,1)} %get-tuple-element.17.refs_1_), channel_id=1, source_target_pairs={{0,32},{32,0},{64,96},{96,64},{1,33},{33,1},{65,97},{97,65},{2,34}... | collective-permute-start | bytes 3145736 | tf_op jit(solution)/shard_map/ppermute | solution.py:414
  12.3 30.6 %collective-permute-start.3 = (bf16[4096,128]{1,0:T(8,128)(2,1)}, bf16[4096,128]{1,0:T(8,128)(2,1)S(1)}, u32[]{:S(2)}, u32[]{:S(2)}) collective-permute-start(bf16[4096,128]{1,0:T(8,128)(2,1)} %get-tuple-element.17.refs_1_), channel_id=1, source_target_pairs={{32,64},{64,32},{96,0},{33,65},{65,33},{97,1},{34,66},{66,34},{98,... | collective-permute-start | bytes 3145736 | tf_op jit(solution)/shard_map/ppermute | solution.py:414
  14.7 28.0 %all-to-all-start = ((bf16[16,128,256]{2,1,0:T(8,128)(2,1)}), bf16[16,128,256]{2,1,0:T(8,128)(2,1)S(1)}, u32[]{:S(2)}, u32[]{:S(2)}) async-start(bf16[16,128,256]{2,1,0:T(8,128)(2,1)} %broadcast_in_dim.6), calls=%async_computation | async-start | bytes 2097152 | tf_op jit(solution)/shard_map/all_to_all | solution.py:431
  22.6 21.1 %collective-permute-start.1 = (bf16[4096,128]{1,0:T(8,128)(2,1)}, bf16[4096,128]{1,0:T(8,128)(2,1)}, u32[]{:S(2)}, u32[]{:S(2)}) collective-permute-start(bf16[4096,128]{1,0:T(8,128)(2,1)} %get-tuple-element.17.refs_1_), channel_id=1, source_target_pairs={{0,1},{1,0},{2,3},{3,2},{4,5},{5,4},{6,7},{7,6},{8,9},{9,8},{10,11... | collective-permute-start | bytes 3145736 | tf_op jit(solution)/shard_map/ppermute | solution.py:411
  42.7 1.0 copy-start.3
  42.9 2.8 %copy-start = (bf16[4096,128]{1,0:T(8,128)(2,1)}, bf16[4096,128]{1,0:T(8,128)(2,1)S(1)}, u32[]{:S(2)}) copy-start(bf16[4096,128]{1,0:T(8,128)(2,1)S(1)} %get-tuple-element.18.refs_3_) | copy-start | bytes 3145732
  42.9 42.0 %copy-start.1 = (bf16[4096,128]{1,0:T(8,128)(2,1)}, bf16[4096,128]{1,0:T(8,128)(2,1)S(1)}, u32[]{:S(2)}) copy-start(bf16[4096,128]{1,0:T(8,128)(2,1)S(1)} %get-tuple-element.20.refs_5_) | copy-start | bytes 3145732
  42.9 2.8 %collective-permute-start.4 = (bf16[4096,128]{1,0:T(8,128)(2,1)S(1)}, bf16[4096,128]{1,0:T(8,128)(2,1)}, u32[]{:S(2)}, u32[]{:S(2)}) collective-permute-start(bf16[4096,128]{1,0:T(8,128)(2,1)S(1)} %get-tuple-element.18.refs_3_), channel_id=1, source_target_pairs={{0,1},{1,0},{2,3},{3,2},{4,5},{5,4},{6,7},{7,6},{8,9},{9,8},{10,11... | collective-permute-start | bytes 3145736 | tf_op jit(solution)/shard_map/ppermute | solution.py:411
  43.7 5.2 %collective-permute-start.5 = (bf16[4096,128]{1,0:T(8,128)(2,1)S(1)}, bf16[4096,128]{1,0:T(8,128)(2,1)S(1)}, u32[]{:S(2)}, u32[]{:S(2)}) collective-permute-start(bf16[4096,128]{1,0:T(8,128)(2,1)S(1)} %get-tuple-element.20.refs_5_), channel_id=1, source_target_pairs={{0,1},{1,0},{2,3},{3,2},{4,5},{5,4},{6,7},{7,6},{8,9},{9,8},{10,11... | collective-permute-start | bytes 3145736 | tf_op jit(solution)/shard_map/ppermute | solution.py:411
  48.9 36.1 %copy-start.2 = (bf16[4096,128]{1,0:T(8,128)(2,1)}, bf16[4096,128]{1,0:T(8,128)(2,1)S(1)}, u32[]{:S(2)}) copy-start(bf16[4096,128]{1,0:T(8,128)(2,1)S(1)} %collective-permute-done.5.refs_0_.refs_6_) | copy-start | bytes 3145732
  48.9 0.8 copy-start.6
  49.6 0.6 copy-start.7
  50.3 12.1 %collective-permute-start.6 = (bf16[64,256]{1,0:T(8,128)(2,1)}, bf16[64,256]{1,0:T(8,128)(2,1)S(1)}, u32[]{:S(2)}, u32[]{:S(2)}) collective-permute-start(bf16[64,256]{1,0:T(8,128)(2,1)} %copy-done.7), channel_id=1, source_target_pairs={{0,96},{32,64},{1,97},{33,65},{2,98},{34,66},{3,99},{35,67},{4,100... | collective-permute-start | bytes 98312 | tf_op jit(solution)/shard_map/ppermute | solution.py:414
  58.5 17.5 %collective-permute-start.7 = (bf16[2048,128]{1,0:T(8,128)(2,1)}, bf16[2048,128]{1,0:T(8,128)(2,1)S(1)}, u32[]{:S(2)}, u32[]{:S(2)}) collective-permute-start(bf16[2048,128]{1,0:T(8,128)(2,1)} %slice.10), channel_id=1, source_target_pairs={{0,32},{32,0},{64,96},{1,33},{33,1},{65,97},{2,34},{34,2},{66,98},... | collective-permute-start | bytes 1572872 | tf_op jit(solution)/shard_map/ppermute | solution.py:414
  60.4 17.7 %collective-permute-start.8 = (bf16[2048,128]{1,0:T(8,128)(2,1)}, bf16[2048,128]{1,0:T(8,128)(2,1)S(1)}, u32[]{:S(2)}, u32[]{:S(2)}) collective-permute-start(bf16[2048,128]{1,0:T(8,128)(2,1)} %slice.11), channel_id=1, source_target_pairs={{0,96},{96,0},{64,32},{1,97},{97,1},{65,33},{2,98},{98,2},{66,34},... | collective-permute-start | bytes 1572872 | tf_op jit(solution)/shard_map/ppermute | solution.py:414
  64.0 18.2 %all-to-all-start.1 = ((bf16[16,64,256]{2,1,0:T(8,128)(2,1)}), bf16[16,64,256]{2,1,0:T(8,128)(2,1)}, u32[]{:S(2)}, u32[]{:S(2)}) async-start(bf16[16,64,256]{2,1,0:T(8,128)(2,1)} %broadcast_in_dim.7), calls=%async_computation.1 | async-start | bytes 1048576 | tf_op jit(solution)/shard_map/all_to_all | solution.py:431
  82.2 2.8 %copy-start.4 = (bf16[2048,128]{1,0:T(8,128)(2,1)}, bf16[2048,128]{1,0:T(8,128)(2,1)S(1)}, u32[]{:S(2)}) copy-start(bf16[2048,128]{1,0:T(8,128)(2,1)S(1)} %get-tuple-element.22.refs_7_) | copy-start | bytes 1572868
  82.2 2.8 %copy-start.5 = (bf16[2048,128]{1,0:T(8,128)(2,1)}, bf16[2048,128]{1,0:T(8,128)(2,1)S(1)}, u32[]{:S(2)}) copy-start(bf16[2048,128]{1,0:T(8,128)(2,1)S(1)} %get-tuple-element.23.refs_8_) | copy-start | bytes 1572868
  82.2 1.9 %collective-permute-start.10 = (bf16[2048,128]{1,0:T(8,128)(2,1)S(1)}, bf16[2048,128]{1,0:T(8,128)(2,1)S(1)}, u32[]{:S(2)}, u32[]{:S(2)}) collective-permute-start(bf16[2048,128]{1,0:T(8,128)(2,1)S(1)} %get-tuple-element.23.refs_8_), channel_id=1, source_target_pairs={{0,1},{1,0},{2,3},{3,2},{4,5},{5,4},{6,7},{7,6},{8,9},{9,8},{10,11... | collective-permute-start | bytes 1572872 | tf_op jit(solution)/shard_map/ppermute | solution.py:411
  82.2 2.8 %collective-permute-start.9 = (bf16[2048,128]{1,0:T(8,128)(2,1)S(1)}, bf16[2048,128]{1,0:T(8,128)(2,1)}, u32[]{:S(2)}, u32[]{:S(2)}) collective-permute-start(bf16[2048,128]{1,0:T(8,128)(2,1)S(1)} %get-tuple-element.22.refs_7_), channel_id=1, source_target_pairs={{0,1},{1,0},{2,3},{3,2},{4,5},{5,4},{6,7},{7,6},{8,9},{9,8},{10,11... | collective-permute-start | bytes 1572872 | tf_op jit(solution)/shard_map/ppermute | solution.py:411
  84.1 0.8 copy-start.8
  113.6 16.4 %all-to-all-start.3 = ((bf16[16,64,256]{2,1,0:T(8,128)(2,1)}), bf16[16,64,256]{2,1,0:T(8,128)(2,1)S(1)}, u32[]{:S(2)}, u32[]{:S(2)}) async-start(bf16[16,64,256]{2,1,0:T(8,128)(2,1)} %section.6), calls=%async_computation.3 | async-start | bytes 1048576 | tf_op jit(solution)/shard_map/all_to_all | solution.py:431
  119.5 4.2 %collective-permute-start.11 = (bf16[128,1024]{1,0:T(8,128)(2,1)S(1)}, bf16[128,1024]{1,0:T(8,128)(2,1)S(1)}, u32[]{:S(2)}, u32[]{:S(2)}) collective-permute-start(bf16[128,1024]{1,0:T(8,128)(2,1)S(1)} %copy-done.10), channel_id=1, source_target_pairs={{0,1},{1,0},{2,3},{3,2},{4,5},{5,4},{6,7},{7,6},{8,9},{9,8},{10,11... | collective-permute-start | bytes 786440 | tf_op jit(solution)/shard_map/ppermute | solution.py:411
  123.7 6.4 %copy-start.11 = (bf16[128,1024]{1,0:T(8,128)(2,1)}, bf16[128,1024]{1,0:T(8,128)(2,1)S(1)}, u32[]{:S(2)}) copy-start(bf16[128,1024]{1,0:T(8,128)(2,1)S(1)} %collective-permute-done.11.refs_12_) | copy-start | bytes 786436
  130.1 0.8 copy-start.9
  134.3 13.7 %all-to-all-start.4 = ((f32[16,4,1024]{2,1,0:T(4,128)}), f32[16,4,1024]{2,1,0:T(4,128)S(1)}, u32[]{:S(2)}, u32[]{:S(2)}) async-start(f32[16,4,1024]{2,1,0:T(4,128)} %section.7.gate_ref), calls=%async_computation.4 | async-start | bytes 524288 | tf_op jit(solution)/shard_map/all_to_all | solution.py:431
  148.0 0.7 copy-start.12
Sparse Core Ops, SparseCore 0:
  10.4 112.1 all-gather.1

commit v5 on v4

--- a/solution.py
+++ b/solution.py
@@ -316,7 +316,7 @@
             send.wait()
 
 
-def section_step(step, x, weights, proj=()):
+def section_step(step, x, weights, gate=None, proj=()):
     blocks, rows, cols = x.shape
     vm = pl.BlockSpec(memory_space=pltpu.VMEM)
     hbm = pl.BlockSpec(memory_space=pl.ANY)
@@ -328,60 +328,75 @@
         width = proj[0].shape[1]
         out = jax.ShapeDtypeStruct((blocks, rows // blocks, width), F32)
         scratch += [pltpu.VMEM((cols, width), BF), pltpu.SemaphoreType.DMA((2,))]
-    return pl.pallas_call(
-        lambda *refs: section_kernel(step, len(proj) > 0, *refs),
+    gates = [] if gate is None else [gate]
+    return pl.pallas_call(
+        lambda *refs: section_kernel(step, len(proj) > 0, *refs[len(gates):]),
         out_shape=out,
-        in_specs=[hbm] * (1 + len(weights) + len(proj)),
+        in_specs=[hbm] * (1 + len(gates) + len(weights) + len(proj)),
         out_specs=[vm, vm] if step == 0 else vm if proj else hbm,
         scratch_shapes=scratch,
         compiler_params=pltpu.CompilerParams(vmem_limit_bytes=VMEM_BYTES),
         cost_estimate=pl.CostEstimate(flops=1, bytes_accessed=1, transcendentals=0),
         name="section",
-    )(x, *weights, *proj)
+    )(*gates, x, *weights, *proj)
 
 
 def prepare_kernel(*refs):
-    sources, outs, scratch = refs[:6], refs[6:8], refs[8:]
-    held, (pack_ref, sems, out_sem) = scratch[:6], scratch[6:]
-    loads = [pltpu.make_async_copy(source, to, sems.at[i]) for i, (source, to) in enumerate(zip(sources, held))]
-    for load in loads:
+    sources, (bars_in, pack_out, w_out, mine_out, theirs_out), scratch = refs[:6], refs[6:11], refs[11:]
+    held, (bars_ref, pack_ref, sems, out_sem) = scratch[:6], scratch[6:]
+    a_ref, o_ref, u_ref, d_ref, w_ref, gain_ref = held
+    y, core = lax.axis_index("y"), lax.axis_index("c")
+    small = fetched(sources[:4] + sources[5:], held[:4] + held[5:], sems)
+    rows = [pltpu.make_async_copy(bars_in.at[m], bars_ref.at[i], sems.at[5 + i])
+            for i, m in enumerate((jnp.minimum(y, 3 - y), jnp.maximum(y, 3 - y)))]
+    depth = w_ref.shape[0]
+    spans = [pl.ds(i * depth // 4, depth // 4) for i in range(4)]
+    loads = [pltpu.make_async_copy(sources[4].at[span], w_ref.at[span], sems.at[7 + i]) for i, span in enumerate(spans)]
+    for load in rows + loads:
         load.start()
-    a_ref, o_ref, u_ref, d_ref, w_ref, gain_ref = held
+    for load in small + rows:
+        load.wait()
     width = o_ref.shape[1]
-    for load in loads[:4]:
-        load.wait()
     for i in range(3):
         pack_ref[i] = a_ref[:, i * width:(i + 1) * width]
     pack_ref[3] = o_ref[...]
     for i in range(4):
         pack_ref[4 + i] = u_ref[:, i * width:(i + 1) * width]
         pack_ref[8 + i] = d_ref[8 * i:8 * i + 8]
-    store = pltpu.make_async_copy(pack_ref, outs[0], out_sem)
+    store = pltpu.make_async_copy(pack_ref, pack_out, out_sem)
     store.start()
-    loads[4].wait()
-    loads[5].wait()
+    count = bars_ref.shape[1] // 2
+    to = lax.broadcasted_iota(jnp.int32, (count, 2 * count), 0)
+    source = lax.broadcasted_iota(jnp.int32, (count, 2 * count), 1)
+    for out_ref, at in ((mine_out, core), (theirs_out, 1 - core)):
+        pick = (source == to // 4 * 8 + 4 * at + to % 4).astype(F32).astype(BF)
+        for i in range(2):
+            out_ref[i * count:(i + 1) * count] = jnp.dot(pick, bars_ref[i], preferred_element_type=F32).astype(BF)
     for i in range(gain_ref.shape[0]):
+        if i % 8 == 0:
+            loads[i // 8].wait()
         span = slice(i * 128, (i + 1) * 128)
         column = jnp.transpose(jnp.broadcast_to(gain_ref[i:i + 1, :], (128, 128)))
-        outs[1][span, :] = (w_ref[span, :].astype(F32) * column).astype(BF)
+        w_out[span, :] = (w_ref[span, :].astype(F32) * column).astype(BF)
     store.wait()
 
 
-def prepare(*sources):
-    depth, cols = sources[4].shape
+def prepare(bars, *sources):
     width = sources[1].shape[1]
     hbm = pl.BlockSpec(memory_space=pl.ANY)
     vm = pl.BlockSpec(memory_space=pltpu.VMEM)
+    rows = jax.ShapeDtypeStruct(bars.shape[1:], BF)
     return pl.pallas_call(
         prepare_kernel,
-        out_shape=[jax.ShapeDtypeStruct((12, 8, width), BF), jax.ShapeDtypeStruct((depth, cols), BF)],
-        in_specs=[hbm] * 6,
-        out_specs=[hbm, vm],
+        out_shape=[jax.ShapeDtypeStruct((12, 8, width), BF), jax.ShapeDtypeStruct(sources[4].shape, BF), rows, rows],
+        in_specs=[hbm] * 7,
+        out_specs=[hbm, vm, vm, vm],
         scratch_shapes=[pltpu.VMEM(v.shape, v.dtype) for v in sources]
-        + [pltpu.VMEM((12, 8, width), BF), pltpu.SemaphoreType.DMA((6,)), pltpu.SemaphoreType.DMA],
+        + [pltpu.VMEM((2,) + bars.shape[1:], BF), pltpu.VMEM((12, 8, width), BF),
+           pltpu.SemaphoreType.DMA((11,)), pltpu.SemaphoreType.DMA],
         compiler_params=pltpu.CompilerParams(vmem_limit_bytes=VMEM_BYTES),
         name="prepare",
-    )(*sources)
+    )(*sources, bars)
 
 
 def after_kernel(*refs):
@@ -416,16 +431,10 @@
     def ordered(mine, theirs, axis):
         return jnp.where(core == 0, jnp.concatenate([mine, theirs], axis), jnp.concatenate([theirs, mine], axis))
 
-    feats = bar_in.shape[2]
-    pack, weight = prepare(
-        attn_in, attn_out, ffn_in, ffn_out, section_weight[0], section_gain.reshape(-1, 128))
+    pack, weight, mine, theirs = prepare(
+        bar_in, attn_in, attn_out, ffn_in, ffn_out, section_weight[0], section_gain.reshape(-1, 128))
     pack = lax.all_gather(pack.reshape(96, width), GROUP, axis=0, tiled=True).reshape(128, 12, 8, width)
-
-    pair = jnp.stack([jnp.minimum(y, 3 - y), jnp.maximum(y, 3 - y)])
-    by_core = jnp.concatenate([lax.dynamic_slice_in_dim(bar_in, pair[i], 1, 0) for i in range(2)])
-    by_core = by_core.reshape(2, 16, 2, 4, feats).transpose(2, 0, 1, 3, 4).reshape(2, 128, feats)
-    mine = lax.dynamic_index_in_dim(by_core, core, 0, keepdims=False)
-    theirs = swap(lax.dynamic_index_in_dim(by_core, 1 - core, 0, keepdims=False))
+    theirs = swap(theirs)
 
     def spread(v):
         return lax.all_to_all(v, ("x", "z"), 0, 0, tiled=True)
@@ -439,15 +448,15 @@
     half = near.shape[0] // 2
     farther = [across(far[:half], (0, 1), (1, 0), (2, 3)), across(near[half:], (0, 3), (3, 0), (2, 1))]
     far_other = swap(far)
-    here, there = section_step(0, x, weights)
-    there = across(after([far_other], [there])[0], (0, 3), (1, 2))
+    here, there = section_step(0, x, weights, far_other)
+    there = across(there, (0, 3), (1, 2))
     x = spread(copies(jnp.where(y < 2, here, there)))
     farther = after([x], farther)
     weights += [far, far_other, *farther, *[swap(w) for w in farther]]
     normed = embed_chars(shifted(char_ids[0]), char_embed, char_pos, norm_gain)
     x = spread(section_step(1, x, weights))
     x = spread(section_step(2, x, weights))
-    out = section_step(3, x, weights, [projection, swap(projection)])
+    out = section_step(3, x, weights, proj=[projection, swap(projection)])
     early = early_decode(out, normed, pack)
     parts = spread(out)
     return late_decode(parts, early, char_ids[0], shifted(char_ids[0]), lengths[0][:, None], char_embed, char_pos, norm_gain, pack)[None]

time: 177 us -> 176 us (level)
  waiting for transfers between devices: 41.8 us -> 45.9 us
  local copies, waits for them, and re-layouts: 11.3 us -> 8.16 us
  blocking collectives: 22.2 us -> 20.1 us
    ppermute x7, waiting for transfers between devices: 3.53 us -> 5.9 us  [swap(): return lax.ppermute(v, 'c', [(0, 1), (1, 0)])]
    all_to_all x1, blocking collectives: 22.2 us -> 20.1 us  [spread(): return lax.all_to_all(v, ('x', 'z'), 0, 0, tiled=True)]
    unnamed x30 -> x28, local copies, waits for them, and re-layouts: 4.45 us -> 3.07 us
where the time goes in v5:
time: 176 us; the launch traced here: 174 us
  Pallas kernels  48.7 us (28%)
  waiting for transfers between devices  45.9 us (26%)
  starting transfers between devices  36.1 us (21%)
  blocking collectives  20.1 us (11%)
  between operations  13.7 us (8%)
  local copies, waits for them, and re-layouts  8.16 us (5%)
    all_to_all x4, waiting for transfers between devices, spread(): return lax.all_to_all(v, ('x', 'z'), 0, 0, tiled=True)  30.9 us
    all_to_all x4, starting transfers between devices, spread(): return lax.all_to_all(v, ('x', 'z'), 0, 0, tiled=True)  22.2 us
    all_to_all x1, blocking collectives, spread(): return lax.all_to_all(v, ('x', 'z'), 0, 0, tiled=True)  20.1 us
    pallas_call x1, Pallas kernels, late_decode(): pl.pallas_call(late_kernel, out_shape=jax.ShapeDtypeStruct((bars, chars),...  20 us
    pallas_call x4, Pallas kernels, section_step(): pl.pallas_call(lambda *refs: section_kernel(step, len(proj) > 0, *refs[le...  12.8 us
    ppermute x5, starting transfers between devices, across(): return lax.ppermute(v, 'y', pairs)  12.5 us
    pallas_call x1, Pallas kernels, early_decode(): pl.pallas_call(early_kernel, out_shape=[jax.ShapeDtypeStruct((tokens, w),...  10.1 us
    ppermute x5, waiting for transfers between devices, across(): return lax.ppermute(v, 'y', pairs)  9.12 us
  transfers between devices with their start and end apart: 17, of which 8 were waited for; matrix products, arithmetic and copies ran while one was open for 4% of the time, Pallas kernels for 15%

profile of v5, /device:TPU:0, one launch (start us, length us, event | category | flops | bytes accessed | tf_op | source)
XLA Modules:
  0.0 174.3 jit_solution(14120951746192071619)
XLA Ops:
  6.5 3.1 %prepare.1 = (bf16[12,8,1024]{2,1,0:T(8,128)(2,1)}, bf16[4096,128]{1,0:T(8,128)(2,1)}, bf16[128,128]{1,0:T(8,128)(2,1)}, bf16[128,128]{1,0:T(8,128)(2,1)}) custom-call(bf16[8,3072]{1,0:T(8,128)(2,1)} %refs_0_.1, bf16[8,1024]{1,0:T(8,128)(2,1)} %refs_1_.1, bf16[8,4096]{1,0:T(8,128)(2,1)} %refs_2_.1, bf16[32,1024]{1,0:T(8,128)(2,1)} %refs_3_.1, ...), custom_call_target="tpu_custom_call" | custom-call | tf_op jit(solution)/shard_map/prepare/pallas_call | solution.py:389
  9.6 0.0 all-gather.2.cloned.1.call-update
  9.7 0.1 collective-permute-start
  9.7 1.7 collective-permute-start.1
  11.5 1.3 collective-permute-start.2
  12.8 0.9 maximum_select_fusion
  13.6 1.1 broadcast_in_dim.6
  14.7 7.9 %all-to-all-start = ((bf16[16,128,256]{2,1,0:T(8,128)(2,1)}), bf16[16,128,256]{2,1,0:T(8,128)(2,1)S(1)}, u32[]{:S(2)}, u32[]{:S(2)}) async-start(bf16[16,128,256]{2,1,0:T(8,128)(2,1)} %broadcast_in_dim.6), calls=%async_computation | async-start | bytes 2097152 | tf_op jit(solution)/shard_map/all_to_all | solution.py:440
  22.6 0.1 collective-permute-start.4
  22.7 20.0 %all-to-all-done.refs_0_.refs_1_ = bf16[16,128,256]{2,1,0:T(8,128)(2,1)S(1)} async-done(((bf16[16,128,256]{2,1,0:T(8,128)(2,1)}), bf16[16,128,256]{2,1,0:T(8,128)(2,1)S(1)}, u32[]{:S(2)}, u32[]{:S(2)}) %all-to-all-start) | async-done | bytes 1048608 | tf_op jit(solution)/shard_map/all_to_all | solution.py:440
  42.7 0.0 collective-permute-done.1.refs_1_
  42.7 0.0 collective-permute-done.2.refs_2_
  42.7 0.1 collective-permute-start.5
  42.8 0.5 collective-permute-start.3
  43.3 2.7 %collective-permute-done.5.refs_5_.refs_4_ = bf16[4096,128]{1,0:T(8,128)(2,1)S(1)} collective-permute-done((bf16[4096,128]{1,0:T(8,128)(2,1)S(1)}, bf16[4096,128]{1,0:T(8,128)(2,1)S(1)}, u32[]{:S(2)}, u32[]{:S(2)}) %collective-permute-start.5) | collective-permute-done | bytes 1048608 | tf_op jit(solution)/shard_map/ppermute | solution.py:426
  46.0 1.0 copy-done.6
  47.0 0.1 collective-permute-done.3.refs_0_.refs_6_
  47.1 3.1 %section.4 = (bf16[64,256]{1,0:T(8,128)(2,1)}, bf16[64,256]{1,0:T(8,128)(2,1)}) custom-call(bf16[4096,128]{1,0:T(8,128)(2,1)} %collective-permute-done.3.refs_0_.refs_6_, bf16[16,128,256]{2,1,0:T(8,128)(2,1)} %copy-done.2, bf16[4096,128]{1,0:T(8,128)(2,1)} %get-tuple-element.21.refs_2_.refs_1_, bf16[4096,128]{1,0:T(8,128)(2,1)} %collective-permute-done.4.refs_3_.refs_2_, ...), custom_call_target="tpu_custom_call" | custom-call | flops 1 | bytes 1 | tf_op jit(solution)/shard_map/section/pallas_call | solution.py:332
  50.2 5.6 %collective-permute-start.6 = (bf16[64,256]{1,0:T(8,128)(2,1)}, bf16[64,256]{1,0:T(8,128)(2,1)S(1)}, u32[]{:S(2)}, u32[]{:S(2)}) collective-permute-start(bf16[64,256]{1,0:T(8,128)(2,1)} %get-tuple-element.25), channel_id=1, source_target_pairs={{0,96},{32,64},{1,97},{33,65},{2,98},{34,66},{3,99},{35,67},{4,100... | collective-permute-start | bytes 98312 | tf_op jit(solution)/shard_map/ppermute | solution.py:429
  55.8 1.9 %slice.11 = bf16[2048,128]{1,0:T(8,128)(2,1)} slice(bf16[4096,128]{1,0:T(8,128)(2,1)} %copy-done), slice={[2048:4096], [0:128]} | slice | bytes 1048576 | tf_op jit(solution)/shard_map/slice | solution.py:449
  57.7 1.9 %collective-permute-start.8 = (bf16[2048,128]{1,0:T(8,128)(2,1)}, bf16[2048,128]{1,0:T(8,128)(2,1)S(1)}, u32[]{:S(2)}, u32[]{:S(2)}) collective-permute-start(bf16[2048,128]{1,0:T(8,128)(2,1)} %slice.11), channel_id=1, source_target_pairs={{0,96},{96,0},{64,32},{1,97},{97,1},{65,33},{2,98},{98,2},{66,34},... | collective-permute-start | bytes 1572872 | tf_op jit(solution)/shard_map/ppermute | solution.py:429
  59.7 1.9 %collective-permute-start.7 = (bf16[2048,128]{1,0:T(8,128)(2,1)S(1)}, bf16[2048,128]{1,0:T(8,128)(2,1)S(1)}, u32[]{:S(2)}, u32[]{:S(2)}) collective-permute-start(bf16[2048,128]{1,0:T(8,128)(2,1)S(1)} %slice.10), channel_id=1, source_target_pairs={{0,32},{32,0},{64,96},{1,33},{33,1},{65,97},{2,34},{34,2},{66,98},... | collective-permute-start | bytes 1572872 | tf_op jit(solution)/shard_map/ppermute | solution.py:429
  61.6 0.8 broadcast_select_fusion
  62.4 0.9 broadcast_in_dim.7
  63.2 4.5 %all-to-all-start.1 = ((bf16[16,64,256]{2,1,0:T(8,128)(2,1)}), bf16[16,64,256]{2,1,0:T(8,128)(2,1)S(1)}, u32[]{:S(2)}, u32[]{:S(2)}) async-start(bf16[16,64,256]{2,1,0:T(8,128)(2,1)} %broadcast_in_dim.7), calls=%async_computation.1 | async-start | bytes 1048576 | tf_op jit(solution)/shard_map/all_to_all | solution.py:440
  67.7 9.1 %collective-permute-done.8.refs_2_ = bf16[2048,128]{1,0:T(8,128)(2,1)S(1)} collective-permute-done((bf16[2048,128]{1,0:T(8,128)(2,1)}, bf16[2048,128]{1,0:T(8,128)(2,1)S(1)}, u32[]{:S(2)}, u32[]{:S(2)}) %collective-permute-start.8) | collective-permute-done | bytes 524320 | tf_op jit(solution)/shard_map/ppermute | solution.py:429
  76.9 2.1 %all-to-all-done.1.refs_0_ = bf16[16,64,256]{2,1,0:T(8,128)(2,1)S(1)} async-done(((bf16[16,64,256]{2,1,0:T(8,128)(2,1)}), bf16[16,64,256]{2,1,0:T(8,128)(2,1)S(1)}, u32[]{:S(2)}, u32[]{:S(2)}) %all-to-all-start.1) | async-done | bytes 524320 | tf_op jit(solution)/shard_map/all_to_all | solution.py:440
  79.0 0.1 collective-permute-start.10
  79.1 0.5 collective-permute-start.9
  79.6 2.9 %collective-permute-done.10.refs_10_ = bf16[2048,128]{1,0:T(8,128)(2,1)S(1)} collective-permute-done((bf16[2048,128]{1,0:T(8,128)(2,1)S(1)}, bf16[2048,128]{1,0:T(8,128)(2,1)S(1)}, u32[]{:S(2)}, u32[]{:S(2)}) %collective-permute-start.10) | collective-permute-done | bytes 524320 | tf_op jit(solution)/shard_map/ppermute | solution.py:426
  82.4 0.2 collective-permute-done.9.refs_9_
  82.7 0.6 copy-done.7
  83.2 3.2 %section.5 = bf16[16,64,256]{2,1,0:T(8,128)(2,1)} custom-call(bf16[16,64,256]{2,1,0:T(8,128)(2,1)} %copy-done.5, bf16[4096,128]{1,0:T(8,128)(2,1)} %get-tuple-element.21.refs_2_.refs_1_, bf16[4096,128]{1,0:T(8,128)(2,1)} %collective-permute-done.4.refs_3_.refs_2_, bf16[4096,128]{1,0:T(8,128)(2,1)} %copy-done, bf16[4096,128]{1,0:T(8,128)(2,1)} %copy-done.6, ...), custom_call_target="tpu_custom_call" | custom-call | flops 1 | bytes 1 | tf_op jit(solution)/shard_map/section/pallas_call | solution.py:332
  86.4 20.1 %all_to_all.25.refs_0_ = bf16[16,64,256]{2,1,0:T(8,128)(2,1)} all-to-all(bf16[16,64,256]{2,1,0:T(8,128)(2,1)} %section.5), channel_id=1, replica_groups=mesh['y'=4,'x'=4,'z'=4,'c'=2] {'x','z'}, dimensions={0} | all-to-all | bytes 1048576 | tf_op jit(solution)/shard_map/all_to_all | solution.py:440
  106.5 3.2 %section.6 = bf16[16,64,256]{2,1,0:T(8,128)(2,1)} custom-call(bf16[16,64,256]{2,1,0:T(8,128)(2,1)} %all_to_all.25.refs_0_, bf16[4096,128]{1,0:T(8,128)(2,1)} %get-tuple-element.21.refs_2_.refs_1_, bf16[4096,128]{1,0:T(8,128)(2,1)} %collective-permute-done.4.refs_3_.refs_2_, bf16[4096,128]{1,0:T(8,128)(2,1)} %copy-done, bf16[4096,128]{1,0:T(8,128)(2,1)} %copy-done.6, ...), custom_call_target="tpu_custom_call" | custom-call | flops 1 | bytes 1 | tf_op jit(solution)/shard_map/section/pallas_call | solution.py:332
  109.7 6.2 %all-to-all-start.3 = ((bf16[16,64,256]{2,1,0:T(8,128)(2,1)}), bf16[16,64,256]{2,1,0:T(8,128)(2,1)S(1)}, u32[]{:S(2)}, u32[]{:S(2)}) async-start(bf16[16,64,256]{2,1,0:T(8,128)(2,1)} %section.6), calls=%async_computation.3 | async-start | bytes 1048576 | tf_op jit(solution)/shard_map/all_to_all | solution.py:440
  115.9 0.1 collective-permute-start.11
  116.0 0.6 copy.18.refs_3_
  116.6 0.6 concatenate.20.prev_ref.refs_2_
  117.3 2.7 %embed.1.n_in = bf16[512,1024]{1,0:T(8,128)(2,1)} custom-call(s32[4,128]{1,0:T(4,128)} %concatenate.20.prev_ref.refs_2_, bf16[128,1024]{1,0:T(8,128)(2,1)} %refs_4_.1, bf16[128,1024]{1,0:T(8,128)(2,1)} %refs_5_.1, f32[3,1024]{1,0:T(4,128)} %refs_6_.3), custom_call_target="tpu_custom_call" | custom-call | tf_op jit(solution)/shard_map/embed/pallas_call | solution.py:41
  120.0 8.7 %all-to-all-done.3.refs_0_ = bf16[16,64,256]{2,1,0:T(8,128)(2,1)S(1)} async-done(((bf16[16,64,256]{2,1,0:T(8,128)(2,1)}), bf16[16,64,256]{2,1,0:T(8,128)(2,1)S(1)}, u32[]{:S(2)}, u32[]{:S(2)}) %all-to-all-start.3) | async-done | bytes 524320 | tf_op jit(solution)/shard_map/all_to_all | solution.py:440
  128.7 0.8 copy-done.8
  129.5 3.4 %section.7.gate_ref = f32[16,4,1024]{2,1,0:T(4,128)} custom-call(bf16[16,64,256]{2,1,0:T(8,128)(2,1)} %copy-done.8, bf16[4096,128]{1,0:T(8,128)(2,1)} %get-tuple-element.21.refs_2_.refs_1_, bf16[4096,128]{1,0:T(8,128)(2,1)} %collective-permute-done.4.refs_3_.refs_2_, bf16[4096,128]{1,0:T(8,128)(2,1)} %copy-done, bf16[4096,128]{1,0:T(8,128)(2,1)} %copy-done.6, ...), custom_call_target="tpu_custom_call" | custom-call | flops 1 | bytes 1 | tf_op jit(solution)/shard_map/section/pallas_call | solution.py:332
  133.0 3.6 %all-to-all-start.4 = ((f32[16,4,1024]{2,1,0:T(4,128)}), f32[16,4,1024]{2,1,0:T(4,128)S(1)}, u32[]{:S(2)}, u32[]{:S(2)}) async-start(f32[16,4,1024]{2,1,0:T(4,128)} %section.7.gate_ref), calls=%async_computation.4 | async-start | bytes 524288 | tf_op jit(solution)/shard_map/all_to_all | solution.py:440
  136.6 0.0 all-gather.2.cloned.1.call-done
  136.6 10.1 %early.1 = (bf16[512,1024]{1,0:T(8,128)(2,1)}, f32[512,1024]{1,0:T(8,128)}, f32[512,128]{1,0:T(8,128)}, f32[512,128]{1,0:T(8,128)}) custom-call(f32[16,4,1024]{2,1,0:T(4,128)} %section.7.gate_ref, bf16[512,1024]{1,0:T(8,128)(2,1)} %embed.1.n_in, bf16[128,12,8,1024]{3,2,1,0:T(8,128)(2,1)} %bitcast.14), custom_call_target="tpu_custom_call" | custom-call | flops 8589934592 | bytes 16777216 | tf_op jit(solution)/shard_map/early/pallas_call | solution.py:121
  146.8 0.7 copy-done.11
  147.5 20.0 %late.1 = f32[4,128]{1,0:T(4,128)} custom-call(f32[16,4,1024]{2,1,0:T(4,128)} %copy-done.11, s32[4,128]{1,0:T(4,128)} %bitcast.11, s32[4,128]{1,0:T(4,128)} %concatenate.20.prev_ref.refs_2_, s32[4,1]{1,0:T(4,128)} %copy.18.refs_3_, bf16[128,1024]{1,0:T(8,128)(2,1)} %refs_4_.1, bf16[128,1024]{1,0:T(8,128)(2,1)} %refs_5_.1, f32[3,1024]{1,0:T(4,128)} %refs_6_.3, ...), custom_call_target="tpu_custom_call" | custom-call | flops 10737418240 | bytes 25165824 | tf_op jit(solution)/shard_map/late/pallas_call | solution.py:227
  (34 shorter events, 0.1 us)
Async XLA Ops:
  6.5 109.3 %copy-start.9 = (bf16[128,1024]{1,0:T(8,128)(2,1)S(1)}, bf16[128,1024]{1,0:T(8,128)(2,1)}, u32[]{:S(2)}) copy-start(bf16[128,1024]{1,0:T(8,128)(2,1)} %refs_11_.1) | copy-start | bytes 786436
  6.5 109.5 %copy-start.13 = (s32[1,4]{1,0:T(1,128)S(1)}, s32[1,4]{1,0:T(1,128)}, u32[]{:S(2)}) copy-start(s32[1,4]{1,0:T(1,128)} %param.18) | copy-start | bytes 52
  6.5 110.1 %copy-start.12 = (s32[1,4,128]{2,1,0:T(4,128)S(1)}, s32[1,4,128]{2,1,0:T(4,128)}, u32[]{:S(2)}) copy-start(s32[1,4,128]{2,1,0:T(4,128)} %param.17) | copy-start | bytes 6148
  6.5 130.1 %all-gather.2.cloned.1.call-start = ((), (), s32[]{:S(2)}) async-start(), calls=%async_computation.5 | async-start | bytes 25362432 | tf_op jit(solution)/shard_map/all_gather | solution.py:436
  9.7 3.1 %collective-permute-start = (bf16[128,128]{1,0:T(8,128)(2,1)}, bf16[128,128]{1,0:T(8,128)(2,1)S(1)}, u32[]{:S(2)}, u32[]{:S(2)}) collective-permute-start(bf16[128,128]{1,0:T(8,128)(2,1)} %get-tuple-element.20), channel_id=1, source_target_pairs={{0,1},{1,0},{2,3},{3,2},{4,5},{5,4},{6,7},{7,6},{8,9},{9,8},{10,11... | collective-permute-start | bytes 98312 | tf_op jit(solution)/shard_map/ppermute | solution.py:426
  9.7 32.9 %collective-permute-start.1 = (bf16[4096,128]{1,0:T(8,128)(2,1)}, bf16[4096,128]{1,0:T(8,128)(2,1)S(1)}, u32[]{:S(2)}, u32[]{:S(2)}) collective-permute-start(bf16[4096,128]{1,0:T(8,128)(2,1)} %get-tuple-element.21.refs_2_.refs_1_), channel_id=1, source_target_pairs={{0,32},{32,0},{64,96},{96,64},{1,33},{33,1},{65,97},{97,65},{2,34}... | collective-permute-start | bytes 3145736 | tf_op jit(solution)/shard_map/ppermute | solution.py:429
  11.5 31.2 %collective-permute-start.2 = (bf16[4096,128]{1,0:T(8,128)(2,1)}, bf16[4096,128]{1,0:T(8,128)(2,1)S(1)}, u32[]{:S(2)}, u32[]{:S(2)}) collective-permute-start(bf16[4096,128]{1,0:T(8,128)(2,1)} %get-tuple-element.21.refs_2_.refs_1_), channel_id=1, source_target_pairs={{32,64},{64,32},{96,0},{33,65},{65,33},{97,1},{34,66},{66,34},{98,... | collective-permute-start | bytes 3145736 | tf_op jit(solution)/shard_map/ppermute | solution.py:429
  14.7 28.0 %all-to-all-start = ((bf16[16,128,256]{2,1,0:T(8,128)(2,1)}), bf16[16,128,256]{2,1,0:T(8,128)(2,1)S(1)}, u32[]{:S(2)}, u32[]{:S(2)}) async-start(bf16[16,128,256]{2,1,0:T(8,128)(2,1)} %broadcast_in_dim.6), calls=%async_computation | async-start | bytes 2097152 | tf_op jit(solution)/shard_map/all_to_all | solution.py:440
  22.6 20.7 %collective-permute-start.4 = (bf16[4096,128]{1,0:T(8,128)(2,1)}, bf16[4096,128]{1,0:T(8,128)(2,1)}, u32[]{:S(2)}, u32[]{:S(2)}) collective-permute-start(bf16[4096,128]{1,0:T(8,128)(2,1)} %get-tuple-element.21.refs_2_.refs_1_), channel_id=1, source_target_pairs={{0,1},{1,0},{2,3},{3,2},{4,5},{5,4},{6,7},{7,6},{8,9},{9,8},{10,11... | collective-permute-start | bytes 3145736 | tf_op jit(solution)/shard_map/ppermute | solution.py:426
  42.7 4.4 %copy-start.2 = (bf16[16,128,256]{2,1,0:T(8,128)(2,1)}, bf16[16,128,256]{2,1,0:T(8,128)(2,1)S(1)}, u32[]{:S(2)}) copy-start(bf16[16,128,256]{2,1,0:T(8,128)(2,1)S(1)} %all-to-all-done.refs_0_.refs_1_) | copy-start | bytes 3145732
  42.7 4.4 %copy-start = (bf16[4096,128]{1,0:T(8,128)(2,1)}, bf16[4096,128]{1,0:T(8,128)(2,1)S(1)}, u32[]{:S(2)}) copy-start(bf16[4096,128]{1,0:T(8,128)(2,1)S(1)} %get-tuple-element.23.refs_4_.refs_3_) | copy-start | bytes 3145732
  42.7 39.9 %copy-start.1 = (bf16[4096,128]{1,0:T(8,128)(2,1)}, bf16[4096,128]{1,0:T(8,128)(2,1)S(1)}, u32[]{:S(2)}) copy-start(bf16[4096,128]{1,0:T(8,128)(2,1)S(1)} %get-tuple-element.22.refs_5_) | copy-start | bytes 3145732
  42.7 3.3 %collective-permute-start.5 = (bf16[4096,128]{1,0:T(8,128)(2,1)S(1)}, bf16[4096,128]{1,0:T(8,128)(2,1)S(1)}, u32[]{:S(2)}, u32[]{:S(2)}) collective-permute-start(bf16[4096,128]{1,0:T(8,128)(2,1)S(1)} %get-tuple-element.23.refs_4_.refs_3_), channel_id=1, source_target_pairs={{0,1},{1,0},{2,3},{3,2},{4,5},{5,4},{6,7},{7,6},{8,9},{9,8},{10,11... | collective-permute-start | bytes 3145736 | tf_op jit(solution)/shard_map/ppermute | solution.py:426
  42.8 4.3 %collective-permute-start.3 = (bf16[4096,128]{1,0:T(8,128)(2,1)S(1)}, bf16[4096,128]{1,0:T(8,128)(2,1)}, u32[]{:S(2)}, u32[]{:S(2)}) collective-permute-start(bf16[4096,128]{1,0:T(8,128)(2,1)S(1)} %get-tuple-element.22.refs_5_), channel_id=1, source_target_pairs={{0,1},{1,0},{2,3},{3,2},{4,5},{5,4},{6,7},{7,6},{8,9},{9,8},{10,11... | collective-permute-start | bytes 3145736 | tf_op jit(solution)/shard_map/ppermute | solution.py:426
  46.0 1.0 copy-start.6
  50.2 11.4 %collective-permute-start.6 = (bf16[64,256]{1,0:T(8,128)(2,1)}, bf16[64,256]{1,0:T(8,128)(2,1)S(1)}, u32[]{:S(2)}, u32[]{:S(2)}) collective-permute-start(bf16[64,256]{1,0:T(8,128)(2,1)} %get-tuple-element.25), channel_id=1, source_target_pairs={{0,96},{32,64},{1,97},{33,65},{2,98},{34,66},{3,99},{35,67},{4,100... | collective-permute-start | bytes 98312 | tf_op jit(solution)/shard_map/ppermute | solution.py:429
  57.7 19.1 %collective-permute-start.8 = (bf16[2048,128]{1,0:T(8,128)(2,1)}, bf16[2048,128]{1,0:T(8,128)(2,1)S(1)}, u32[]{:S(2)}, u32[]{:S(2)}) collective-permute-start(bf16[2048,128]{1,0:T(8,128)(2,1)} %slice.11), channel_id=1, source_target_pairs={{0,96},{96,0},{64,32},{1,97},{97,1},{65,33},{2,98},{98,2},{66,34},... | collective-permute-start | bytes 1572872 | tf_op jit(solution)/shard_map/ppermute | solution.py:429
  59.7 17.2 %collective-permute-start.7 = (bf16[2048,128]{1,0:T(8,128)(2,1)S(1)}, bf16[2048,128]{1,0:T(8,128)(2,1)S(1)}, u32[]{:S(2)}, u32[]{:S(2)}) collective-permute-start(bf16[2048,128]{1,0:T(8,128)(2,1)S(1)} %slice.10), channel_id=1, source_target_pairs={{0,32},{32,0},{64,96},{1,33},{33,1},{65,97},{2,34},{34,2},{66,98},... | collective-permute-start | bytes 1572872 | tf_op jit(solution)/shard_map/ppermute | solution.py:429
  63.2 15.7 %all-to-all-start.1 = ((bf16[16,64,256]{2,1,0:T(8,128)(2,1)}), bf16[16,64,256]{2,1,0:T(8,128)(2,1)S(1)}, u32[]{:S(2)}, u32[]{:S(2)}) async-start(bf16[16,64,256]{2,1,0:T(8,128)(2,1)} %broadcast_in_dim.7), calls=%async_computation.1 | async-start | bytes 1048576 | tf_op jit(solution)/shard_map/all_to_all | solution.py:440
  79.0 3.7 %copy-start.5 = (bf16[16,64,256]{2,1,0:T(8,128)(2,1)}, bf16[16,64,256]{2,1,0:T(8,128)(2,1)S(1)}, u32[]{:S(2)}) copy-start(bf16[16,64,256]{2,1,0:T(8,128)(2,1)S(1)} %all-to-all-done.1.refs_0_) | copy-start | bytes 1572868
  79.0 3.7 %copy-start.3 = (bf16[2048,128]{1,0:T(8,128)(2,1)}, bf16[2048,128]{1,0:T(8,128)(2,1)S(1)}, u32[]{:S(2)}) copy-start(bf16[2048,128]{1,0:T(8,128)(2,1)S(1)} %get-tuple-element.27.refs_8_) | copy-start | bytes 1572868
  79.0 3.7 %copy-start.4 = (bf16[2048,128]{1,0:T(8,128)(2,1)}, bf16[2048,128]{1,0:T(8,128)(2,1)S(1)}, u32[]{:S(2)}) copy-start(bf16[2048,128]{1,0:T(8,128)(2,1)S(1)} %get-tuple-element.26.refs_7_) | copy-start | bytes 1572868
  79.0 3.4 %collective-permute-start.10 = (bf16[2048,128]{1,0:T(8,128)(2,1)S(1)}, bf16[2048,128]{1,0:T(8,128)(2,1)S(1)}, u32[]{:S(2)}, u32[]{:S(2)}) collective-permute-start(bf16[2048,128]{1,0:T(8,128)(2,1)S(1)} %get-tuple-element.27.refs_8_), channel_id=1, source_target_pairs={{0,1},{1,0},{2,3},{3,2},{4,5},{5,4},{6,7},{7,6},{8,9},{9,8},{10,11... | collective-permute-start | bytes 1572872 | tf_op jit(solution)/shard_map/ppermute | solution.py:426
  79.1 3.6 %collective-permute-start.9 = (bf16[2048,128]{1,0:T(8,128)(2,1)S(1)}, bf16[2048,128]{1,0:T(8,128)(2,1)}, u32[]{:S(2)}, u32[]{:S(2)}) collective-permute-start(bf16[2048,128]{1,0:T(8,128)(2,1)S(1)} %get-tuple-element.26.refs_7_), channel_id=1, source_target_pairs={{0,1},{1,0},{2,3},{3,2},{4,5},{5,4},{6,7},{7,6},{8,9},{9,8},{10,11... | collective-permute-start | bytes 1572872 | tf_op jit(solution)/shard_map/ppermute | solution.py:426
  82.4 0.8 copy-start.7
  109.7 19.1 %all-to-all-start.3 = ((bf16[16,64,256]{2,1,0:T(8,128)(2,1)}), bf16[16,64,256]{2,1,0:T(8,128)(2,1)S(1)}, u32[]{:S(2)}, u32[]{:S(2)}) async-start(bf16[16,64,256]{2,1,0:T(8,128)(2,1)} %section.6), calls=%async_computation.3 | async-start | bytes 1048576 | tf_op jit(solution)/shard_map/all_to_all | solution.py:440
  115.9 4.1 %collective-permute-start.11 = (bf16[128,1024]{1,0:T(8,128)(2,1)S(1)}, bf16[128,1024]{1,0:T(8,128)(2,1)S(1)}, u32[]{:S(2)}, u32[]{:S(2)}) collective-permute-start(bf16[128,1024]{1,0:T(8,128)(2,1)S(1)} %copy-done.9), channel_id=1, source_target_pairs={{0,1},{1,0},{2,3},{3,2},{4,5},{5,4},{6,7},{7,6},{8,9},{9,8},{10,11... | collective-permute-start | bytes 786440 | tf_op jit(solution)/shard_map/ppermute | solution.py:426
  120.0 8.7 %copy-start.10 = (bf16[128,1024]{1,0:T(8,128)(2,1)}, bf16[128,1024]{1,0:T(8,128)(2,1)S(1)}, u32[]{:S(2)}) copy-start(bf16[128,1024]{1,0:T(8,128)(2,1)S(1)} %collective-permute-done.11.refs_12_) | copy-start | bytes 786436
  128.7 0.8 copy-start.8
  133.0 13.8 %all-to-all-start.4 = ((f32[16,4,1024]{2,1,0:T(4,128)}), f32[16,4,1024]{2,1,0:T(4,128)S(1)}, u32[]{:S(2)}, u32[]{:S(2)}) async-start(f32[16,4,1024]{2,1,0:T(4,128)} %section.7.gate_ref), calls=%async_computation.4 | async-start | bytes 524288 | tf_op jit(solution)/shard_map/all_to_all | solution.py:440
  146.8 0.7 copy-start.11
Sparse Core Ops, SparseCore 0:
  10.4 114.6 all-gather.1

commit v6 on v5

--- a/solution.py
+++ b/solution.py
@@ -69,7 +69,7 @@
             q_store.start()
 
     def stores(b):
-        rows = pl.ds(pl.multiple_of(b * chars, chars), chars)
+        rows = pl.ds(b * chars, chars)
         return [pltpu.make_async_copy(source.at[rows], to.at[rows], out_sems.at[3 * b + i])
                 for i, (source, to) in enumerate(((acc_ref, acc_out), (top_ref, top_out), (sum_ref, sum_out)))]
 
@@ -81,7 +81,7 @@
     column = lax.broadcasted_iota(jnp.int32, (2 * chars, 128), 1)
 
     def attend(b, carry):
-        rows = pl.ds(pl.multiple_of(b * chars, chars), chars)
+        rows = pl.ds(b * chars, chars)
         tops = jnp.full((chars, 128), -1e30, F32)
         sums = jnp.zeros((chars, 128), F32)
         for h in range(width // 128):
@@ -107,7 +107,8 @@
             store.start()
         return carry
 
-    lax.fori_loop(0, bars, attend, 0)
+    for b in range(bars):
+        attend(b, 0)
     q_store.wait()
     for b in range(bars):
         for store in stores(b):
@@ -203,9 +204,13 @@
             copies[8 + j].start()
         if j < 2:
             copies[5 + j].start()
-        mid_ref[...] = jax.nn.gelu(jnp.dot(n_ref[...], wup[j].reshape(width, width), preferred_element_type=F32)).astype(BF)
-        copies[7 + j].wait()
-        x_ref[...] += jnp.dot(mid_ref[...], wdn[32 * j:32 * j + 32].reshape(width, width), preferred_element_type=F32)
+        made = jnp.dot(n_ref[...], wup[j].reshape(width, width), preferred_element_type=F32)
+        mid_ref[:, j % 4 * width:(j % 4 + 1) * width] = jax.nn.gelu(made).astype(BF)
+        if j % 4 == 3:
+            for i in range(j - 3, j + 1):
+                copies[7 + i].wait()
+            rows = slice(32 * (j - 3), 32 * j + 32)
+            x_ref[...] += jnp.dot(mid_ref[...], wdn[rows].reshape(4 * width, width), preferred_element_type=F32)
     last = rms_rows(x_ref[...], gain_ref[2:3]).astype(BF)
     logits = lax.dot_general(embed_ref[...], last, (((1,), (1,)), ((), ())), preferred_element_type=F32)
     top = jnp.max(logits, axis=0, keepdims=True)
@@ -229,7 +234,7 @@
         out_shape=jax.ShapeDtypeStruct((bars, chars), F32),
         in_specs=[pl.BlockSpec(memory_space=pl.ANY)] * 12,
         out_specs=pl.BlockSpec(memory_space=pltpu.VMEM),
-        scratch_shapes=[pltpu.VMEM(v.shape, v.dtype) for v in sources] + [t(F32), t(BF), t(BF), t(BF),
+        scratch_shapes=[pltpu.VMEM(v.shape, v.dtype) for v in sources] + [t(F32), t(BF), t(BF), pltpu.VMEM((tokens, 4 * width), BF),
                         pltpu.VMEM((2, 128, 8, width), BF), pltpu.VMEM((128, 8, width), BF),
                         pltpu.VMEM((4, 128, 8, width), BF), pltpu.VMEM((128, 4, 8, width), BF),
                         pltpu.SemaphoreType.DMA((11,)), pltpu.SemaphoreType.DMA((11,))],

time: 176 us -> 174 us (0.989)
  transfers between devices with their start and end apart: 17 -> 17, of which waited for: 8 -> 8; matrix products, arithmetic and copies ran while one was open for 4% -> 4% of each run, Pallas kernels for 15% -> 14%
where the time goes in v6:
time: 174 us; the launch traced here: 173 us
  Pallas kernels  47.4 us (27%)
  waiting for transfers between devices  45.9 us (26%)
  starting transfers between devices  36.3 us (21%)
  blocking collectives  20.1 us (12%)
  between operations  13.7 us (8%)
  local copies, waits for them, and re-layouts  8.16 us (5%)
    all_to_all x4, waiting for transfers between devices, spread(): return lax.all_to_all(v, ('x', 'z'), 0, 0, tiled=True)  30.9 us
    all_to_all x4, starting transfers between devices, spread(): return lax.all_to_all(v, ('x', 'z'), 0, 0, tiled=True)  22.4 us
    all_to_all x1, blocking collectives, spread(): return lax.all_to_all(v, ('x', 'z'), 0, 0, tiled=True)  20.1 us
    pallas_call x1, Pallas kernels, late_decode(): pl.pallas_call(late_kernel, out_shape=jax.ShapeDtypeStruct((bars, chars),...  19.7 us
    pallas_call x4, Pallas kernels, section_step(): pl.pallas_call(lambda *refs: section_kernel(step, len(proj) > 0, *refs[le...  12.8 us
    ppermute x5, starting transfers between devices, across(): return lax.ppermute(v, 'y', pairs)  12.5 us
    ppermute x5, waiting for transfers between devices, across(): return lax.ppermute(v, 'y', pairs)  9.12 us
    pallas_call x1, Pallas kernels, early_decode(): pl.pallas_call(early_kernel, out_shape=[jax.ShapeDtypeStruct((tokens, w),...  9.09 us
  transfers between devices with their start and end apart: 17, of which 8 were waited for; matrix products, arithmetic and copies ran while one was open for 4% of the time, Pallas kernels for 14%

profile of v6, /device:TPU:0, one launch (start us, length us, event | category | flops | bytes accessed | tf_op | source)
XLA Modules:
  0.0 173.1 jit_solution(9342126813336354029)
XLA Ops:
  6.5 3.1 %prepare.1 = (bf16[12,8,1024]{2,1,0:T(8,128)(2,1)}, bf16[4096,128]{1,0:T(8,128)(2,1)}, bf16[128,128]{1,0:T(8,128)(2,1)}, bf16[128,128]{1,0:T(8,128)(2,1)}) custom-call(bf16[8,3072]{1,0:T(8,128)(2,1)} %refs_0_.1, bf16[8,1024]{1,0:T(8,128)(2,1)} %refs_1_.1, bf16[8,4096]{1,0:T(8,128)(2,1)} %refs_2_.1, bf16[32,1024]{1,0:T(8,128)(2,1)} %refs_3_.1, ...), custom_call_target="tpu_custom_call" | custom-call | tf_op jit(solution)/shard_map/prepare/pallas_call | solution.py:394
  9.6 0.0 all-gather.2.cloned.1.call-update
  9.7 0.1 collective-permute-start
  9.7 1.7 %collective-permute-start.1 = (bf16[4096,128]{1,0:T(8,128)(2,1)}, bf16[4096,128]{1,0:T(8,128)(2,1)S(1)}, u32[]{:S(2)}, u32[]{:S(2)}) collective-permute-start(bf16[4096,128]{1,0:T(8,128)(2,1)} %get-tuple-element.21.refs_2_.refs_1_), channel_id=1, source_target_pairs={{0,32},{32,0},{64,96},{96,64},{1,33},{33,1},{65,97},{97,65},{2,34}... | collective-permute-start | bytes 3145736 | tf_op jit(solution)/shard_map/ppermute | solution.py:434
  11.5 1.3 collective-permute-start.2
  12.8 0.9 maximum_select_fusion
  13.6 1.1 broadcast_in_dim.6
  14.7 7.9 %all-to-all-start = ((bf16[16,128,256]{2,1,0:T(8,128)(2,1)}), bf16[16,128,256]{2,1,0:T(8,128)(2,1)S(1)}, u32[]{:S(2)}, u32[]{:S(2)}) async-start(bf16[16,128,256]{2,1,0:T(8,128)(2,1)} %broadcast_in_dim.6), calls=%async_computation | async-start | bytes 2097152 | tf_op jit(solution)/shard_map/all_to_all | solution.py:445
  22.6 0.1 collective-permute-start.4
  22.7 20.0 %all-to-all-done.refs_0_.refs_1_ = bf16[16,128,256]{2,1,0:T(8,128)(2,1)S(1)} async-done(((bf16[16,128,256]{2,1,0:T(8,128)(2,1)}), bf16[16,128,256]{2,1,0:T(8,128)(2,1)S(1)}, u32[]{:S(2)}, u32[]{:S(2)}) %all-to-all-start) | async-done | bytes 1048608 | tf_op jit(solution)/shard_map/all_to_all | solution.py:445
  42.7 0.0 collective-permute-done.1.refs_1_
  42.7 0.1 collective-permute-start.5
  42.8 0.5 collective-permute-start.3
  43.3 0.0 collective-permute-done.4.refs_3_.refs_2_
  43.3 2.7 %collective-permute-done.5.refs_5_.refs_4_ = bf16[4096,128]{1,0:T(8,128)(2,1)S(1)} collective-permute-done((bf16[4096,128]{1,0:T(8,128)(2,1)S(1)}, bf16[4096,128]{1,0:T(8,128)(2,1)S(1)}, u32[]{:S(2)}, u32[]{:S(2)}) %collective-permute-start.5) | collective-permute-done | bytes 1048608 | tf_op jit(solution)/shard_map/ppermute | solution.py:431
  46.0 1.0 copy-done.6
  47.0 0.1 collective-permute-done.3.refs_0_.refs_6_
  47.1 3.1 %section.4 = (bf16[64,256]{1,0:T(8,128)(2,1)}, bf16[64,256]{1,0:T(8,128)(2,1)}) custom-call(bf16[4096,128]{1,0:T(8,128)(2,1)} %collective-permute-done.3.refs_0_.refs_6_, bf16[16,128,256]{2,1,0:T(8,128)(2,1)} %copy-done.2, bf16[4096,128]{1,0:T(8,128)(2,1)} %get-tuple-element.21.refs_2_.refs_1_, bf16[4096,128]{1,0:T(8,128)(2,1)} %collective-permute-done.4.refs_3_.refs_2_, ...), custom_call_target="tpu_custom_call" | custom-call | flops 1 | bytes 1 | tf_op jit(solution)/shard_map/section/pallas_call | solution.py:337
  50.2 5.6 %collective-permute-start.6 = (bf16[64,256]{1,0:T(8,128)(2,1)}, bf16[64,256]{1,0:T(8,128)(2,1)S(1)}, u32[]{:S(2)}, u32[]{:S(2)}) collective-permute-start(bf16[64,256]{1,0:T(8,128)(2,1)} %get-tuple-element.25), channel_id=1, source_target_pairs={{0,96},{32,64},{1,97},{33,65},{2,98},{34,66},{3,99},{35,67},{4,100... | collective-permute-start | bytes 98312 | tf_op jit(solution)/shard_map/ppermute | solution.py:434
  55.8 1.9 %slice.11 = bf16[2048,128]{1,0:T(8,128)(2,1)} slice(bf16[4096,128]{1,0:T(8,128)(2,1)} %copy-done), slice={[2048:4096], [0:128]} | slice | bytes 1048576 | tf_op jit(solution)/shard_map/slice | solution.py:454
  57.7 1.9 %collective-permute-start.8 = (bf16[2048,128]{1,0:T(8,128)(2,1)}, bf16[2048,128]{1,0:T(8,128)(2,1)S(1)}, u32[]{:S(2)}, u32[]{:S(2)}) collective-permute-start(bf16[2048,128]{1,0:T(8,128)(2,1)} %slice.11), channel_id=1, source_target_pairs={{0,96},{96,0},{64,32},{1,97},{97,1},{65,33},{2,98},{98,2},{66,34},... | collective-permute-start | bytes 1572872 | tf_op jit(solution)/shard_map/ppermute | solution.py:434
  59.7 1.9 %collective-permute-start.7 = (bf16[2048,128]{1,0:T(8,128)(2,1)S(1)}, bf16[2048,128]{1,0:T(8,128)(2,1)S(1)}, u32[]{:S(2)}, u32[]{:S(2)}) collective-permute-start(bf16[2048,128]{1,0:T(8,128)(2,1)S(1)} %slice.10), channel_id=1, source_target_pairs={{0,32},{32,0},{64,96},{1,33},{33,1},{65,97},{2,34},{34,2},{66,98},... | collective-permute-start | bytes 1572872 | tf_op jit(solution)/shard_map/ppermute | solution.py:434
  61.6 0.8 broadcast_select_fusion
  62.4 0.9 broadcast_in_dim.7
  63.2 4.5 %all-to-all-start.1 = ((bf16[16,64,256]{2,1,0:T(8,128)(2,1)}), bf16[16,64,256]{2,1,0:T(8,128)(2,1)S(1)}, u32[]{:S(2)}, u32[]{:S(2)}) async-start(bf16[16,64,256]{2,1,0:T(8,128)(2,1)} %broadcast_in_dim.7), calls=%async_computation.1 | async-start | bytes 1048576 | tf_op jit(solution)/shard_map/all_to_all | solution.py:445
  67.7 9.1 %collective-permute-done.8.refs_2_ = bf16[2048,128]{1,0:T(8,128)(2,1)S(1)} collective-permute-done((bf16[2048,128]{1,0:T(8,128)(2,1)}, bf16[2048,128]{1,0:T(8,128)(2,1)S(1)}, u32[]{:S(2)}, u32[]{:S(2)}) %collective-permute-start.8) | collective-permute-done | bytes 524320 | tf_op jit(solution)/shard_map/ppermute | solution.py:434
  76.9 2.1 %all-to-all-done.1.refs_0_ = bf16[16,64,256]{2,1,0:T(8,128)(2,1)S(1)} async-done(((bf16[16,64,256]{2,1,0:T(8,128)(2,1)}), bf16[16,64,256]{2,1,0:T(8,128)(2,1)S(1)}, u32[]{:S(2)}, u32[]{:S(2)}) %all-to-all-start.1) | async-done | bytes 524320 | tf_op jit(solution)/shard_map/all_to_all | solution.py:445
  79.0 0.1 collective-permute-start.10
  79.1 0.5 collective-permute-start.9
  79.6 2.9 %collective-permute-done.10.refs_10_ = bf16[2048,128]{1,0:T(8,128)(2,1)S(1)} collective-permute-done((bf16[2048,128]{1,0:T(8,128)(2,1)S(1)}, bf16[2048,128]{1,0:T(8,128)(2,1)S(1)}, u32[]{:S(2)}, u32[]{:S(2)}) %collective-permute-start.10) | collective-permute-done | bytes 524320 | tf_op jit(solution)/shard_map/ppermute | solution.py:431
  82.4 0.2 collective-permute-done.9.refs_9_
  82.7 0.6 copy-done.7
  83.2 3.2 %section.5 = bf16[16,64,256]{2,1,0:T(8,128)(2,1)} custom-call(bf16[16,64,256]{2,1,0:T(8,128)(2,1)} %copy-done.5, bf16[4096,128]{1,0:T(8,128)(2,1)} %get-tuple-element.21.refs_2_.refs_1_, bf16[4096,128]{1,0:T(8,128)(2,1)} %collective-permute-done.4.refs_3_.refs_2_, bf16[4096,128]{1,0:T(8,128)(2,1)} %copy-done, bf16[4096,128]{1,0:T(8,128)(2,1)} %copy-done.6, ...), custom_call_target="tpu_custom_call" | custom-call | flops 1 | bytes 1 | tf_op jit(solution)/shard_map/section/pallas_call | solution.py:337
  86.4 20.1 %all_to_all.25.refs_0_ = bf16[16,64,256]{2,1,0:T(8,128)(2,1)} all-to-all(bf16[16,64,256]{2,1,0:T(8,128)(2,1)} %section.5), channel_id=1, replica_groups=mesh['y'=4,'x'=4,'z'=4,'c'=2] {'x','z'}, dimensions={0} | all-to-all | bytes 1048576 | tf_op jit(solution)/shard_map/all_to_all | solution.py:445
  106.5 3.2 %section.6 = bf16[16,64,256]{2,1,0:T(8,128)(2,1)} custom-call(bf16[16,64,256]{2,1,0:T(8,128)(2,1)} %all_to_all.25.refs_0_, bf16[4096,128]{1,0:T(8,128)(2,1)} %get-tuple-element.21.refs_2_.refs_1_, bf16[4096,128]{1,0:T(8,128)(2,1)} %collective-permute-done.4.refs_3_.refs_2_, bf16[4096,128]{1,0:T(8,128)(2,1)} %copy-done, bf16[4096,128]{1,0:T(8,128)(2,1)} %copy-done.6, ...), custom_call_target="tpu_custom_call" | custom-call | flops 1 | bytes 1 | tf_op jit(solution)/shard_map/section/pallas_call | solution.py:337
  109.7 6.2 %all-to-all-start.3 = ((bf16[16,64,256]{2,1,0:T(8,128)(2,1)}), bf16[16,64,256]{2,1,0:T(8,128)(2,1)S(1)}, u32[]{:S(2)}, u32[]{:S(2)}) async-start(bf16[16,64,256]{2,1,0:T(8,128)(2,1)} %section.6), calls=%async_computation.3 | async-start | bytes 1048576 | tf_op jit(solution)/shard_map/all_to_all | solution.py:445
  115.9 0.1 collective-permute-start.11
  116.0 0.6 copy.18.refs_3_
  116.6 0.6 concatenate.20.prev_ref.refs_2_
  117.3 2.7 %embed.1.n_in = bf16[512,1024]{1,0:T(8,128)(2,1)} custom-call(s32[4,128]{1,0:T(4,128)} %concatenate.20.prev_ref.refs_2_, bf16[128,1024]{1,0:T(8,128)(2,1)} %refs_4_.1, bf16[128,1024]{1,0:T(8,128)(2,1)} %refs_5_.1, f32[3,1024]{1,0:T(4,128)} %refs_6_.3), custom_call_target="tpu_custom_call" | custom-call | tf_op jit(solution)/shard_map/embed/pallas_call | solution.py:41
  120.0 8.7 %all-to-all-done.3.refs_0_ = bf16[16,64,256]{2,1,0:T(8,128)(2,1)S(1)} async-done(((bf16[16,64,256]{2,1,0:T(8,128)(2,1)}), bf16[16,64,256]{2,1,0:T(8,128)(2,1)S(1)}, u32[]{:S(2)}, u32[]{:S(2)}) %all-to-all-start.3) | async-done | bytes 524320 | tf_op jit(solution)/shard_map/all_to_all | solution.py:445
  128.7 0.8 copy-done.8
  129.5 3.4 %section.7.gate_ref = f32[16,4,1024]{2,1,0:T(4,128)} custom-call(bf16[16,64,256]{2,1,0:T(8,128)(2,1)} %copy-done.8, bf16[4096,128]{1,0:T(8,128)(2,1)} %get-tuple-element.21.refs_2_.refs_1_, bf16[4096,128]{1,0:T(8,128)(2,1)} %collective-permute-done.4.refs_3_.refs_2_, bf16[4096,128]{1,0:T(8,128)(2,1)} %copy-done, bf16[4096,128]{1,0:T(8,128)(2,1)} %copy-done.6, ...), custom_call_target="tpu_custom_call" | custom-call | flops 1 | bytes 1 | tf_op jit(solution)/shard_map/section/pallas_call | solution.py:337
  133.0 3.8 %all-to-all-start.4 = ((f32[16,4,1024]{2,1,0:T(4,128)}), f32[16,4,1024]{2,1,0:T(4,128)S(1)}, u32[]{:S(2)}, u32[]{:S(2)}) async-start(f32[16,4,1024]{2,1,0:T(4,128)} %section.7.gate_ref), calls=%async_computation.4 | async-start | bytes 524288 | tf_op jit(solution)/shard_map/all_to_all | solution.py:445
  136.8 0.0 all-gather.2.cloned.1.call-done
  136.8 9.1 %early.1 = (bf16[512,1024]{1,0:T(8,128)(2,1)}, f32[512,1024]{1,0:T(8,128)}, f32[512,128]{1,0:T(8,128)}, f32[512,128]{1,0:T(8,128)}) custom-call(f32[16,4,1024]{2,1,0:T(4,128)} %section.7.gate_ref, bf16[512,1024]{1,0:T(8,128)(2,1)} %embed.1.n_in, bf16[128,12,8,1024]{3,2,1,0:T(8,128)(2,1)} %bitcast.14), custom_call_target="tpu_custom_call" | custom-call | flops 8589934592 | bytes 16777216 | tf_op jit(solution)/shard_map/early/pallas_call | solution.py:122
  145.9 0.7 copy-done.11
  146.6 19.7 %late.1 = f32[4,128]{1,0:T(4,128)} custom-call(f32[16,4,1024]{2,1,0:T(4,128)} %copy-done.11, s32[4,128]{1,0:T(4,128)} %bitcast.11, s32[4,128]{1,0:T(4,128)} %concatenate.20.prev_ref.refs_2_, s32[4,1]{1,0:T(4,128)} %copy.18.refs_3_, bf16[128,1024]{1,0:T(8,128)(2,1)} %refs_4_.1, bf16[128,1024]{1,0:T(8,128)(2,1)} %refs_5_.1, f32[3,1024]{1,0:T(4,128)} %refs_6_.3, ...), custom_call_target="tpu_custom_call" | custom-call | flops 10737418240 | bytes 25165824 | tf_op jit(solution)/shard_map/late/pallas_call | solution.py:232
  (34 shorter events, 0.1 us)
Async XLA Ops:
  6.5 109.3 %copy-start.9 = (bf16[128,1024]{1,0:T(8,128)(2,1)S(1)}, bf16[128,1024]{1,0:T(8,128)(2,1)}, u32[]{:S(2)}) copy-start(bf16[128,1024]{1,0:T(8,128)(2,1)} %refs_11_.1) | copy-start | bytes 786436
  6.5 109.5 %copy-start.13 = (s32[1,4]{1,0:T(1,128)S(1)}, s32[1,4]{1,0:T(1,128)}, u32[]{:S(2)}) copy-start(s32[1,4]{1,0:T(1,128)} %param.18) | copy-start | bytes 52
  6.5 110.1 %copy-start.12 = (s32[1,4,128]{2,1,0:T(4,128)S(1)}, s32[1,4,128]{2,1,0:T(4,128)}, u32[]{:S(2)}) copy-start(s32[1,4,128]{2,1,0:T(4,128)} %param.17) | copy-start | bytes 6148
  6.5 130.3 %all-gather.2.cloned.1.call-start = ((), (), s32[]{:S(2)}) async-start(), calls=%async_computation.5 | async-start | bytes 25362432 | tf_op jit(solution)/shard_map/all_gather | solution.py:441
  9.7 3.1 %collective-permute-start = (bf16[128,128]{1,0:T(8,128)(2,1)}, bf16[128,128]{1,0:T(8,128)(2,1)S(1)}, u32[]{:S(2)}, u32[]{:S(2)}) collective-permute-start(bf16[128,128]{1,0:T(8,128)(2,1)} %get-tuple-element.20), channel_id=1, source_target_pairs={{0,1},{1,0},{2,3},{3,2},{4,5},{5,4},{6,7},{7,6},{8,9},{9,8},{10,11... | collective-permute-start | bytes 98312 | tf_op jit(solution)/shard_map/ppermute | solution.py:431
  9.7 32.9 %collective-permute-start.1 = (bf16[4096,128]{1,0:T(8,128)(2,1)}, bf16[4096,128]{1,0:T(8,128)(2,1)S(1)}, u32[]{:S(2)}, u32[]{:S(2)}) collective-permute-start(bf16[4096,128]{1,0:T(8,128)(2,1)} %get-tuple-element.21.refs_2_.refs_1_), channel_id=1, source_target_pairs={{0,32},{32,0},{64,96},{96,64},{1,33},{33,1},{65,97},{97,65},{2,34}... | collective-permute-start | bytes 3145736 | tf_op jit(solution)/shard_map/ppermute | solution.py:434
  11.5 31.2 %collective-permute-start.2 = (bf16[4096,128]{1,0:T(8,128)(2,1)}, bf16[4096,128]{1,0:T(8,128)(2,1)S(1)}, u32[]{:S(2)}, u32[]{:S(2)}) collective-permute-start(bf16[4096,128]{1,0:T(8,128)(2,1)} %get-tuple-element.21.refs_2_.refs_1_), channel_id=1, source_target_pairs={{32,64},{64,32},{96,0},{33,65},{65,33},{97,1},{34,66},{66,34},{98,... | collective-permute-start | bytes 3145736 | tf_op jit(solution)/shard_map/ppermute | solution.py:434
  14.7 28.0 %all-to-all-start = ((bf16[16,128,256]{2,1,0:T(8,128)(2,1)}), bf16[16,128,256]{2,1,0:T(8,128)(2,1)S(1)}, u32[]{:S(2)}, u32[]{:S(2)}) async-start(bf16[16,128,256]{2,1,0:T(8,128)(2,1)} %broadcast_in_dim.6), calls=%async_computation | async-start | bytes 2097152 | tf_op jit(solution)/shard_map/all_to_all | solution.py:445
  22.6 20.7 %collective-permute-start.4 = (bf16[4096,128]{1,0:T(8,128)(2,1)}, bf16[4096,128]{1,0:T(8,128)(2,1)}, u32[]{:S(2)}, u32[]{:S(2)}) collective-permute-start(bf16[4096,128]{1,0:T(8,128)(2,1)} %get-tuple-element.21.refs_2_.refs_1_), channel_id=1, source_target_pairs={{0,1},{1,0},{2,3},{3,2},{4,5},{5,4},{6,7},{7,6},{8,9},{9,8},{10,11... | collective-permute-start | bytes 3145736 | tf_op jit(solution)/shard_map/ppermute | solution.py:431
  42.7 4.4 %copy-start.2 = (bf16[16,128,256]{2,1,0:T(8,128)(2,1)}, bf16[16,128,256]{2,1,0:T(8,128)(2,1)S(1)}, u32[]{:S(2)}) copy-start(bf16[16,128,256]{2,1,0:T(8,128)(2,1)S(1)} %all-to-all-done.refs_0_.refs_1_) | copy-start | bytes 3145732
  42.7 4.4 %copy-start = (bf16[4096,128]{1,0:T(8,128)(2,1)}, bf16[4096,128]{1,0:T(8,128)(2,1)S(1)}, u32[]{:S(2)}) copy-start(bf16[4096,128]{1,0:T(8,128)(2,1)S(1)} %get-tuple-element.23.refs_4_.refs_3_) | copy-start | bytes 3145732
  42.7 39.9 %copy-start.1 = (bf16[4096,128]{1,0:T(8,128)(2,1)}, bf16[4096,128]{1,0:T(8,128)(2,1)S(1)}, u32[]{:S(2)}) copy-start(bf16[4096,128]{1,0:T(8,128)(2,1)S(1)} %get-tuple-element.22.refs_5_) | copy-start | bytes 3145732
  42.7 3.3 %collective-permute-start.5 = (bf16[4096,128]{1,0:T(8,128)(2,1)S(1)}, bf16[4096,128]{1,0:T(8,128)(2,1)S(1)}, u32[]{:S(2)}, u32[]{:S(2)}) collective-permute-start(bf16[4096,128]{1,0:T(8,128)(2,1)S(1)} %get-tuple-element.23.refs_4_.refs_3_), channel_id=1, source_target_pairs={{0,1},{1,0},{2,3},{3,2},{4,5},{5,4},{6,7},{7,6},{8,9},{9,8},{10,11... | collective-permute-start | bytes 3145736 | tf_op jit(solution)/shard_map/ppermute | solution.py:431
  42.8 4.3 %collective-permute-start.3 = (bf16[4096,128]{1,0:T(8,128)(2,1)S(1)}, bf16[4096,128]{1,0:T(8,128)(2,1)}, u32[]{:S(2)}, u32[]{:S(2)}) collective-permute-start(bf16[4096,128]{1,0:T(8,128)(2,1)S(1)} %get-tuple-element.22.refs_5_), channel_id=1, source_target_pairs={{0,1},{1,0},{2,3},{3,2},{4,5},{5,4},{6,7},{7,6},{8,9},{9,8},{10,11... | collective-permute-start | bytes 3145736 | tf_op jit(solution)/shard_map/ppermute | solution.py:431
  46.0 1.0 copy-start.6
  50.2 11.4 %collective-permute-start.6 = (bf16[64,256]{1,0:T(8,128)(2,1)}, bf16[64,256]{1,0:T(8,128)(2,1)S(1)}, u32[]{:S(2)}, u32[]{:S(2)}) collective-permute-start(bf16[64,256]{1,0:T(8,128)(2,1)} %get-tuple-element.25), channel_id=1, source_target_pairs={{0,96},{32,64},{1,97},{33,65},{2,98},{34,66},{3,99},{35,67},{4,100... | collective-permute-start | bytes 98312 | tf_op jit(solution)/shard_map/ppermute | solution.py:434
  57.7 19.1 %collective-permute-start.8 = (bf16[2048,128]{1,0:T(8,128)(2,1)}, bf16[2048,128]{1,0:T(8,128)(2,1)S(1)}, u32[]{:S(2)}, u32[]{:S(2)}) collective-permute-start(bf16[2048,128]{1,0:T(8,128)(2,1)} %slice.11), channel_id=1, source_target_pairs={{0,96},{96,0},{64,32},{1,97},{97,1},{65,33},{2,98},{98,2},{66,34},... | collective-permute-start | bytes 1572872 | tf_op jit(solution)/shard_map/ppermute | solution.py:434
  59.7 17.2 %collective-permute-start.7 = (bf16[2048,128]{1,0:T(8,128)(2,1)S(1)}, bf16[2048,128]{1,0:T(8,128)(2,1)S(1)}, u32[]{:S(2)}, u32[]{:S(2)}) collective-permute-start(bf16[2048,128]{1,0:T(8,128)(2,1)S(1)} %slice.10), channel_id=1, source_target_pairs={{0,32},{32,0},{64,96},{1,33},{33,1},{65,97},{2,34},{34,2},{66,98},... | collective-permute-start | bytes 1572872 | tf_op jit(solution)/shard_map/ppermute | solution.py:434
  63.2 15.7 %all-to-all-start.1 = ((bf16[16,64,256]{2,1,0:T(8,128)(2,1)}), bf16[16,64,256]{2,1,0:T(8,128)(2,1)S(1)}, u32[]{:S(2)}, u32[]{:S(2)}) async-start(bf16[16,64,256]{2,1,0:T(8,128)(2,1)} %broadcast_in_dim.7), calls=%async_computation.1 | async-start | bytes 1048576 | tf_op jit(solution)/shard_map/all_to_all | solution.py:445
  79.0 3.7 %copy-start.5 = (bf16[16,64,256]{2,1,0:T(8,128)(2,1)}, bf16[16,64,256]{2,1,0:T(8,128)(2,1)S(1)}, u32[]{:S(2)}) copy-start(bf16[16,64,256]{2,1,0:T(8,128)(2,1)S(1)} %all-to-all-done.1.refs_0_) | copy-start | bytes 1572868
  79.0 3.7 %copy-start.3 = (bf16[2048,128]{1,0:T(8,128)(2,1)}, bf16[2048,128]{1,0:T(8,128)(2,1)S(1)}, u32[]{:S(2)}) copy-start(bf16[2048,128]{1,0:T(8,128)(2,1)S(1)} %get-tuple-element.27.refs_8_) | copy-start | bytes 1572868
  79.0 3.7 %copy-start.4 = (bf16[2048,128]{1,0:T(8,128)(2,1)}, bf16[2048,128]{1,0:T(8,128)(2,1)S(1)}, u32[]{:S(2)}) copy-start(bf16[2048,128]{1,0:T(8,128)(2,1)S(1)} %get-tuple-element.26.refs_7_) | copy-start | bytes 1572868
  79.0 3.4 %collective-permute-start.10 = (bf16[2048,128]{1,0:T(8,128)(2,1)S(1)}, bf16[2048,128]{1,0:T(8,128)(2,1)S(1)}, u32[]{:S(2)}, u32[]{:S(2)}) collective-permute-start(bf16[2048,128]{1,0:T(8,128)(2,1)S(1)} %get-tuple-element.27.refs_8_), channel_id=1, source_target_pairs={{0,1},{1,0},{2,3},{3,2},{4,5},{5,4},{6,7},{7,6},{8,9},{9,8},{10,11... | collective-permute-start | bytes 1572872 | tf_op jit(solution)/shard_map/ppermute | solution.py:431
  79.1 3.6 %collective-permute-start.9 = (bf16[2048,128]{1,0:T(8,128)(2,1)S(1)}, bf16[2048,128]{1,0:T(8,128)(2,1)}, u32[]{:S(2)}, u32[]{:S(2)}) collective-permute-start(bf16[2048,128]{1,0:T(8,128)(2,1)S(1)} %get-tuple-element.26.refs_7_), channel_id=1, source_target_pairs={{0,1},{1,0},{2,3},{3,2},{4,5},{5,4},{6,7},{7,6},{8,9},{9,8},{10,11... | collective-permute-start | bytes 1572872 | tf_op jit(solution)/shard_map/ppermute | solution.py:431
  82.4 0.8 copy-start.7
  109.7 19.1 %all-to-all-start.3 = ((bf16[16,64,256]{2,1,0:T(8,128)(2,1)}), bf16[16,64,256]{2,1,0:T(8,128)(2,1)S(1)}, u32[]{:S(2)}, u32[]{:S(2)}) async-start(bf16[16,64,256]{2,1,0:T(8,128)(2,1)} %section.6), calls=%async_computation.3 | async-start | bytes 1048576 | tf_op jit(solution)/shard_map/all_to_all | solution.py:445
  115.9 4.1 %collective-permute-start.11 = (bf16[128,1024]{1,0:T(8,128)(2,1)S(1)}, bf16[128,1024]{1,0:T(8,128)(2,1)S(1)}, u32[]{:S(2)}, u32[]{:S(2)}) collective-permute-start(bf16[128,1024]{1,0:T(8,128)(2,1)S(1)} %copy-done.9), channel_id=1, source_target_pairs={{0,1},{1,0},{2,3},{3,2},{4,5},{5,4},{6,7},{7,6},{8,9},{9,8},{10,11... | collective-permute-start | bytes 786440 | tf_op jit(solution)/shard_map/ppermute | solution.py:431
  120.0 8.7 %copy-start.10 = (bf16[128,1024]{1,0:T(8,128)(2,1)}, bf16[128,1024]{1,0:T(8,128)(2,1)S(1)}, u32[]{:S(2)}) copy-start(bf16[128,1024]{1,0:T(8,128)(2,1)S(1)} %collective-permute-done.11.refs_12_) | copy-start | bytes 786436
  128.7 0.8 copy-start.8
  133.0 13.0 %all-to-all-start.4 = ((f32[16,4,1024]{2,1,0:T(4,128)}), f32[16,4,1024]{2,1,0:T(4,128)S(1)}, u32[]{:S(2)}, u32[]{:S(2)}) async-start(f32[16,4,1024]{2,1,0:T(4,128)} %section.7.gate_ref), calls=%async_computation.4 | async-start | bytes 524288 | tf_op jit(solution)/shard_map/all_to_all | solution.py:445
  145.9 0.7 copy-start.11
Sparse Core Ops, SparseCore 0:
  10.4 114.6 all-gather.1
